TPU v7x, 256 devices: a whole 4x4x8 slice. The times are simulated.
256 devices in a mesh: gx: 32 (over z_hi, y, core), gy: 8 (over z_lo, x).
Axes of the slice: x: 4, y: 4, z: 8 (z_hi: 4, z_lo: 2; z = z_hi * 2 + z_lo), core: 2. Of those that a mesh axis runs over, the one named last changes fastest.
Arguments:
- tokens: bfloat16 [256, 16384], P('gy', 'gx'), may hold values from -6 to 6
- gate_payload: bfloat16 [16384, 26624], P('gx', 'gy'), may hold values from -0.09375 to 0.09375
- gate_scales: float32 [128, 208], P('gx', 'gy'), may hold values from 0.5 to 2
- up_payload: bfloat16 [16384, 26624], P('gx', 'gy'), may hold values from -0.046875 to 0.046875
- up_scales: float32 [128, 208], P('gx', 'gy'), may hold values from 0.5 to 2
- down_payload: bfloat16 [26624, 16384], P('gy', 'gx'), may hold values from -0.0390625 to 0.0390625
- down_scales: float32 [208, 128], P('gy', 'gx'), may hold values from 0.5 to 2
Outputs:
- mixed: bfloat16 [256, 16384], P('gy', 'gx')
All inputs are finite; a program needn't handle non-finite values.
Results may differ from a plain program's by a relative error of at most 0.007.
Values may be sent and summed in bfloat16 or wider, within the bound.
No kernel may reach another device: no remote copies, remote signals or barrier semaphores. Data moves between devices by JAX's collectives and lax.ppermute only.
A program may use at most 64 MiB of HBM per device.

v0:
```python
import jax
import jax.numpy as jnp
from jax import lax
from jax.sharding import PartitionSpec as P

BLOCK = 128


def dequantize(payload, scales):
    row_count, col_count = payload.shape
    blocked = payload.reshape(row_count // BLOCK, BLOCK, col_count // BLOCK, BLOCK).astype(
        jnp.float32
    )
    blocked = blocked * scales[:, None, :, None]
    return blocked.reshape(row_count, col_count).astype(jnp.bfloat16)


def local(tokens, gate_payload, gate_scales, up_payload, up_scales, down_payload, down_scales):
    features = lax.all_gather(tokens, "gy", axis=0, tiled=True)
    gate_weight = dequantize(gate_payload, gate_scales)
    up_weight = dequantize(up_payload, up_scales)
    down_weight = dequantize(down_payload, down_scales)
    token_count = features.shape[0]
    gate_term = lax.dot_general(
        gate_weight, features, (((0,), (1,)), ((), ())), preferred_element_type=jnp.float32
    )
    up_term = lax.dot_general(
        up_weight, features, (((0,), (1,)), ((), ())), preferred_element_type=jnp.float32
    )
    summed = lax.psum_scatter(
        jnp.concatenate([gate_term, up_term], axis=1), "gx", scatter_dimension=0, tiled=True
    )
    hidden_units = (jax.nn.silu(summed[:, :token_count]) * summed[:, token_count:]).astype(
        jnp.bfloat16
    )
    terms = lax.dot_general(
        lax.all_gather(hidden_units, "gx", axis=0, tiled=True),
        down_weight,
        (((0,), (0,)), ((), ())),
        preferred_element_type=jnp.float32,
    )
    return lax.psum_scatter(terms, "gy", scatter_dimension=0, tiled=True).astype(jnp.bfloat16)


def solution(mesh):
    placed = (
        P("gy", "gx"),
        P("gx", "gy"),
        P("gx", "gy"),
        P("gx", "gy"),
        P("gx", "gy"),
        P("gy", "gx"),
        P("gy", "gx"),
    )
    return jax.shard_map(
        local, mesh=mesh, in_specs=placed, out_specs=P("gy", "gx"), check_vma=False
    )
```

profile of v0, /device:TPU:8, one launch (start us, length us, event | category | flops | bytes accessed | tf_op | source)
XLA Modules:
  0.0 281.3 jit_solution(8331532744808512743)
XLA Ops:
  6.5 0.0 reduce-scatter.7.cloned.1.call-start
  6.5 31.4 %all_gather.6 = bf16[256,512]{1,0:T(8,128)(2,1)} all-gather(bf16[32,512]{1,0:T(8,128)(2,1)} %param.7), channel_id=1, replica_groups=mesh['gx'=32,'gy'=8] {'gy'}, dimensions={0}, use_global_device_ids=true | all-gather | bytes 294912 | tf_op jit(solution)/shard_map/all_gather | solution.py:19
  37.9 0.8 copy.15
  38.7 0.0 copy-start.4
  38.7 5.6 %copy.14 = bf16[512,3328]{0,1:T(8,128)(2,1)} copy(bf16[512,3328]{1,0:T(8,128)(2,1)} %param.8) | data formatting | bytes 6815744 | tf_op args[1]
  44.3 0.0 copy-done.4
  44.3 0.1 copy.17
  44.4 4.2 %copy.16 = bf16[512,3328]{0,1:T(8,128)(2,1)S(1)} copy(bf16[512,3328]{1,0:T(8,128)(2,1)} %param.10) | data formatting | bytes 6815744 | tf_op args[3]
  48.6 0.0 copy-start
  48.6 0.0 copy-start.2
  48.6 0.9 mul.40
  49.6 1.0 copy-done
  50.6 0.0 copy-done.2
  50.6 1.1 fusion.3
  51.7 0.9 mul.43
  52.6 1.2 fusion.5
  53.9 3.3 %pad_maximum_fusion = f32[3328,512]{0,1:T(8,128)} fusion(f32[3328,256]{0,1:T(8,128)S(1)} %fusion.5, f32[3328,256]{0,1:T(8,128)S(1)} %fusion.3), kind=kLoop, calls=%fused_computation.6 | loop fusion | flops 1703936 | bytes 13631488 | tf_op jit(solution)/shard_map/concatenate | solution.py:31
  57.2 7.6 %copy.20 = f32[3328,512]{1,0:T(8,128)} copy(f32[3328,512]{0,1:T(8,128)} %pad_maximum_fusion) | data formatting | bytes 13631488
  64.8 0.0 copy-start.5
  64.8 0.0 reduce-scatter.7.cloned.1.call-update
  64.8 0.0 all-gather.2.cloned.1.call-start
  64.9 112.6 %reduce-scatter.7.cloned.1.call-done = f32[104,512]{1,0:T(8,128)} async-done(((f32[3328,512]{1,0:T(8,128)}), f32[104,512]{1,0:T(8,128)}) %reduce-scatter.7.cloned.1.call-update) | async-done | bytes 213008
  177.5 1.0 fusion.9
  178.4 0.1 copy.22
  178.5 0.1 copy.23
  178.7 0.7 copy.18
  179.4 0.0 all-gather.2.cloned.1.call-update
  179.4 0.0 reduce-scatter.5.cloned.1.call-start
  179.5 0.0 copy-done.5
  179.5 0.1 copy.19
  179.6 0.0 copy-start.1
  179.6 51.5 %all-gather.2.cloned.1.call-done = bf16[3328,256]{1,0:T(8,128)(2,1)} async-done(((bf16[104,256]{1,0:T(8,128)(2,1)}), bf16[3328,256]{1,0:T(8,128)(2,1)}) %all-gather.2.cloned.1.call-update) | async-done | bytes 1703952 | tf_op jit(solution)/shard_map/all_gather | solution.py:37
  231.1 0.0 copy-start.3
  231.1 0.9 mul.48
  232.1 0.0 copy-done.1
  232.1 0.5 copy-done.3
  232.6 1.9 fusion.7
  234.5 0.0 reduce-scatter.5.cloned.1.call-update
  234.6 38.8 %reduce-scatter.5.cloned.1.call-done = f32[32,512]{1,0:T(8,128)} async-done(((f32[256,512]{1,0:T(8,128)}), f32[32,512]{1,0:T(8,128)}) %reduce-scatter.5.cloned.1.call-update) | async-done | bytes 65552 | tf_op jit(solution)/shard_map/reduce_scatter | solution.py:42
  273.4 1.5 convert_element_type.34
  (1 shorter events, 0.0 us)
Async XLA Ops:
  6.5 170.9 %reduce-scatter.7.cloned.1.call-start = ((), (), s32[]{:S(2)}) async-start(), calls=%async_computation.4 | async-start | bytes 7028736
  38.7 5.6 %copy-start.4 = (f32[4,26]{1,0:T(4,128)S(1)}, f32[4,26]{1,0:T(4,128)}, u32[]{:S(2)}) copy-start(f32[4,26]{1,0:T(4,128)} %param.11) | copy-start | bytes 1252
  48.6 2.0 copy-start
  48.6 2.0 copy-start.2
  64.8 114.7 %copy-start.5 = (f32[26,4]{0,1:T(4,128)S(1)}, f32[26,4]{0,1:T(4,128)}, u32[]{:S(2)}) copy-start(f32[26,4]{0,1:T(4,128)} %param.13) | copy-start | bytes 1252
  64.8 166.3 %all-gather.2.cloned.1.call-start = ((), (), s32[]{:S(2)}) async-start(), calls=%async_computation.2 | async-start | bytes 1757184 | tf_op jit(solution)/shard_map/all_gather | solution.py:37
  179.4 93.9 %reduce-scatter.5.cloned.1.call-start = ((), (), s32[]{:S(2)}) async-start(), calls=%async_computation.3 | async-start | bytes 589824 | tf_op jit(solution)/shard_map/reduce_scatter | solution.py:42
  179.6 52.5 %copy-start.1 = (bf16[3328,512]{1,0:T(8,128)(2,1)S(1)}, bf16[3328,512]{1,0:T(8,128)(2,1)}, u32[]{:S(2)}) copy-start(bf16[3328,512]{1,0:T(8,128)(2,1)} %param.12) | copy-start | bytes 10223620
  231.1 1.5 copy-start.3
Sparse Core Ops, SparseCore 0:
  65.0 112.4 reduce-scatter.6
  180.4 50.6 all-gather.1
  234.7 38.6 reduce-scatter.4
where the time goes:
time: 282 us; the launch traced here: 281 us
  waiting for transfers between devices  203 us (72%)
  blocking collectives  31.4 us (11%)
  local copies, waits for them, and re-layouts  24.6 us (9%)
  between operations  13.2 us (5%)
  other arithmetic  4.8 us (2%)
  matrix products  4.26 us (2%)
    unnamed x4, waiting for transfers between devices  113 us
    all_gather x1, waiting for transfers between devices, local(): lax.all_gather(hidden_units, 'gx', axis=0, tiled=True)  51.5 us
    reduce_scatter x1, waiting for transfers between devices, local(): lax.psum_scatter(terms, 'gy', scatter_dimension=0, tiled=True)  38.8 us
    all_gather x1, blocking collectives, local(): features = lax.all_gather(tokens, 'gy', axis=0, tiled=True)  31.4 us
    unnamed x20, local copies, waits for them, and re-layouts  20.1 us
  transfers between devices with their start and end apart: 3, of which 3 were waited for; matrix products, arithmetic and copies ran while one was open for 0% of the time, Pallas kernels for 0%

commit v1 on v0

v1 whole, which is shorter than its diff:
```python
import jax
import jax.numpy as jnp
from jax import lax
from jax.experimental import pallas as pl
from jax.experimental.pallas import tpu as pltpu
from jax.sharding import PartitionSpec as P

BLOCK = 128
F32 = jnp.float32
BF16 = jnp.bfloat16
NZ, NY, NC, NG = 4, 4, 2, 8


def gx_pairs(dz, dy, dc):
    pairs = []
    for z in range(NZ):
        for y in range(NY):
            for c in range(NC):
                src = (z * NY + y) * NC + c
                dst = (((z + dz) % NZ) * NY + (y + dy) % NY) * NC + (c + dc) % NC
                pairs.append((src, dst))
    return pairs


def move_gx(x, dz=0, dy=0, dc=0):
    return lax.ppermute(x, "gx", gx_pairs(dz, dy, dc))


def move_gy(x, k):
    return lax.ppermute(x, "gy", [(i, (i + k) % NG) for i in range(NG)])


def scaled(payload, scale):
    return (payload.astype(F32) * scale).astype(BF16)


def pair_kernel(half, gate, up, gate_scales, up_scales, out):
    column = half[0] * pl.num_programs(0) + pl.program_id(0)
    for row in range(gate.shape[0] // BLOCK):
        rows = slice(row * BLOCK, (row + 1) * BLOCK)
        out[rows, :BLOCK] = scaled(gate[rows, :], gate_scales[row, column])
        out[rows, BLOCK:] = scaled(up[rows, :], up_scales[row, column])


def pair_weights(half, gate, gate_scales, up, up_scales):
    rows, columns = gate.shape
    blocks = columns // (2 * BLOCK)
    weight = pl.BlockSpec((rows, BLOCK), lambda i, h: (0, h[0] * blocks + i))
    scales = pl.BlockSpec(memory_space=pltpu.SMEM)
    return pl.pallas_call(
        pair_kernel,
        out_shape=jax.ShapeDtypeStruct((rows, columns), BF16),
        grid_spec=pltpu.PrefetchScalarGridSpec(
            num_scalar_prefetch=1,
            grid=(blocks,),
            in_specs=[weight, weight, scales, scales],
            out_specs=pl.BlockSpec((rows, 2 * BLOCK), lambda i, h: (0, i)),
        ),
        cost_estimate=pl.CostEstimate(
            flops=2 * rows * columns, bytes_accessed=4 * rows * columns, transcendentals=0
        ),
    )(half, gate, up, gate_scales, up_scales)


def down_kernel(half, payload, scales, out):
    base = half[0] * (payload.shape[0] // BLOCK)
    column = pl.program_id(0)
    for row in range(payload.shape[0] // BLOCK):
        rows = slice(row * BLOCK, (row + 1) * BLOCK)
        out[rows, :] = scaled(payload[rows, :], scales[base + row, column])


def down_weights(half, payload, scales):
    rows, columns = payload.shape
    rows //= 2
    return pl.pallas_call(
        down_kernel,
        out_shape=jax.ShapeDtypeStruct((rows, columns), BF16),
        grid_spec=pltpu.PrefetchScalarGridSpec(
            num_scalar_prefetch=1,
            grid=(columns // BLOCK,),
            in_specs=[
                pl.BlockSpec((rows, BLOCK), lambda i, h: (h[0], i)),
                pl.BlockSpec(memory_space=pltpu.SMEM),
            ],
            out_specs=pl.BlockSpec((rows, BLOCK), lambda i, h: (0, i)),
        ),
        cost_estimate=pl.CostEstimate(
            flops=rows * columns, bytes_accessed=4 * rows * columns, transcendentals=0
        ),
    )(half, payload, scales)


def turned(x, y, z):
    x = lax.dynamic_slice_in_dim(jnp.concatenate([x, x], 0), y, NY, 0)
    return lax.dynamic_slice_in_dim(jnp.concatenate([x, x], 1), z, NZ, 1)


def dot(a, b):
    return lax.dot_general(a, b, (((1,), (0,)), ((), ())), preferred_element_type=F32)


def local(tokens, gate_payload, gate_scales, up_payload, up_scales, down_payload, down_scales):
    index = lax.axis_index("gx")
    z, y, c = index // (NY * NC), (index // NC) % NY, index % NC
    mine = jnp.reshape(c, (1,)).astype(jnp.int32)
    other = 1 - mine

    blocks = [tokens] + [move_gy(tokens, k) for k in range(1, NG)]
    w_other = pair_weights(other, gate_payload, gate_scales, up_payload, up_scales)
    w_mine = pair_weights(mine, gate_payload, gate_scales, up_payload, up_scales)
    d_mine = down_weights(mine, down_payload, down_scales)
    d_other = down_weights(other, down_payload, down_scales)

    width = tokens.shape[1]
    features = jnp.concatenate(blocks, axis=0)
    count = features.shape[0]
    part = count // (NY * NZ)
    features = turned(features.reshape(NY, NZ, part, width), y, z).reshape(count, width)

    received = move_gx(dot(features, w_other).astype(BF16), dc=1)
    total = dot(features, w_mine) + received.astype(F32)

    for steps, kind in ((NY, "dy"), (NZ, "dz")):
        rows = total.shape[0] // steps
        parts = [
            move_gx(total[k * rows : (k + 1) * rows].astype(BF16), **{kind: k})
            for k in range(1, steps)
        ]
        total = total[:rows]
        for piece in parts:
            total = total + piece.astype(F32)

    pairs = total.reshape(part, -1, 2, BLOCK)
    hidden = (jax.nn.silu(pairs[:, :, 0]) * pairs[:, :, 1]).astype(BF16).reshape(part, -1)

    for steps, kind in ((NZ, "dz"), (NY, "dy")):
        hidden = jnp.concatenate(
            [hidden] + [move_gx(hidden, **{kind: -k}) for k in range(1, steps)], axis=0
        )
    theirs = move_gx(hidden, dc=1)
    terms = dot(hidden, d_mine) + dot(theirs, d_other)

    terms = turned(terms.reshape(NY, NZ, part, -1), (NY - y) % NY, (NZ - z) % NZ)
    terms = terms.reshape(NG, count // NG, -1)
    result = terms[0]
    for piece in [move_gy(terms[k].astype(BF16), NG - k) for k in range(1, NG)]:
        result = result + piece.astype(F32)
    return result.astype(BF16)


def solution(mesh):
    placed = (
        P("gy", "gx"),
        P("gx", "gy"),
        P("gx", "gy"),
        P("gx", "gy"),
        P("gx", "gy"),
        P("gy", "gx"),
        P("gy", "gx"),
    )
    return jax.shard_map(
        local, mesh=mesh, in_specs=placed, out_specs=P("gy", "gx"), check_vma=False
    )
```

time: 282 us -> 138 us (0.49)
  waiting for transfers between devices: 203 us -> 44.4 us
  starting transfers between devices: 0.09 us -> 52.7 us
  blocking collectives: 31.4 us -> 0 us
  Pallas kernels: 0 us -> 25.8 us
  local copies, waits for them, and re-layouts: 24.6 us -> 3.21 us
  between operations: 13.2 us -> 0.28 us
  matrix products: 4.26 us -> 8.54 us
  other arithmetic: 4.8 us -> 1.52 us
    unnamed x4 -> x0, waiting for transfers between devices: 113 us -> none
    ppermute x0 -> x28, starting transfers between devices: none -> 52.7 us  [the longest x14 29 us: move_gx(): return lax.ppermute(x, 'gx', gx_pairs(dz, dy, dc))]
    all_gather x1 -> x0, waiting for transfers between devices: 51.5 us -> none  [local(): lax.all_gather(hidden_units, 'gx', axis=0, tiled=True)]
    ppermute x0 -> x28, waiting for transfers between devices: none -> 44.4 us  [the longest x14 36.3 us: move_gx(): return lax.ppermute(x, 'gx', gx_pairs(dz, dy, dc))]
    reduce_scatter x1 -> x0, waiting for transfers between devices: 38.8 us -> none  [local(): lax.psum_scatter(terms, 'gy', scatter_dimension=0, tiled=True)]
    all_gather x1 -> x0, blocking collectives: 31.4 us -> none  [local(): features = lax.all_gather(tokens, 'gy', axis=0, tiled=True)]
    pallas_call x0 -> x4, Pallas kernels: none -> 25.8 us  [the longest x2 18 us: pair_weights(): pl.pallas_call(pair_kernel, out_shape=jax.ShapeDtypeStruct((rows, columns...]
    unnamed x20 -> x21, local copies, waits for them, and re-layouts: 20.1 us -> 2.41 us
  transfers between devices with their start and end apart: 3 -> 28, of which waited for: 3 -> 13; matrix products, arithmetic and copies ran while one was open for 0% -> 1% of each run, Pallas kernels for 0% -> 19%
where the time goes in v1:
time: 138 us; the launch traced here: 136 us
  starting transfers between devices  52.7 us (38%)
  waiting for transfers between devices  44.4 us (32%)
  Pallas kernels  25.8 us (19%)
  matrix products  8.54 us (6%)
  local copies, waits for them, and re-layouts  3.21 us (2%)
  other arithmetic  1.52 us (1%)
    ppermute x14, waiting for transfers between devices, move_gx(): return lax.ppermute(x, 'gx', gx_pairs(dz, dy, dc))  36.3 us
    ppermute x14, starting transfers between devices, move_gx(): return lax.ppermute(x, 'gx', gx_pairs(dz, dy, dc))  29 us
    ppermute x14, starting transfers between devices, move_gy(): return lax.ppermute(x, 'gy', [(i, (i + k) % NG) for i in range(NG)])  23.7 us
    pallas_call x2, Pallas kernels, pair_weights(): pl.pallas_call(pair_kernel, out_shape=jax.ShapeDtypeStruct((rows, columns...  18 us
    dot_general x4, matrix products, dot(): lax.dot_general(a, b, (((1,), (0,)), ((), ())), preferred_element_type=F32)  8.54 us
    ppermute x14, waiting for transfers between devices, move_gy(): return lax.ppermute(x, 'gy', [(i, (i + k) % NG) for i in range(NG)])  8.13 us
    pallas_call x2, Pallas kernels, down_weights(): pl.pallas_call(down_kernel, out_shape=jax.ShapeDtypeStruct((rows, columns...  7.8 us
  transfers between devices with their start and end apart: 28, of which 13 were waited for; matrix products, arithmetic and copies ran while one was open for 1% of the time, Pallas kernels for 19%

profile of v1, /device:TPU:8, one launch (start us, length us, event | category | flops | bytes accessed | tf_op | source)
XLA Modules:
  0.0 136.5 jit_solution(7510124600352936227)
XLA Ops:
  0.0 1.5 %collective-permute-start = (bf16[32,512]{1,0:T(8,128)(2,1)}, bf16[32,512]{1,0:T(8,128)(2,1)S(1)}, u32[]{:S(2)}, u32[]{:S(2)}) collective-permute-start(bf16[32,512]{1,0:T(8,128)(2,1)} %param.7), channel_id=1, source_target_pairs={{0,1},{1,2},{2,3},{3,4},{4,5},{5,6},{6,7},{7,0},{8,9},{9,10},{10,1... | collective-permute-start | bytes 98312 | tf_op jit(solution)/shard_map/ppermute | solution.py:30
  1.5 2.7 %collective-permute-start.1 = (bf16[32,512]{1,0:T(8,128)(2,1)}, bf16[32,512]{1,0:T(8,128)(2,1)S(1)}, u32[]{:S(2)}, u32[]{:S(2)}) collective-permute-start(bf16[32,512]{1,0:T(8,128)(2,1)} %param.7), channel_id=1, source_target_pairs={{0,2},{1,3},{2,4},{3,5},{4,6},{5,7},{6,0},{7,1},{8,10},{9,11},{10,... | collective-permute-start | bytes 98312 | tf_op jit(solution)/shard_map/ppermute | solution.py:30
  4.2 2.8 %collective-permute-start.2 = (bf16[32,512]{1,0:T(8,128)(2,1)}, bf16[32,512]{1,0:T(8,128)(2,1)S(1)}, u32[]{:S(2)}, u32[]{:S(2)}) collective-permute-start(bf16[32,512]{1,0:T(8,128)(2,1)} %param.7), channel_id=1, source_target_pairs={{0,3},{1,4},{2,5},{3,6},{4,7},{5,0},{6,1},{7,2},{8,11},{9,12},{10,... | collective-permute-start | bytes 98312 | tf_op jit(solution)/shard_map/ppermute | solution.py:30
  7.1 1.9 %collective-permute-start.4 = (bf16[32,512]{1,0:T(8,128)(2,1)}, bf16[32,512]{1,0:T(8,128)(2,1)S(1)}, u32[]{:S(2)}, u32[]{:S(2)}) collective-permute-start(bf16[32,512]{1,0:T(8,128)(2,1)} %param.7), channel_id=1, source_target_pairs={{0,5},{1,6},{2,7},{3,0},{4,1},{5,2},{6,3},{7,4},{8,13},{9,14},{10,... | collective-permute-start | bytes 98312 | tf_op jit(solution)/shard_map/ppermute | solution.py:30
  9.1 0.8 constant_dynamic-update-slice_fusion.7
  9.9 9.0 %shard_map.74 = bf16[512,3328]{1,0:T(8,128)(2,1)} custom-call(s32[1]{0:T(128)S(6)} %sub.18.half, bf16[512,3328]{1,0:T(8,128)(2,1)} %gate.3, bf16[512,3328]{1,0:T(8,128)(2,1)} %up.3, f32[4,26]{1,0:T(4,128)} %gate_scales.3, f32[4,26]{1,0:T(4,128)} %up_scales.3), custom_call_target="tpu_custom_call" | custom-call | flops 3407872 | bytes 6815744 | tf_op jit(solution)/shard_map/pallas_call | solution.py:50
  18.9 1.8 %collective-permute-start.5 = (bf16[32,512]{1,0:T(8,128)(2,1)S(1)}, bf16[32,512]{1,0:T(8,128)(2,1)S(1)}, u32[]{:S(2)}, u32[]{:S(2)}) collective-permute-start(bf16[32,512]{1,0:T(8,128)(2,1)S(1)} %copy-done.2), channel_id=1, source_target_pairs={{0,6},{1,7},{2,0},{3,1},{4,2},{5,3},{6,4},{7,5},{8,14},{9,15},{10,... | collective-permute-start | bytes 98312 | tf_op jit(solution)/shard_map/ppermute | solution.py:30
  20.7 1.7 %collective-permute-start.6 = (bf16[32,512]{1,0:T(8,128)(2,1)S(1)}, bf16[32,512]{1,0:T(8,128)(2,1)S(1)}, u32[]{:S(2)}, u32[]{:S(2)}) collective-permute-start(bf16[32,512]{1,0:T(8,128)(2,1)S(1)} %copy-done.2), channel_id=1, source_target_pairs={{0,7},{1,0},{2,1},{3,2},{4,3},{5,4},{6,5},{7,6},{8,15},{9,8},{10,9... | collective-permute-start | bytes 98312 | tf_op jit(solution)/shard_map/ppermute | solution.py:30
  22.5 1.9 %collective-permute-done.5 = bf16[32,512]{1,0:T(8,128)(2,1)S(1)} collective-permute-done((bf16[32,512]{1,0:T(8,128)(2,1)S(1)}, bf16[32,512]{1,0:T(8,128)(2,1)S(1)}, u32[]{:S(2)}, u32[]{:S(2)}) %collective-permute-start.5) | collective-permute-done | bytes 32800 | tf_op jit(solution)/shard_map/ppermute | solution.py:30
  24.4 0.2 collective-permute-done.6
  24.8 4.3 %convolution_convert_fusion = bf16[256,3328]{1,0:T(8,128)(2,1)} fusion(bf16[256,512]{1,0:T(8,128)(2,1)S(1)} %bitcast.68, bf16[512,3328]{1,0:T(8,128)(2,1)} %shard_map.74), kind=kOutput, calls=%fused_computation | convolution fusion | flops 873267200 | bytes 5373952 | tf_op jit(solution)/shard_map/dot_general | solution.py:100
  29.1 9.0 %shard_map.73 = bf16[512,3328]{1,0:T(8,128)(2,1)} custom-call(s32[1]{0:T(128)} %bitcast.2.half, bf16[512,3328]{1,0:T(8,128)(2,1)} %gate.3, bf16[512,3328]{1,0:T(8,128)(2,1)} %up.3, f32[4,26]{1,0:T(4,128)} %gate_scales.3, f32[4,26]{1,0:T(4,128)} %up_scales.3), custom_call_target="tpu_custom_call" | custom-call | flops 3407872 | bytes 6815744 | tf_op jit(solution)/shard_map/pallas_call | solution.py:50
  38.1 3.0 %fusion.23 = (bf16[256,3328]{1,0:T(8,128)(2,1)S(1)}, f32[256,3328]{1,0:T(8,128)S(1)}) fusion(bf16[256,3328]{1,0:T(8,128)(2,1)S(1)} %collective-permute-done.7, bf16[256,512]{1,0:T(8,128)(2,1)S(1)} %bitcast.69, bf16[512,3328]{1,0:T(8,128)(2,1)} %shard_map.73), kind=kOutput, calls=%fused_computation.63 | convolution fusion | flops 874971136 | bytes 10485760 | tf_op jit(solution)/shard_map/dot_general | solution.py:100
  41.2 0.5 collective-permute-start.10
  41.7 1.6 %collective-permute-start.8 = (bf16[64,3328]{1,0:T(8,128)(2,1)S(1)}, bf16[64,3328]{1,0:T(8,128)(2,1)S(1)}, u32[]{:S(2)}, u32[]{:S(2)}) collective-permute-start(bf16[64,3328]{1,0:T(8,128)(2,1)S(1)} %get-tuple-element.13), channel_id=1, source_target_pairs={{0,16},{8,24},{16,32},{24,40},{32,48},{40,56},{48,0},{56,8},{64,80... | collective-permute-start | bytes 1277960 | tf_op jit(solution)/shard_map/ppermute | solution.py:26
  43.3 3.5 %collective-permute-start.9 = (bf16[64,3328]{1,0:T(8,128)(2,1)S(1)}, bf16[64,3328]{1,0:T(8,128)(2,1)S(1)}, u32[]{:S(2)}, u32[]{:S(2)}) collective-permute-start(bf16[64,3328]{1,0:T(8,128)(2,1)S(1)} %get-tuple-element.15), channel_id=1, source_target_pairs={{0,32},{8,40},{16,48},{24,56},{32,0},{40,8},{48,16},{56,24},{64,96... | collective-permute-start | bytes 1277960 | tf_op jit(solution)/shard_map/ppermute | solution.py:26
  46.8 6.7 %collective-permute-done.10 = bf16[64,3328]{1,0:T(8,128)(2,1)S(1)} collective-permute-done((bf16[64,3328]{1,0:T(8,128)(2,1)S(1)}, bf16[64,3328]{1,0:T(8,128)(2,1)S(1)}, u32[]{:S(2)}, u32[]{:S(2)}) %collective-permute-start.10) | collective-permute-done | bytes 426016 | tf_op jit(solution)/shard_map/ppermute | solution.py:26
  53.5 1.8 %collective-permute-done.8 = bf16[64,3328]{1,0:T(8,128)(2,1)S(1)} collective-permute-done((bf16[64,3328]{1,0:T(8,128)(2,1)S(1)}, bf16[64,3328]{1,0:T(8,128)(2,1)S(1)}, u32[]{:S(2)}, u32[]{:S(2)}) %collective-permute-start.8) | collective-permute-done | bytes 426016 | tf_op jit(solution)/shard_map/ppermute | solution.py:26
  55.3 8.3 %collective-permute-done.9 = bf16[64,3328]{1,0:T(8,128)(2,1)S(1)} collective-permute-done((bf16[64,3328]{1,0:T(8,128)(2,1)S(1)}, bf16[64,3328]{1,0:T(8,128)(2,1)S(1)}, u32[]{:S(2)}, u32[]{:S(2)}) %collective-permute-start.9) | collective-permute-done | bytes 426016 | tf_op jit(solution)/shard_map/ppermute | solution.py:26
  63.6 0.2 fusion.21
  63.8 3.3 %collective-permute-start.11 = (bf16[16,3328]{1,0:T(8,128)(2,1)S(1)}, bf16[16,3328]{1,0:T(8,128)(2,1)S(1)}, u32[]{:S(2)}, u32[]{:S(2)}) collective-permute-start(bf16[16,3328]{1,0:T(8,128)(2,1)S(1)} %get-tuple-element.16), channel_id=1, source_target_pairs={{0,64},{8,72},{16,80},{24,88},{32,96},{40,104},{48,112},{56,120},{... | collective-permute-start | bytes 319496 | tf_op jit(solution)/shard_map/ppermute | solution.py:26
  67.2 4.8 %collective-permute-start.12 = (bf16[16,3328]{1,0:T(8,128)(2,1)S(1)}, bf16[16,3328]{1,0:T(8,128)(2,1)S(1)}, u32[]{:S(2)}, u32[]{:S(2)}) collective-permute-start(bf16[16,3328]{1,0:T(8,128)(2,1)S(1)} %get-tuple-element.18), channel_id=1, source_target_pairs={{0,128},{8,136},{16,144},{24,152},{32,160},{40,168},{48,176},{56,1... | collective-permute-start | bytes 319496 | tf_op jit(solution)/shard_map/ppermute | solution.py:26
  72.0 2.7 %collective-permute-start.13 = (bf16[16,3328]{1,0:T(8,128)(2,1)S(1)}, bf16[16,3328]{1,0:T(8,128)(2,1)S(1)}, u32[]{:S(2)}, u32[]{:S(2)}) collective-permute-start(bf16[16,3328]{1,0:T(8,128)(2,1)S(1)} %get-tuple-element.17), channel_id=1, source_target_pairs={{0,192},{8,200},{16,208},{24,216},{32,224},{40,232},{48,240},{56,2... | collective-permute-start | bytes 319496 | tf_op jit(solution)/shard_map/ppermute | solution.py:26
  74.7 4.5 %collective-permute-done.12 = bf16[16,3328]{1,0:T(8,128)(2,1)S(1)} collective-permute-done((bf16[16,3328]{1,0:T(8,128)(2,1)S(1)}, bf16[16,3328]{1,0:T(8,128)(2,1)S(1)}, u32[]{:S(2)}, u32[]{:S(2)}) %collective-permute-start.12) | collective-permute-done | bytes 106528 | tf_op jit(solution)/shard_map/ppermute | solution.py:26
  79.2 2.8 %collective-permute-done.13 = bf16[16,3328]{1,0:T(8,128)(2,1)S(1)} collective-permute-done((bf16[16,3328]{1,0:T(8,128)(2,1)S(1)}, bf16[16,3328]{1,0:T(8,128)(2,1)S(1)}, u32[]{:S(2)}, u32[]{:S(2)}) %collective-permute-start.13) | collective-permute-done | bytes 106528 | tf_op jit(solution)/shard_map/ppermute | solution.py:26
  82.2 0.5 slice_reduce_fusion.1
  82.8 3.7 %collective-permute-start.14 = (bf16[16,1664]{1,0:T(8,128)(2,1)S(1)}, bf16[16,1664]{1,0:T(8,128)(2,1)S(1)}, u32[]{:S(2)}, u32[]{:S(2)}) collective-permute-start(bf16[16,1664]{1,0:T(8,128)(2,1)S(1)} %get-tuple-element.8), channel_id=1, source_target_pairs={{0,192},{8,200},{16,208},{24,216},{32,224},{40,232},{48,240},{56,2... | collective-permute-start | bytes 159752 | tf_op jit(solution)/shard_map/ppermute | solution.py:26
  86.5 0.8 collective-permute-start.15
  87.2 2.8 %collective-permute-start.16 = (bf16[16,1664]{1,0:T(8,128)(2,1)S(1)}, bf16[16,1664]{1,0:T(8,128)(2,1)S(1)}, u32[]{:S(2)}, u32[]{:S(2)}) collective-permute-start(bf16[16,1664]{1,0:T(8,128)(2,1)S(1)} %get-tuple-element.8), channel_id=1, source_target_pairs={{0,64},{8,72},{16,80},{24,88},{32,96},{40,104},{48,112},{56,120},{... | collective-permute-start | bytes 159752 | tf_op jit(solution)/shard_map/ppermute | solution.py:26
  90.1 5.6 %collective-permute-done.15 = bf16[16,1664]{1,0:T(8,128)(2,1)S(1)} collective-permute-done((bf16[16,1664]{1,0:T(8,128)(2,1)S(1)}, bf16[16,1664]{1,0:T(8,128)(2,1)S(1)}, u32[]{:S(2)}, u32[]{:S(2)}) %collective-permute-start.15) | collective-permute-done | bytes 53280 | tf_op jit(solution)/shard_map/ppermute | solution.py:26
  95.7 3.5 %collective-permute-start.17 = (bf16[64,1664]{1,0:T(8,128)(2,1)S(1)}, bf16[64,1664]{1,0:T(8,128)(2,1)S(1)}, u32[]{:S(2)}, u32[]{:S(2)}) collective-permute-start(bf16[64,1664]{1,0:T(8,128)(2,1)S(1)} %pad_maximum_fusion), channel_id=1, source_target_pairs={{0,48},{8,56},{16,0},{24,8},{32,16},{40,24},{48,32},{56,40},{64,11... | collective-permute-start | bytes 638984 | tf_op jit(solution)/shard_map/ppermute | solution.py:26
  99.2 1.7 %collective-permute-start.19 = (bf16[64,1664]{1,0:T(8,128)(2,1)S(1)}, bf16[64,1664]{1,0:T(8,128)(2,1)S(1)}, u32[]{:S(2)}, u32[]{:S(2)}) collective-permute-start(bf16[64,1664]{1,0:T(8,128)(2,1)S(1)} %pad_maximum_fusion), channel_id=1, source_target_pairs={{0,16},{8,24},{16,32},{24,40},{32,48},{40,56},{48,0},{56,8},{64,80... | collective-permute-start | bytes 638984 | tf_op jit(solution)/shard_map/ppermute | solution.py:26
  101.0 3.0 %collective-permute-done.17 = bf16[64,1664]{1,0:T(8,128)(2,1)S(1)} collective-permute-done((bf16[64,1664]{1,0:T(8,128)(2,1)S(1)}, bf16[64,1664]{1,0:T(8,128)(2,1)S(1)}, u32[]{:S(2)}, u32[]{:S(2)}) %collective-permute-start.17) | collective-permute-done | bytes 213024 | tf_op jit(solution)/shard_map/ppermute | solution.py:26
  104.0 3.5 %collective-permute-done.18 = bf16[64,1664]{1,0:T(8,128)(2,1)S(1)} collective-permute-done((bf16[64,1664]{1,0:T(8,128)(2,1)S(1)}, bf16[64,1664]{1,0:T(8,128)(2,1)S(1)}, u32[]{:S(2)}, u32[]{:S(2)}) %collective-permute-start.18) | collective-permute-done | bytes 213024 | tf_op jit(solution)/shard_map/ppermute | solution.py:26
  107.8 0.7 copy.8.scales
  108.4 3.9 %shard_map.76 = bf16[1664,512]{1,0:T(8,128)(2,1)} custom-call(s32[1]{0:T(128)S(6)} %sub.18.half, bf16[3328,512]{1,0:T(8,128)(2,1)} %payload.3, f32[26,4]{1,0:T(8,128)} %copy.8.scales), custom_call_target="tpu_custom_call" | custom-call | flops 851968 | bytes 3407872 | tf_op jit(solution)/shard_map/pallas_call | solution.py:76
  112.3 3.9 %shard_map.75 = bf16[1664,512]{1,0:T(8,128)(2,1)} custom-call(s32[1]{0:T(128)} %bitcast.2.half, bf16[3328,512]{1,0:T(8,128)(2,1)} %payload.3, f32[26,4]{1,0:T(8,128)} %copy.8.scales), custom_call_target="tpu_custom_call" | custom-call | flops 851968 | bytes 3407872 | tf_op jit(solution)/shard_map/pallas_call | solution.py:76
  116.3 0.6 fusion.26
  116.9 0.8 copy-done
  117.7 0.6 convolution_add_fusion
  118.7 0.8 collective-permute-start.21
  119.5 1.6 %collective-permute-start.22 = (bf16[32,512]{1,0:T(8,128)(2,1)S(1)}, bf16[32,512]{1,0:T(8,128)(2,1)S(1)}, u32[]{:S(2)}, u32[]{:S(2)}) collective-permute-start(bf16[32,512]{1,0:T(8,128)(2,1)S(1)} %get-tuple-element.25), channel_id=1, source_target_pairs={{0,6},{1,7},{2,0},{3,1},{4,2},{5,3},{6,4},{7,5},{8,14},{9,15},{10,... | collective-permute-start | bytes 98312 | tf_op jit(solution)/shard_map/ppermute | solution.py:30
  121.1 2.7 %collective-permute-start.23 = (bf16[32,512]{1,0:T(8,128)(2,1)S(1)}, bf16[32,512]{1,0:T(8,128)(2,1)S(1)}, u32[]{:S(2)}, u32[]{:S(2)}) collective-permute-start(bf16[32,512]{1,0:T(8,128)(2,1)S(1)} %get-tuple-element.24), channel_id=1, source_target_pairs={{0,5},{1,6},{2,7},{3,0},{4,1},{5,2},{6,3},{7,4},{8,13},{9,14},{10,... | collective-permute-start | bytes 98312 | tf_op jit(solution)/shard_map/ppermute | solution.py:30
  123.7 2.9 %collective-permute-start.25 = (bf16[32,512]{1,0:T(8,128)(2,1)S(1)}, bf16[32,512]{1,0:T(8,128)(2,1)S(1)}, u32[]{:S(2)}, u32[]{:S(2)}) collective-permute-start(bf16[32,512]{1,0:T(8,128)(2,1)S(1)} %get-tuple-element.22), channel_id=1, source_target_pairs={{0,3},{1,4},{2,5},{3,6},{4,7},{5,0},{6,1},{7,2},{8,11},{9,12},{10,... | collective-permute-start | bytes 98312 | tf_op jit(solution)/shard_map/ppermute | solution.py:30
  126.6 3.2 %collective-permute-start.26 = (bf16[32,512]{1,0:T(8,128)(2,1)S(1)}, bf16[32,512]{1,0:T(8,128)(2,1)S(1)}, u32[]{:S(2)}, u32[]{:S(2)}) collective-permute-start(bf16[32,512]{1,0:T(8,128)(2,1)S(1)} %get-tuple-element.21), channel_id=1, source_target_pairs={{0,2},{1,3},{2,4},{3,5},{4,6},{5,7},{6,0},{7,1},{8,10},{9,11},{10,... | collective-permute-start | bytes 98312 | tf_op jit(solution)/shard_map/ppermute | solution.py:30
  130.0 2.9 %collective-permute-done.26 = bf16[32,512]{1,0:T(8,128)(2,1)S(1)} collective-permute-done((bf16[32,512]{1,0:T(8,128)(2,1)S(1)}, bf16[32,512]{1,0:T(8,128)(2,1)S(1)}, u32[]{:S(2)}, u32[]{:S(2)}) %collective-permute-start.26) | collective-permute-done | bytes 32800 | tf_op jit(solution)/shard_map/ppermute | solution.py:30
  132.9 2.9 %collective-permute-done.27 = bf16[32,512]{1,0:T(8,128)(2,1)S(1)} collective-permute-done((bf16[32,512]{1,0:T(8,128)(2,1)S(1)}, bf16[32,512]{1,0:T(8,128)(2,1)S(1)}, u32[]{:S(2)}, u32[]{:S(2)}) %collective-permute-start.27) | collective-permute-done | bytes 32800 | tf_op jit(solution)/shard_map/ppermute | solution.py:30
  135.8 0.7 fusion.19
  (54 shorter events, 1.4 us)
Async XLA Ops:
  0.0 18.9 %collective-permute-start = (bf16[32,512]{1,0:T(8,128)(2,1)}, bf16[32,512]{1,0:T(8,128)(2,1)S(1)}, u32[]{:S(2)}, u32[]{:S(2)}) collective-permute-start(bf16[32,512]{1,0:T(8,128)(2,1)} %param.7), channel_id=1, source_target_pairs={{0,1},{1,2},{2,3},{3,4},{4,5},{5,6},{6,7},{7,0},{8,9},{9,10},{10,1... | collective-permute-start | bytes 98312 | tf_op jit(solution)/shard_map/ppermute | solution.py:30
  1.5 19.2 %collective-permute-start.1 = (bf16[32,512]{1,0:T(8,128)(2,1)}, bf16[32,512]{1,0:T(8,128)(2,1)S(1)}, u32[]{:S(2)}, u32[]{:S(2)}) collective-permute-start(bf16[32,512]{1,0:T(8,128)(2,1)} %param.7), channel_id=1, source_target_pairs={{0,2},{1,3},{2,4},{3,5},{4,6},{5,7},{6,0},{7,1},{8,10},{9,11},{10,... | collective-permute-start | bytes 98312 | tf_op jit(solution)/shard_map/ppermute | solution.py:30
  4.2 18.2 %collective-permute-start.2 = (bf16[32,512]{1,0:T(8,128)(2,1)}, bf16[32,512]{1,0:T(8,128)(2,1)S(1)}, u32[]{:S(2)}, u32[]{:S(2)}) collective-permute-start(bf16[32,512]{1,0:T(8,128)(2,1)} %param.7), channel_id=1, source_target_pairs={{0,3},{1,4},{2,5},{3,6},{4,7},{5,0},{6,1},{7,2},{8,11},{9,12},{10,... | collective-permute-start | bytes 98312 | tf_op jit(solution)/shard_map/ppermute | solution.py:30
  7.0 15.4 %collective-permute-start.3 = (bf16[32,512]{1,0:T(8,128)(2,1)}, bf16[32,512]{1,0:T(8,128)(2,1)S(1)}, u32[]{:S(2)}, u32[]{:S(2)}) collective-permute-start(bf16[32,512]{1,0:T(8,128)(2,1)} %param.7), channel_id=1, source_target_pairs={{0,4},{1,5},{2,6},{3,7},{4,0},{5,1},{6,2},{7,3},{8,12},{9,13},{10,... | collective-permute-start | bytes 98312 | tf_op jit(solution)/shard_map/ppermute | solution.py:30
  7.1 15.3 %collective-permute-start.4 = (bf16[32,512]{1,0:T(8,128)(2,1)}, bf16[32,512]{1,0:T(8,128)(2,1)S(1)}, u32[]{:S(2)}, u32[]{:S(2)}) collective-permute-start(bf16[32,512]{1,0:T(8,128)(2,1)} %param.7), channel_id=1, source_target_pairs={{0,5},{1,6},{2,7},{3,0},{4,1},{5,2},{6,3},{7,4},{8,13},{9,14},{10,... | collective-permute-start | bytes 98312 | tf_op jit(solution)/shard_map/ppermute | solution.py:30
  9.9 9.0 %copy-start.2 = (bf16[32,512]{1,0:T(8,128)(2,1)S(1)}, bf16[32,512]{1,0:T(8,128)(2,1)}, u32[]{:S(2)}) copy-start(bf16[32,512]{1,0:T(8,128)(2,1)} %param.7) | copy-start | bytes 98308
  18.9 5.5 %collective-permute-start.5 = (bf16[32,512]{1,0:T(8,128)(2,1)S(1)}, bf16[32,512]{1,0:T(8,128)(2,1)S(1)}, u32[]{:S(2)}, u32[]{:S(2)}) collective-permute-start(bf16[32,512]{1,0:T(8,128)(2,1)S(1)} %copy-done.2), channel_id=1, source_target_pairs={{0,6},{1,7},{2,0},{3,1},{4,2},{5,3},{6,4},{7,5},{8,14},{9,15},{10,... | collective-permute-start | bytes 98312 | tf_op jit(solution)/shard_map/ppermute | solution.py:30
  20.7 3.9 %collective-permute-start.6 = (bf16[32,512]{1,0:T(8,128)(2,1)S(1)}, bf16[32,512]{1,0:T(8,128)(2,1)S(1)}, u32[]{:S(2)}, u32[]{:S(2)}) collective-permute-start(bf16[32,512]{1,0:T(8,128)(2,1)S(1)} %copy-done.2), channel_id=1, source_target_pairs={{0,7},{1,0},{2,1},{3,2},{4,3},{5,4},{6,5},{7,6},{8,15},{9,8},{10,9... | collective-permute-start | bytes 98312 | tf_op jit(solution)/shard_map/ppermute | solution.py:30
  29.1 9.0 %collective-permute-start.7 = (bf16[256,3328]{1,0:T(8,128)(2,1)}, bf16[256,3328]{1,0:T(8,128)(2,1)S(1)}, u32[]{:S(2)}, u32[]{:S(2)}) collective-permute-start(bf16[256,3328]{1,0:T(8,128)(2,1)} %convolution_convert_fusion), channel_id=1, source_target_pairs={{0,8},{8,0},{16,24},{24,16},{32,40},{40,32},{48,56},{56,48},{64,72... | collective-permute-start | bytes 5111816 | tf_op jit(solution)/shard_map/ppermute | solution.py:26
  41.2 12.3 %collective-permute-start.10 = (bf16[64,3328]{1,0:T(8,128)(2,1)S(1)}, bf16[64,3328]{1,0:T(8,128)(2,1)S(1)}, u32[]{:S(2)}, u32[]{:S(2)}) collective-permute-start(bf16[64,3328]{1,0:T(8,128)(2,1)S(1)} %get-tuple-element.14), channel_id=1, source_target_pairs={{0,48},{8,56},{16,0},{24,8},{32,16},{40,24},{48,32},{56,40},{64,11... | collective-permute-start | bytes 1277960 | tf_op jit(solution)/shard_map/ppermute | solution.py:26
  41.7 13.6 %collective-permute-start.8 = (bf16[64,3328]{1,0:T(8,128)(2,1)S(1)}, bf16[64,3328]{1,0:T(8,128)(2,1)S(1)}, u32[]{:S(2)}, u32[]{:S(2)}) collective-permute-start(bf16[64,3328]{1,0:T(8,128)(2,1)S(1)} %get-tuple-element.13), channel_id=1, source_target_pairs={{0,16},{8,24},{16,32},{24,40},{32,48},{40,56},{48,0},{56,8},{64,80... | collective-permute-start | bytes 1277960 | tf_op jit(solution)/shard_map/ppermute | solution.py:26
  43.3 20.3 %collective-permute-start.9 = (bf16[64,3328]{1,0:T(8,128)(2,1)S(1)}, bf16[64,3328]{1,0:T(8,128)(2,1)S(1)}, u32[]{:S(2)}, u32[]{:S(2)}) collective-permute-start(bf16[64,3328]{1,0:T(8,128)(2,1)S(1)} %get-tuple-element.15), channel_id=1, source_target_pairs={{0,32},{8,40},{16,48},{24,56},{32,0},{40,8},{48,16},{56,24},{64,96... | collective-permute-start | bytes 1277960 | tf_op jit(solution)/shard_map/ppermute | solution.py:26
  63.6 44.1 %copy-start.3 = (f32[26,4]{0,1:T(4,128)S(1)}, f32[26,4]{0,1:T(4,128)}, u32[]{:S(2)}) copy-start(f32[26,4]{0,1:T(4,128)} %param.13) | copy-start | bytes 1252
  63.8 10.9 %collective-permute-start.11 = (bf16[16,3328]{1,0:T(8,128)(2,1)S(1)}, bf16[16,3328]{1,0:T(8,128)(2,1)S(1)}, u32[]{:S(2)}, u32[]{:S(2)}) collective-permute-start(bf16[16,3328]{1,0:T(8,128)(2,1)S(1)} %get-tuple-element.16), channel_id=1, source_target_pairs={{0,64},{8,72},{16,80},{24,88},{32,96},{40,104},{48,112},{56,120},{... | collective-permute-start | bytes 319496 | tf_op jit(solution)/shard_map/ppermute | solution.py:26
  67.2 12.0 %collective-permute-start.12 = (bf16[16,3328]{1,0:T(8,128)(2,1)S(1)}, bf16[16,3328]{1,0:T(8,128)(2,1)S(1)}, u32[]{:S(2)}, u32[]{:S(2)}) collective-permute-start(bf16[16,3328]{1,0:T(8,128)(2,1)S(1)} %get-tuple-element.18), channel_id=1, source_target_pairs={{0,128},{8,136},{16,144},{24,152},{32,160},{40,168},{48,176},{56,1... | collective-permute-start | bytes 319496 | tf_op jit(solution)/shard_map/ppermute | solution.py:26
  72.0 9.9 %collective-permute-start.13 = (bf16[16,3328]{1,0:T(8,128)(2,1)S(1)}, bf16[16,3328]{1,0:T(8,128)(2,1)S(1)}, u32[]{:S(2)}, u32[]{:S(2)}) collective-permute-start(bf16[16,3328]{1,0:T(8,128)(2,1)S(1)} %get-tuple-element.17), channel_id=1, source_target_pairs={{0,192},{8,200},{16,208},{24,216},{32,224},{40,232},{48,240},{56,2... | collective-permute-start | bytes 319496 | tf_op jit(solution)/shard_map/ppermute | solution.py:26
  82.8 7.3 %collective-permute-start.14 = (bf16[16,1664]{1,0:T(8,128)(2,1)S(1)}, bf16[16,1664]{1,0:T(8,128)(2,1)S(1)}, u32[]{:S(2)}, u32[]{:S(2)}) collective-permute-start(bf16[16,1664]{1,0:T(8,128)(2,1)S(1)} %get-tuple-element.8), channel_id=1, source_target_pairs={{0,192},{8,200},{16,208},{24,216},{32,224},{40,232},{48,240},{56,2... | collective-permute-start | bytes 159752 | tf_op jit(solution)/shard_map/ppermute | solution.py:26
  86.5 9.2 %collective-permute-start.15 = (bf16[16,1664]{1,0:T(8,128)(2,1)S(1)}, bf16[16,1664]{1,0:T(8,128)(2,1)S(1)}, u32[]{:S(2)}, u32[]{:S(2)}) collective-permute-start(bf16[16,1664]{1,0:T(8,128)(2,1)S(1)} %get-tuple-element.8), channel_id=1, source_target_pairs={{0,128},{8,136},{16,144},{24,152},{32,160},{40,168},{48,176},{56,1... | collective-permute-start | bytes 159752 | tf_op jit(solution)/shard_map/ppermute | solution.py:26
  87.2 8.5 %collective-permute-start.16 = (bf16[16,1664]{1,0:T(8,128)(2,1)S(1)}, bf16[16,1664]{1,0:T(8,128)(2,1)S(1)}, u32[]{:S(2)}, u32[]{:S(2)}) collective-permute-start(bf16[16,1664]{1,0:T(8,128)(2,1)S(1)} %get-tuple-element.8), channel_id=1, source_target_pairs={{0,64},{8,72},{16,80},{24,88},{32,96},{40,104},{48,112},{56,120},{... | collective-permute-start | bytes 159752 | tf_op jit(solution)/shard_map/ppermute | solution.py:26
  95.7 8.3 %collective-permute-start.17 = (bf16[64,1664]{1,0:T(8,128)(2,1)S(1)}, bf16[64,1664]{1,0:T(8,128)(2,1)S(1)}, u32[]{:S(2)}, u32[]{:S(2)}) collective-permute-start(bf16[64,1664]{1,0:T(8,128)(2,1)S(1)} %pad_maximum_fusion), channel_id=1, source_target_pairs={{0,48},{8,56},{16,0},{24,8},{32,16},{40,24},{48,32},{56,40},{64,11... | collective-permute-start | bytes 638984 | tf_op jit(solution)/shard_map/ppermute | solution.py:26
  99.2 8.3 %collective-permute-start.18 = (bf16[64,1664]{1,0:T(8,128)(2,1)S(1)}, bf16[64,1664]{1,0:T(8,128)(2,1)S(1)}, u32[]{:S(2)}, u32[]{:S(2)}) collective-permute-start(bf16[64,1664]{1,0:T(8,128)(2,1)S(1)} %pad_maximum_fusion), channel_id=1, source_target_pairs={{0,32},{8,40},{16,48},{24,56},{32,0},{40,8},{48,16},{56,24},{64,96... | collective-permute-start | bytes 638984 | tf_op jit(solution)/shard_map/ppermute | solution.py:26
  99.2 8.4 %collective-permute-start.19 = (bf16[64,1664]{1,0:T(8,128)(2,1)S(1)}, bf16[64,1664]{1,0:T(8,128)(2,1)S(1)}, u32[]{:S(2)}, u32[]{:S(2)}) collective-permute-start(bf16[64,1664]{1,0:T(8,128)(2,1)S(1)} %pad_maximum_fusion), channel_id=1, source_target_pairs={{0,16},{8,24},{16,32},{24,40},{32,48},{40,56},{48,0},{56,8},{64,80... | collective-permute-start | bytes 638984 | tf_op jit(solution)/shard_map/ppermute | solution.py:26
  107.6 8.7 %collective-permute-start.20 = (bf16[256,1664]{1,0:T(8,128)(2,1)S(1)}, bf16[256,1664]{1,0:T(8,128)(2,1)S(1)}, u32[]{:S(2)}, u32[]{:S(2)}) collective-permute-start(bf16[256,1664]{1,0:T(8,128)(2,1)S(1)} %constant_dynamic-update-slice_fusion.8), channel_id=1, source_target_pairs={{0,8},{8,0},{16,24},{24,16},{32,40},{40,32},{48,56},{56,48},{64,72... | collective-permute-start | bytes 2555912 | tf_op jit(solution)/shard_map/ppermute | solution.py:26
  112.3 4.0 %copy-start.1 = (bf16[1664,512]{1,0:T(8,128)(2,1)S(1)}, bf16[1664,512]{1,0:T(8,128)(2,1)}, u32[]{:S(2)}) copy-start(bf16[1664,512]{1,0:T(8,128)(2,1)} %shard_map.76) | copy-start | bytes 5111812
  116.3 1.5 %copy-start = (bf16[1664,512]{1,0:T(8,128)(2,1)S(1)}, bf16[1664,512]{1,0:T(8,128)(2,1)}, u32[]{:S(2)}) copy-start(bf16[1664,512]{1,0:T(8,128)(2,1)} %shard_map.75) | copy-start | bytes 5111812
  118.7 7.9 %collective-permute-start.21 = (bf16[32,512]{1,0:T(8,128)(2,1)S(1)}, bf16[32,512]{1,0:T(8,128)(2,1)S(1)}, u32[]{:S(2)}, u32[]{:S(2)}) collective-permute-start(bf16[32,512]{1,0:T(8,128)(2,1)S(1)} %get-tuple-element.19), channel_id=1, source_target_pairs={{0,7},{1,0},{2,1},{3,2},{4,3},{5,4},{6,5},{7,6},{8,15},{9,8},{10,9... | collective-permute-start | bytes 98312 | tf_op jit(solution)/shard_map/ppermute | solution.py:30
  119.5 10.3 %collective-permute-start.22 = (bf16[32,512]{1,0:T(8,128)(2,1)S(1)}, bf16[32,512]{1,0:T(8,128)(2,1)S(1)}, u32[]{:S(2)}, u32[]{:S(2)}) collective-permute-start(bf16[32,512]{1,0:T(8,128)(2,1)S(1)} %get-tuple-element.25), channel_id=1, source_target_pairs={{0,6},{1,7},{2,0},{3,1},{4,2},{5,3},{6,4},{7,5},{8,14},{9,15},{10,... | collective-permute-start | bytes 98312 | tf_op jit(solution)/shard_map/ppermute | solution.py:30
  121.1 8.7 %collective-permute-start.23 = (bf16[32,512]{1,0:T(8,128)(2,1)S(1)}, bf16[32,512]{1,0:T(8,128)(2,1)S(1)}, u32[]{:S(2)}, u32[]{:S(2)}) collective-permute-start(bf16[32,512]{1,0:T(8,128)(2,1)S(1)} %get-tuple-element.24), channel_id=1, source_target_pairs={{0,5},{1,6},{2,7},{3,0},{4,1},{5,2},{6,3},{7,4},{8,13},{9,14},{10,... | collective-permute-start | bytes 98312 | tf_op jit(solution)/shard_map/ppermute | solution.py:30
  123.7 6.1 %collective-permute-start.24 = (bf16[32,512]{1,0:T(8,128)(2,1)S(1)}, bf16[32,512]{1,0:T(8,128)(2,1)S(1)}, u32[]{:S(2)}, u32[]{:S(2)}) collective-permute-start(bf16[32,512]{1,0:T(8,128)(2,1)S(1)} %get-tuple-element.23), channel_id=1, source_target_pairs={{0,4},{1,5},{2,6},{3,7},{4,0},{5,1},{6,2},{7,3},{8,12},{9,13},{10,... | collective-permute-start | bytes 98312 | tf_op jit(solution)/shard_map/ppermute | solution.py:30
  123.7 6.2 %collective-permute-start.25 = (bf16[32,512]{1,0:T(8,128)(2,1)S(1)}, bf16[32,512]{1,0:T(8,128)(2,1)S(1)}, u32[]{:S(2)}, u32[]{:S(2)}) collective-permute-start(bf16[32,512]{1,0:T(8,128)(2,1)S(1)} %get-tuple-element.22), channel_id=1, source_target_pairs={{0,3},{1,4},{2,5},{3,6},{4,7},{5,0},{6,1},{7,2},{8,11},{9,12},{10,... | collective-permute-start | bytes 98312 | tf_op jit(solution)/shard_map/ppermute | solution.py:30
  126.6 6.3 %collective-permute-start.26 = (bf16[32,512]{1,0:T(8,128)(2,1)S(1)}, bf16[32,512]{1,0:T(8,128)(2,1)S(1)}, u32[]{:S(2)}, u32[]{:S(2)}) collective-permute-start(bf16[32,512]{1,0:T(8,128)(2,1)S(1)} %get-tuple-element.21), channel_id=1, source_target_pairs={{0,2},{1,3},{2,4},{3,5},{4,6},{5,7},{6,0},{7,1},{8,10},{9,11},{10,... | collective-permute-start | bytes 98312 | tf_op jit(solution)/shard_map/ppermute | solution.py:30
  129.8 6.0 %collective-permute-start.27 = (bf16[32,512]{1,0:T(8,128)(2,1)S(1)}, bf16[32,512]{1,0:T(8,128)(2,1)S(1)}, u32[]{:S(2)}, u32[]{:S(2)}) collective-permute-start(bf16[32,512]{1,0:T(8,128)(2,1)S(1)} %get-tuple-element.20), channel_id=1, source_target_pairs={{0,1},{1,2},{2,3},{3,4},{4,5},{5,6},{6,7},{7,0},{8,9},{9,10},{10,1... | collective-permute-start | bytes 98312 | tf_op jit(solution)/shard_map/ppermute | solution.py:30

commit v2 on v0

v2 whole, which is shorter than its diff:
```python
import jax
import jax.numpy as jnp
from jax import lax
from jax.experimental import pallas as pl
from jax.experimental.pallas import tpu as pltpu
from jax.sharding import PartitionSpec as P

BLOCK = 128
F32 = jnp.float32
BF16 = jnp.bfloat16
NZ, NY, NC, NL, NX = 4, 4, 2, 2, 4
ROWS = 8
SMEM = pl.BlockSpec(memory_space=pltpu.SMEM)
VMEM = pl.BlockSpec(memory_space=pltpu.VMEM)
HBM = pl.BlockSpec(memory_space=pltpu.HBM)
MIB = 2**20


def move_gx(x, dz=0, dy=0, dc=0):
    pairs = []
    for z in range(NZ):
        for y in range(NY):
            for c in range(NC):
                src = (z * NY + y) * NC + c
                dst = (((z + dz) % NZ) * NY + (y + dy) % NY) * NC + (c + dc) % NC
                pairs.append((src, dst))
    return lax.ppermute(x, "gx", pairs)


def move_gy(x, dl=0, dx=0):
    pairs = []
    for l in range(NL):
        for i in range(NX):
            pairs.append((l * NX + i, (l + dl) % NL * NX + (i + dx) % NX))
    return lax.ppermute(x, "gy", pairs)


def after(x, *others):
    return lax.optimization_barrier((x, *others))[0]


def in_vmem(x):
    return pltpu.with_memory_space_constraint(x, pltpu.VMEM)


def local_call(kernel, outs, *arrays, scalars=(), scratch=(), limit=8, flops=0):
    moved = sum(a.size * a.dtype.itemsize for a in arrays)
    return pl.pallas_call(
        kernel,
        in_specs=[SMEM] * len(scalars) + [VMEM] * len(arrays),
        out_specs=[VMEM] * len(outs),
        out_shape=[pltpu.VMEM(shape, dtype) for shape, dtype in outs],
        scratch_shapes=list(scratch),
        compiler_params=pltpu.CompilerParams(vmem_limit_bytes=limit * MIB),
        cost_estimate=pl.CostEstimate(flops=flops, bytes_accessed=moved, transcendentals=0),
    )(*scalars, *[in_vmem(a) for a in arrays])


def weights_kernel(steps, payload, scales, out, held, sems):
    rows = payload.shape[0] // steps
    copies = [
        pltpu.make_async_copy(
            payload.at[pl.ds(i * rows, rows)], held.at[pl.ds(i * rows, rows)], sems.at[i]
        )
        for i in range(steps)
    ]
    for copy in copies:
        copy.start()
    for i, copy in enumerate(copies):
        copy.wait()
        for row in range(i * rows // BLOCK, (i + 1) * rows // BLOCK):
            for col in range(payload.shape[1] // BLOCK):
                at = (
                    slice(row * BLOCK, (row + 1) * BLOCK),
                    slice(col * BLOCK, (col + 1) * BLOCK),
                )
                out[at] = (held[at].astype(F32) * scales[row, col]).astype(BF16)


def weights(payload, scales, steps):
    rows, cols = payload.shape
    return pl.pallas_call(
        lambda *refs: weights_kernel(steps, *refs),
        in_specs=[HBM, SMEM],
        out_specs=VMEM,
        out_shape=pltpu.VMEM((rows, cols), BF16),
        scratch_shapes=[pltpu.VMEM((rows, cols), BF16), pltpu.SemaphoreType.DMA((steps,))],
        compiler_params=pltpu.CompilerParams(vmem_limit_bytes=16 * MIB),
        cost_estimate=pl.CostEstimate(
            flops=rows * cols, bytes_accessed=4 * rows * cols, transcendentals=0
        ),
    )(pltpu.with_memory_space_constraint(payload, pltpu.HBM), scales)


def join_kernel(*refs):
    *pieces, out = refs
    at = 0
    for piece in pieces:
        rows = piece.shape[0]
        out[at : at + rows, :] = piece[...]
        at += rows


def join(*pieces):
    shape = (sum(p.shape[0] for p in pieces), pieces[0].shape[1])
    return local_call(join_kernel, [(shape, BF16)], *pieces)[0]


def order_kernel(where, out):
    row = lax.broadcasted_iota(jnp.int32, out.shape, 0)
    column = lax.broadcasted_iota(jnp.int32, out.shape, 1)
    block, inner = row // ROWS, row % ROWS
    c, y, z = block // (NY * NZ), block // NZ % NY, block % NZ
    c, y, z = (where[0] + c) % NC, (where[1] + y) % NY, (where[2] + z) % NZ
    chosen = ((c * NY + y) * NZ + z) * ROWS + inner
    out[...] = jnp.where(chosen == column, 1.0, 0.0).astype(BF16)


def turned_row(place, where):
    c, y, z = place // (NY * NZ), place // NZ % NY, place % NZ
    c, y, z = (where[0] + c) % NC, (where[1] + y) % NY, (where[2] + z) % NZ
    return pl.multiple_of(((c * NY + y) * NZ + z) * ROWS, ROWS)


def first_kernel(*refs):
    *pieces, order, gate, up, sent, kept = refs
    rows = jnp.concatenate([piece[...] for piece in pieces], axis=0)
    features = jnp.dot(order[...], rows, preferred_element_type=F32).astype(BF16)
    half = order.shape[0] // NC
    width = gate.shape[1]
    for number, weight in ((0, gate), (1, up)):
        for col in range(0, width, 2 * BLOCK):
            product = jnp.dot(
                features, weight[:, col : col + 2 * BLOCK], preferred_element_type=F32
            )
            out = slice(number * width + col, number * width + col + 2 * BLOCK)
            kept[:, out] = product[:half]
            sent[:, out] = product[half:].astype(BF16)


def first_products(order, pieces, gate, up):
    count = sum(p.shape[0] for p in pieces)
    depth, width = gate.shape
    shape = (count // NC, 2 * width)
    return local_call(
        first_kernel,
        [(shape, BF16), (shape, F32)],
        *pieces,
        order,
        gate,
        up,
        flops=4 * count * depth * width,
    )


def columns(ref):
    return [slice(i, i + 2 * BLOCK) for i in range(0, ref.shape[1], 2 * BLOCK)]


def summed(kept, received, part, cols):
    step = kept.shape[0] // 8
    rows = slice(part * step, (part + 1) * step)
    return kept[rows, cols] + received[rows, cols].astype(F32)


def leave_kernel(kept, received, far0, far1, next1, back0):
    for part, out in ((4, far0), (5, far1), (3, next1), (6, back0)):
        for cols in columns(kept):
            out[:, cols] = summed(kept, received, part, cols).astype(BF16)


def relay_kernel(kept, received, relay0, relay1, through0, through1):
    for part, relay, out in ((2, relay0, through0), (7, relay1, through1)):
        for cols in columns(kept):
            value = summed(kept, received, part, cols) + relay[:, cols].astype(F32)
            out[:, cols] = value.astype(BF16)


def over_y_kernel(kept, received, direct0, direct1, through0, through1, mine, one, two, three):
    for part, direct, through in ((0, direct0, through0), (1, direct1, through1)):
        for cols in columns(kept):
            value = summed(kept, received, part, cols)
            value = value + direct[:, cols].astype(F32) + through[:, cols].astype(F32)
            for i in (0, 1):
                out = (mine, one, two, three)[2 * part + i]
                out[:, cols] = value[i * ROWS : (i + 1) * ROWS].astype(out.dtype)


def hidden_kernel(mine, one, two, three, hidden):
    width = hidden.shape[1]
    for cols in columns(hidden):
        gate, up = (
            mine[:, at]
            + one[:, at].astype(F32)
            + two[:, at].astype(F32)
            + three[:, at].astype(F32)
            for at in (cols, slice(width + cols.start, width + cols.stop))
        )
        hidden[:, cols] = (jax.nn.silu(gate) * up).astype(BF16)


def rows_kernel(a, b, c, d, out):
    for i, pair in ((0, (a, b)), (2, (c, d))):
        for cols in columns(out):
            value = jnp.concatenate([piece[:, cols].astype(F32) for piece in pair], axis=0)
            out[i * ROWS : (i + 2) * ROWS, cols] = value.astype(BF16)


def last_kernel(where, *refs):
    *hidden, weight, kept, one, two, three, terms = refs
    count = terms.shape[0]
    rows = jnp.concatenate([piece[...] for piece in hidden], axis=0)
    product = jnp.dot(rows, weight[...], preferred_element_type=F32)
    for place in range(count // ROWS):
        terms[pl.ds(turned_row(place, where), ROWS), :] = product[
            place * ROWS : (place + 1) * ROWS
        ]
    for i, out in enumerate((kept, one, two, three)):
        rows = slice(i * count // NX, (i + 1) * count // NX)
        out[...] = terms[rows, :].astype(out.dtype)


def last_products(where, pieces, weight):
    count = sum(p.shape[0] for p in pieces)
    depth, cols = weight.shape
    shape = (count // NX, cols)
    return local_call(
        last_kernel,
        [(shape, F32)] + [(shape, BF16)] * 3,
        *pieces,
        weight,
        scalars=[where],
        scratch=[pltpu.VMEM((count, cols), F32)],
        limit=12,
        flops=2 * count * depth * cols,
    )


def over_x_kernel(total, one, two, three, kept, sent):
    half = total.shape[0] // NL
    for i, out in ((1, sent), (0, kept)):
        rows = slice(i * half, (i + 1) * half)
        value = total[rows, :] + one[rows, :].astype(F32)
        value = value + two[rows, :].astype(F32) + three[rows, :].astype(F32)
        out[...] = value.astype(out.dtype)


def local(tokens, gate_payload, gate_scales, up_payload, up_scales, down_payload, down_scales):
    index = lax.axis_index("gx")
    where = jnp.stack([index % NC, (index // NC) % NY, index // (NY * NC)]).astype(jnp.int32)

    count = tokens.shape[0] * NL * NX
    (order,) = local_call(order_kernel, [((count, count), BF16)], scalars=[where])
    gate = weights(gate_payload, gate_scales, 4)
    up = weights(up_payload, up_scales, 4)
    pair = after(join(tokens, move_gy(tokens, dl=1)), gate, order)
    two, one, three = move_gy(pair, dx=2), move_gy(pair, dx=1), move_gy(pair, dx=3)
    pieces = [pair, one, two, after(three, up)]

    sent, kept = first_products(order, pieces, gate, up)
    received = move_gx(sent, dc=1)

    rows, cols = kept.shape
    step = (rows // 8, cols)
    far0, far1, next1, back0 = local_call(leave_kernel, [(step, BF16)] * 4, kept, received)
    relay0, relay1 = move_gx(far0, dy=1), move_gx(far1, dy=-1)
    direct1, direct0 = move_gx(next1, dy=1), move_gx(back0, dy=-1)
    through0, through1 = local_call(
        relay_kernel, [(step, BF16)] * 2, kept, received, relay0, relay1
    )
    down = weights(after(down_payload, through0), down_scales, 13)
    through0, through1 = move_gx(through0, dy=1), move_gx(through1, dy=-1)
    mine, one, two, three = local_call(
        over_y_kernel,
        [((ROWS, cols), F32)] + [((ROWS, cols), BF16)] * 3,
        after(kept, down),
        received,
        direct0,
        direct1,
        through0,
        through1,
    )
    two, one, three = move_gx(two, dz=2), move_gx(one, dz=1), move_gx(three, dz=3)
    units = cols // 2
    (hidden,) = local_call(hidden_kernel, [((ROWS, units), BF16)], mine, one, two, three)

    two, one, three = move_gx(hidden, dz=-2), move_gx(hidden, dz=-1), move_gx(hidden, dz=-3)
    (hidden,) = local_call(rows_kernel, [((NZ * ROWS, units), BF16)], hidden, one, two, three)
    two, one, three = move_gx(hidden, dy=-2), move_gx(hidden, dy=-1), move_gx(hidden, dy=-3)
    mine = [hidden, one, two, three]
    theirs = [move_gx(block, dc=1) for block in mine]
    total, one, two, three = last_products(where, mine + theirs, down)

    two, one, three = move_gy(two, dx=-2), move_gy(one, dx=-1), move_gy(three, dx=-3)
    shape = (total.shape[0] // NL, total.shape[1])
    total, sent = local_call(over_x_kernel, [(shape, F32), (shape, BF16)], total, one, two, three)
    return (total + move_gy(sent, dl=1).astype(F32)).astype(BF16)


def solution(mesh):
    placed = (
        P("gy", "gx"),
        P("gx", "gy"),
        P("gx", "gy"),
        P("gx", "gy"),
        P("gx", "gy"),
        P("gy", "gx"),
        P("gy", "gx"),
    )
    return jax.shard_map(
        local, mesh=mesh, in_specs=placed, out_specs=P("gy", "gx"), check_vma=False
    )
```

time: 282 us -> 100 us (0.35)
  waiting for transfers between devices: 203 us -> 43.8 us
  starting transfers between devices: 0.09 us -> 38.4 us
  blocking collectives: 31.4 us -> 0 us
  local copies, waits for them, and re-layouts: 24.6 us -> 0.79 us
  Pallas kernels: 0 us -> 16.1 us
  between operations: 13.2 us -> 0.16 us
  matrix products: 4.26 us -> 0 us
  other arithmetic: 4.8 us -> 0.7 us
    unnamed x4 -> x0, waiting for transfers between devices: 113 us -> none
    all_gather x1 -> x0, waiting for transfers between devices: 51.5 us -> none  [local(): lax.all_gather(hidden_units, 'gx', axis=0, tiled=True)]
    ppermute x0 -> x28, waiting for transfers between devices: none -> 43.8 us  [the longest x20 33.2 us: move_gx(): return lax.ppermute(x, 'gx', pairs)]
    reduce_scatter x1 -> x0, waiting for transfers between devices: 38.8 us -> none  [local(): lax.psum_scatter(terms, 'gy', scatter_dimension=0, tiled=True)]
    ppermute x0 -> x28, starting transfers between devices: none -> 38.4 us  [the longest x20 27.4 us: move_gx(): return lax.ppermute(x, 'gx', pairs)]
    all_gather x1 -> x0, blocking collectives: 31.4 us -> none  [local(): features = lax.all_gather(tokens, 'gy', axis=0, tiled=True)]
    unnamed x20 -> x13, local copies, waits for them, and re-layouts: 20.1 us -> 0.79 us
    pallas_call x0 -> x13, Pallas kernels: none -> 16.1 us  [the longest x3 8.26 us: weights(): pl.pallas_call(lambda *refs: weights_kernel(steps, *refs), in_specs=[HBM,...]
  transfers between devices with their start and end apart: 3 -> 28, of which waited for: 3 -> 18; matrix products, arithmetic and copies ran while one was open for 0% -> 0% of each run, Pallas kernels for 0% -> 10%
where the time goes in v2:
time: 100 us; the launch traced here: 99.9 us
  waiting for transfers between devices  43.8 us (44%)
  starting transfers between devices  38.4 us (38%)
  Pallas kernels  16.1 us (16%)
    ppermute x20, waiting for transfers between devices, move_gx(): return lax.ppermute(x, 'gx', pairs)  33.2 us
    ppermute x20, starting transfers between devices, move_gx(): return lax.ppermute(x, 'gx', pairs)  27.4 us
    ppermute x8, starting transfers between devices, move_gy(): return lax.ppermute(x, 'gy', pairs)  11 us
    ppermute x8, waiting for transfers between devices, move_gy(): return lax.ppermute(x, 'gy', pairs)  10.6 us
    pallas_call x3, Pallas kernels, weights(): pl.pallas_call(lambda *refs: weights_kernel(steps, *refs), in_specs=[HBM,...  8.26 us
    pallas_call x10, Pallas kernels, local_call(): pl.pallas_call(kernel, in_specs=[SMEM] * len(scalars) + [VMEM] * len(arra...  7.84 us
  transfers between devices with their start and end apart: 28, of which 18 were waited for; matrix products, arithmetic and copies ran while one was open for 0% of the time, Pallas kernels for 10%

profile of v2, /device:TPU:8, one launch (start us, length us, event | category | flops | bytes accessed | tf_op | source)
XLA Modules:
  0.0 99.9 jit_solution(10817375868647214077)
XLA Ops:
  0.0 1.9 %collective-permute-start = (bf16[32,512]{1,0:T(8,128)(2,1)}, bf16[32,512]{1,0:T(8,128)(2,1)S(1)}, u32[]{:S(2)}, u32[]{:S(2)}) collective-permute-start(bf16[32,512]{1,0:T(8,128)(2,1)} %refs_0_.3), channel_id=1, source_target_pairs={{0,4},{1,5},{2,6},{3,7},{4,0},{5,1},{6,2},{7,3},{8,12},{9,13},{10,... | collective-permute-start | bytes 98312 | tf_op jit(solution)/shard_map/ppermute | solution.py:35
  2.0 0.8 shard_map.75.refs_4_
  2.8 0.7 copy-done.3
  3.5 2.7 %shard_map.74.refs_5_ = bf16[512,3328]{1,0:T(8,128)(2,1)S(1)} custom-call(bf16[512,3328]{1,0:T(8,128)(2,1)} %refs_0_.4, f32[4,26]{1,0:T(4,128)S(1)} %copy-done.3), custom_call_target="tpu_custom_call" | custom-call | flops 1703936 | bytes 6815744 | tf_op jit(solution)/shard_map/pallas_call | solution.py:82
  6.2 2.8 %collective-permute-start.3 = (bf16[64,512]{1,0:T(8,128)(2,1)S(1)}, bf16[64,512]{1,0:T(8,128)(2,1)S(1)}, u32[]{:S(2)}, u32[]{:S(2)}) collective-permute-start(bf16[64,512]{1,0:T(8,128)(2,1)S(1)} %shard_map.73.refs_0_), channel_id=1, source_target_pairs={{0,3},{1,0},{2,1},{3,2},{4,7},{5,4},{6,5},{7,6},{8,11},{9,8},{10,9... | collective-permute-start | bytes 196616 | tf_op jit(solution)/shard_map/ppermute | solution.py:35
  9.1 2.3 %collective-permute-start.2 = (bf16[64,512]{1,0:T(8,128)(2,1)S(1)}, bf16[64,512]{1,0:T(8,128)(2,1)S(1)}, u32[]{:S(2)}, u32[]{:S(2)}) collective-permute-start(bf16[64,512]{1,0:T(8,128)(2,1)S(1)} %shard_map.73.refs_0_), channel_id=1, source_target_pairs={{0,2},{1,3},{2,0},{3,1},{4,6},{5,7},{6,4},{7,5},{8,10},{9,11},{10,... | collective-permute-start | bytes 196616 | tf_op jit(solution)/shard_map/ppermute | solution.py:35
  11.4 2.7 %shard_map.76.refs_6_ = bf16[512,3328]{1,0:T(8,128)(2,1)S(1)} custom-call(bf16[512,3328]{1,0:T(8,128)(2,1)} %refs_0_.5, f32[4,26]{1,0:T(4,128)S(1)} %copy-done.4), custom_call_target="tpu_custom_call" | custom-call | flops 1703936 | bytes 6815744 | tf_op jit(solution)/shard_map/pallas_call | solution.py:82
  14.1 1.2 %collective-permute-done.1.refs_1_ = bf16[64,512]{1,0:T(8,128)(2,1)S(1)} collective-permute-done((bf16[64,512]{1,0:T(8,128)(2,1)S(1)}, bf16[64,512]{1,0:T(8,128)(2,1)S(1)}, u32[]{:S(2)}, u32[]{:S(2)}) %collective-permute-start.1) | collective-permute-done | bytes 65568 | tf_op jit(solution)/shard_map/ppermute | solution.py:35
  15.2 2.1 %shard_map.77 = (bf16[128,6656]{1,0:T(8,128)(2,1)S(1)}, f32[128,6656]{1,0:T(8,128)S(1)}) custom-call(bf16[64,512]{1,0:T(8,128)(2,1)S(1)} %shard_map.73.refs_0_, bf16[64,512]{1,0:T(8,128)(2,1)S(1)} %collective-permute-done.1.refs_1_, bf16[64,512]{1,0:T(8,128)(2,1)S(1)} %collective-permute-done.2.refs_2_, bf16[64,512]{1,0:T(8,128)(2,1)S(1)} %collective-permute-done.3.refs_3_, ...), custom_call_target="tpu_custom_call" | custom-call | flops 1744830464 | bytes 7208960 | tf_op jit(solution)/shard_map/pallas_call | solution.py:48
  17.4 3.6 %collective-permute-done.4.received = bf16[128,6656]{1,0:T(8,128)(2,1)S(1)} collective-permute-done((bf16[128,6656]{1,0:T(8,128)(2,1)S(1)}, bf16[128,6656]{1,0:T(8,128)(2,1)S(1)}, u32[]{:S(2)}, u32[]{:S(2)}) %collective-permute-start.4) | collective-permute-done | bytes 1703968 | tf_op jit(solution)/shard_map/ppermute | solution.py:27
  21.0 1.0 shard_map.78
  22.0 1.6 %collective-permute-start.5 = (bf16[16,6656]{1,0:T(8,128)(2,1)S(1)}, bf16[16,6656]{1,0:T(8,128)(2,1)S(1)}, u32[]{:S(2)}, u32[]{:S(2)}) collective-permute-start(bf16[16,6656]{1,0:T(8,128)(2,1)S(1)} %get-tuple-element.31), channel_id=1, source_target_pairs={{0,16},{8,24},{16,32},{24,40},{32,48},{40,56},{48,0},{56,8},{64,80... | collective-permute-start | bytes 638984 | tf_op jit(solution)/shard_map/ppermute | solution.py:27
  23.6 0.4 collective-permute-start.6
  24.0 1.7 %collective-permute-start.7 = (bf16[16,6656]{1,0:T(8,128)(2,1)}, bf16[16,6656]{1,0:T(8,128)(2,1)}, u32[]{:S(2)}, u32[]{:S(2)}) collective-permute-start(bf16[16,6656]{1,0:T(8,128)(2,1)} %get-tuple-element.36), channel_id=1, source_target_pairs={{0,48},{8,56},{16,0},{24,8},{32,16},{40,24},{48,32},{56,40},{64,11... | collective-permute-start | bytes 638984 | tf_op jit(solution)/shard_map/ppermute | solution.py:27
  25.7 0.4 collective-permute-start.8
  26.0 4.0 %collective-permute-done.5.relay0 = bf16[16,6656]{1,0:T(8,128)(2,1)S(1)} collective-permute-done((bf16[16,6656]{1,0:T(8,128)(2,1)S(1)}, bf16[16,6656]{1,0:T(8,128)(2,1)S(1)}, u32[]{:S(2)}, u32[]{:S(2)}) %collective-permute-start.5) | collective-permute-done | bytes 213024 | tf_op jit(solution)/shard_map/ppermute | solution.py:27
  30.1 1.6 %collective-permute-done.6.relay1 = bf16[16,6656]{1,0:T(8,128)(2,1)S(1)} collective-permute-done((bf16[16,6656]{1,0:T(8,128)(2,1)S(1)}, bf16[16,6656]{1,0:T(8,128)(2,1)S(1)}, u32[]{:S(2)}, u32[]{:S(2)}) %collective-permute-start.6) | collective-permute-done | bytes 213024 | tf_op jit(solution)/shard_map/ppermute | solution.py:27
  31.7 0.8 shard_map.79
  32.5 0.4 collective-permute-start.10
  33.0 1.6 %collective-permute-start.9 = (bf16[16,6656]{1,0:T(8,128)(2,1)}, bf16[16,6656]{1,0:T(8,128)(2,1)}, u32[]{:S(2)}, u32[]{:S(2)}) collective-permute-start(bf16[16,6656]{1,0:T(8,128)(2,1)} %get-tuple-element.33), channel_id=1, source_target_pairs={{0,16},{8,24},{16,32},{24,40},{32,48},{40,56},{48,0},{56,8},{64,80... | collective-permute-start | bytes 638984 | tf_op jit(solution)/shard_map/ppermute | solution.py:27
  34.7 2.9 %shard_map.80.refs_8_ = bf16[3328,512]{1,0:T(8,128)(2,1)S(1)} custom-call(bf16[3328,512]{1,0:T(8,128)(2,1)} %refs_0_.6, f32[26,4]{1,0:T(8,128)S(1)} %copy.8.refs_1_), custom_call_target="tpu_custom_call" | custom-call | flops 1703936 | bytes 6815744 | tf_op jit(solution)/shard_map/pallas_call | solution.py:82
  37.6 2.3 %collective-permute-done.10.through1 = bf16[16,6656]{1,0:T(8,128)(2,1)} collective-permute-done((bf16[16,6656]{1,0:T(8,128)(2,1)}, bf16[16,6656]{1,0:T(8,128)(2,1)}, u32[]{:S(2)}, u32[]{:S(2)}) %collective-permute-start.10) | collective-permute-done | bytes 213024 | tf_op jit(solution)/shard_map/ppermute | solution.py:27
  39.8 0.2 collective-permute-done.9.through0
  40.0 1.4 %shard_map.81 = (f32[8,6656]{1,0:T(8,128)S(1)}, bf16[8,6656]{1,0:T(8,128)(2,1)S(1)}, bf16[8,6656]{1,0:T(8,128)(2,1)S(1)}, bf16[8,6656]{1,0:T(8,128)(2,1)S(1)}) custom-call(f32[128,6656]{1,0:T(8,128)S(1)} %get-tuple-element.35.kept, bf16[128,6656]{1,0:T(8,128)(2,1)S(1)} %copy-done.1, bf16[16,6656]{1,0:T(8,128)(2,1)} %collective-permute-done.7.direct0, ...), custom_call_target="tpu_custom_call" | custom-call | bytes 5963776 | tf_op jit(solution)/shard_map/pallas_call | solution.py:48
  41.4 3.4 %collective-permute-start.11 = (bf16[8,6656]{1,0:T(8,128)(2,1)S(1)}, bf16[8,6656]{1,0:T(8,128)(2,1)S(1)}, u32[]{:S(2)}, u32[]{:S(2)}) collective-permute-start(bf16[8,6656]{1,0:T(8,128)(2,1)S(1)} %get-tuple-element.40), channel_id=1, source_target_pairs={{0,64},{8,72},{16,80},{24,88},{32,96},{40,104},{48,112},{56,120},{... | collective-permute-start | bytes 319496 | tf_op jit(solution)/shard_map/ppermute | solution.py:27
  44.8 4.5 %collective-permute-start.12 = (bf16[8,6656]{1,0:T(8,128)(2,1)S(1)}, bf16[8,6656]{1,0:T(8,128)(2,1)S(1)}, u32[]{:S(2)}, u32[]{:S(2)}) collective-permute-start(bf16[8,6656]{1,0:T(8,128)(2,1)S(1)} %get-tuple-element.41), channel_id=1, source_target_pairs={{0,128},{8,136},{16,144},{24,152},{32,160},{40,168},{48,176},{56,1... | collective-permute-start | bytes 319496 | tf_op jit(solution)/shard_map/ppermute | solution.py:27
  49.2 2.7 %collective-permute-start.13 = (bf16[8,6656]{1,0:T(8,128)(2,1)S(1)}, bf16[8,6656]{1,0:T(8,128)(2,1)S(1)}, u32[]{:S(2)}, u32[]{:S(2)}) collective-permute-start(bf16[8,6656]{1,0:T(8,128)(2,1)S(1)} %get-tuple-element.42), channel_id=1, source_target_pairs={{0,192},{8,200},{16,208},{24,216},{32,224},{40,232},{48,240},{56,2... | collective-permute-start | bytes 319496 | tf_op jit(solution)/shard_map/ppermute | solution.py:27
  51.9 3.1 %collective-permute-done.12.two = bf16[8,6656]{1,0:T(8,128)(2,1)S(1)} collective-permute-done((bf16[8,6656]{1,0:T(8,128)(2,1)S(1)}, bf16[8,6656]{1,0:T(8,128)(2,1)S(1)}, u32[]{:S(2)}, u32[]{:S(2)}) %collective-permute-start.12) | collective-permute-done | bytes 106528 | tf_op jit(solution)/shard_map/ppermute | solution.py:27
  55.0 3.2 %collective-permute-done.13.three = bf16[8,6656]{1,0:T(8,128)(2,1)S(1)} collective-permute-done((bf16[8,6656]{1,0:T(8,128)(2,1)S(1)}, bf16[8,6656]{1,0:T(8,128)(2,1)S(1)}, u32[]{:S(2)}, u32[]{:S(2)}) %collective-permute-start.13) | collective-permute-done | bytes 106528 | tf_op jit(solution)/shard_map/ppermute | solution.py:27
  58.3 3.6 %collective-permute-start.14 = (bf16[8,3328]{1,0:T(8,128)(2,1)S(1)}, bf16[8,3328]{1,0:T(8,128)(2,1)S(1)}, u32[]{:S(2)}, u32[]{:S(2)}) collective-permute-start(bf16[8,3328]{1,0:T(8,128)(2,1)S(1)} %shard_map.82.a), channel_id=1, source_target_pairs={{0,192},{8,200},{16,208},{24,216},{32,224},{40,232},{48,240},{56,2... | collective-permute-start | bytes 159752 | tf_op jit(solution)/shard_map/ppermute | solution.py:27
  61.9 2.2 %collective-permute-start.15 = (bf16[8,3328]{1,0:T(8,128)(2,1)S(1)}, bf16[8,3328]{1,0:T(8,128)(2,1)S(1)}, u32[]{:S(2)}, u32[]{:S(2)}) collective-permute-start(bf16[8,3328]{1,0:T(8,128)(2,1)S(1)} %shard_map.82.a), channel_id=1, source_target_pairs={{0,128},{8,136},{16,144},{24,152},{32,160},{40,168},{48,176},{56,1... | collective-permute-start | bytes 159752 | tf_op jit(solution)/shard_map/ppermute | solution.py:27
  64.1 1.5 %collective-permute-start.16 = (bf16[8,3328]{1,0:T(8,128)(2,1)S(1)}, bf16[8,3328]{1,0:T(8,128)(2,1)S(1)}, u32[]{:S(2)}, u32[]{:S(2)}) collective-permute-start(bf16[8,3328]{1,0:T(8,128)(2,1)S(1)} %shard_map.82.a), channel_id=1, source_target_pairs={{0,64},{8,72},{16,80},{24,88},{32,96},{40,104},{48,112},{56,120},{... | collective-permute-start | bytes 159752 | tf_op jit(solution)/shard_map/ppermute | solution.py:27
  65.6 5.4 %collective-permute-done.15.c = bf16[8,3328]{1,0:T(8,128)(2,1)S(1)} collective-permute-done((bf16[8,3328]{1,0:T(8,128)(2,1)S(1)}, bf16[8,3328]{1,0:T(8,128)(2,1)S(1)}, u32[]{:S(2)}, u32[]{:S(2)}) %collective-permute-start.15) | collective-permute-done | bytes 53280 | tf_op jit(solution)/shard_map/ppermute | solution.py:27
  71.0 0.3 collective-permute-start.17
  71.3 3.0 %collective-permute-start.18 = (bf16[32,3328]{1,0:T(8,128)(2,1)S(1)}, bf16[32,3328]{1,0:T(8,128)(2,1)S(1)}, u32[]{:S(2)}, u32[]{:S(2)}) collective-permute-start(bf16[32,3328]{1,0:T(8,128)(2,1)S(1)} %shard_map.83.refs_0_), channel_id=1, source_target_pairs={{0,32},{8,40},{16,48},{24,56},{32,0},{40,8},{48,16},{56,24},{64,96... | collective-permute-start | bytes 638984 | tf_op jit(solution)/shard_map/ppermute | solution.py:27
  74.4 4.8 %collective-permute-done.17.refs_1_ = bf16[32,3328]{1,0:T(8,128)(2,1)S(1)} collective-permute-done((bf16[32,3328]{1,0:T(8,128)(2,1)S(1)}, bf16[32,3328]{1,0:T(8,128)(2,1)S(1)}, u32[]{:S(2)}, u32[]{:S(2)}) %collective-permute-start.17) | collective-permute-done | bytes 213024 | tf_op jit(solution)/shard_map/ppermute | solution.py:27
  79.2 2.6 %collective-permute-done.18.refs_2_ = bf16[32,3328]{1,0:T(8,128)(2,1)S(1)} collective-permute-done((bf16[32,3328]{1,0:T(8,128)(2,1)S(1)}, bf16[32,3328]{1,0:T(8,128)(2,1)S(1)}, u32[]{:S(2)}, u32[]{:S(2)}) %collective-permute-start.18) | collective-permute-done | bytes 213024 | tf_op jit(solution)/shard_map/ppermute | solution.py:27
  81.8 1.0 collective-permute-done.19.refs_3_
  82.8 0.5 collective-permute-done.22.refs_6_
  83.2 1.0 collective-permute-done.23.refs_7_
  84.2 1.6 %shard_map.84 = (f32[64,512]{1,0:T(8,128)S(1)}, bf16[64,512]{1,0:T(8,128)(2,1)S(1)}, bf16[64,512]{1,0:T(8,128)(2,1)S(1)}, bf16[64,512]{1,0:T(8,128)(2,1)S(1)}) custom-call(s32[3]{0:T(128)S(1)} %pad_add_fusion.where, bf16[32,3328]{1,0:T(8,128)(2,1)S(1)} %shard_map.83.refs_0_, bf16[32,3328]{1,0:T(8,128)(2,1)S(1)} %collective-permute-done.17.refs_1_, ...), custom_call_target="tpu_custom_call" | custom-call | flops 872415232 | bytes 5111808 | tf_op jit(solution)/shard_map/pallas_call | solution.py:48
  85.8 2.9 %collective-permute-start.24 = (bf16[64,512]{1,0:T(8,128)(2,1)S(1)}, bf16[64,512]{1,0:T(8,128)(2,1)S(1)}, u32[]{:S(2)}, u32[]{:S(2)}) collective-permute-start(bf16[64,512]{1,0:T(8,128)(2,1)S(1)} %get-tuple-element.44), channel_id=1, source_target_pairs={{0,3},{1,0},{2,1},{3,2},{4,7},{5,4},{6,5},{7,6},{8,11},{9,8},{10,9... | collective-permute-start | bytes 196616 | tf_op jit(solution)/shard_map/ppermute | solution.py:35
  88.7 1.0 collective-permute-start.26
  89.7 2.1 %collective-permute-done.24.one = bf16[64,512]{1,0:T(8,128)(2,1)S(1)} collective-permute-done((bf16[64,512]{1,0:T(8,128)(2,1)S(1)}, bf16[64,512]{1,0:T(8,128)(2,1)S(1)}, u32[]{:S(2)}, u32[]{:S(2)}) %collective-permute-start.24) | collective-permute-done | bytes 65568 | tf_op jit(solution)/shard_map/ppermute | solution.py:35
  91.8 3.0 %collective-permute-done.25.two = bf16[64,512]{1,0:T(8,128)(2,1)S(1)} collective-permute-done((bf16[64,512]{1,0:T(8,128)(2,1)S(1)}, bf16[64,512]{1,0:T(8,128)(2,1)S(1)}, u32[]{:S(2)}, u32[]{:S(2)}) %collective-permute-start.25) | collective-permute-done | bytes 65568 | tf_op jit(solution)/shard_map/ppermute | solution.py:35
  94.8 0.4 collective-permute-done.26.three
  95.3 3.9 %collective-permute-done.27 = bf16[32,512]{1,0:T(8,128)(2,1)S(1)} collective-permute-done((bf16[32,512]{1,0:T(8,128)(2,1)S(1)}, bf16[32,512]{1,0:T(8,128)(2,1)S(1)}, u32[]{:S(2)}, u32[]{:S(2)}) %collective-permute-start.27) | collective-permute-done | bytes 32800 | tf_op jit(solution)/shard_map/ppermute | solution.py:35
  99.2 0.6 add_convert_fusion
  (36 shorter events, 0.7 us)
Async XLA Ops:
  0.0 6.2 %collective-permute-start = (bf16[32,512]{1,0:T(8,128)(2,1)}, bf16[32,512]{1,0:T(8,128)(2,1)S(1)}, u32[]{:S(2)}, u32[]{:S(2)}) collective-permute-start(bf16[32,512]{1,0:T(8,128)(2,1)} %refs_0_.3), channel_id=1, source_target_pairs={{0,4},{1,5},{2,6},{3,7},{4,0},{5,1},{6,2},{7,3},{8,12},{9,13},{10,... | collective-permute-start | bytes 98312 | tf_op jit(solution)/shard_map/ppermute | solution.py:35
  2.8 0.7 copy-start.3
  3.5 2.7 %copy-start.2 = (bf16[32,512]{1,0:T(8,128)(2,1)S(1)}, bf16[32,512]{1,0:T(8,128)(2,1)}, u32[]{:S(2)}) copy-start(bf16[32,512]{1,0:T(8,128)(2,1)} %refs_0_.3) | copy-start | bytes 98308
  3.5 7.9 %copy-start.4 = (f32[4,26]{1,0:T(4,128)S(1)}, f32[4,26]{1,0:T(4,128)}, u32[]{:S(2)}) copy-start(f32[4,26]{1,0:T(4,128)} %refs_1_.4) | copy-start | bytes 1252
  6.2 7.8 %collective-permute-start.3 = (bf16[64,512]{1,0:T(8,128)(2,1)S(1)}, bf16[64,512]{1,0:T(8,128)(2,1)S(1)}, u32[]{:S(2)}, u32[]{:S(2)}) collective-permute-start(bf16[64,512]{1,0:T(8,128)(2,1)S(1)} %shard_map.73.refs_0_), channel_id=1, source_target_pairs={{0,3},{1,0},{2,1},{3,2},{4,7},{5,4},{6,5},{7,6},{8,11},{9,8},{10,9... | collective-permute-start | bytes 196616 | tf_op jit(solution)/shard_map/ppermute | solution.py:35
  9.1 6.2 %collective-permute-start.1 = (bf16[64,512]{1,0:T(8,128)(2,1)S(1)}, bf16[64,512]{1,0:T(8,128)(2,1)S(1)}, u32[]{:S(2)}, u32[]{:S(2)}) collective-permute-start(bf16[64,512]{1,0:T(8,128)(2,1)S(1)} %shard_map.73.refs_0_), channel_id=1, source_target_pairs={{0,1},{1,2},{2,3},{3,0},{4,5},{5,6},{6,7},{7,4},{8,9},{9,10},{10,1... | collective-permute-start | bytes 196616 | tf_op jit(solution)/shard_map/ppermute | solution.py:35
  9.1 6.2 %collective-permute-start.2 = (bf16[64,512]{1,0:T(8,128)(2,1)S(1)}, bf16[64,512]{1,0:T(8,128)(2,1)S(1)}, u32[]{:S(2)}, u32[]{:S(2)}) collective-permute-start(bf16[64,512]{1,0:T(8,128)(2,1)S(1)} %shard_map.73.refs_0_), channel_id=1, source_target_pairs={{0,2},{1,3},{2,0},{3,1},{4,6},{5,7},{6,4},{7,5},{8,10},{9,11},{10,... | collective-permute-start | bytes 196616 | tf_op jit(solution)/shard_map/ppermute | solution.py:35
  17.3 3.7 %collective-permute-start.4 = (bf16[128,6656]{1,0:T(8,128)(2,1)S(1)}, bf16[128,6656]{1,0:T(8,128)(2,1)S(1)}, u32[]{:S(2)}, u32[]{:S(2)}) collective-permute-start(bf16[128,6656]{1,0:T(8,128)(2,1)S(1)} %get-tuple-element.30), channel_id=1, source_target_pairs={{0,8},{8,0},{16,24},{24,16},{32,40},{40,32},{48,56},{56,48},{64,72... | collective-permute-start | bytes 5111816 | tf_op jit(solution)/shard_map/ppermute | solution.py:27
  21.0 11.5 %copy-start = (bf16[128,6656]{1,0:T(8,128)(2,1)}, bf16[128,6656]{1,0:T(8,128)(2,1)S(1)}, u32[]{:S(2)}) copy-start(bf16[128,6656]{1,0:T(8,128)(2,1)S(1)} %collective-permute-done.4.received) | copy-start | bytes 5111812
  22.0 12.6 %copy-start.5 = (f32[26,4]{0,1:T(4,128)S(1)}, f32[26,4]{0,1:T(4,128)}, u32[]{:S(2)}) copy-start(f32[26,4]{0,1:T(4,128)} %param.13) | copy-start | bytes 1252
  22.0 8.1 %collective-permute-start.5 = (bf16[16,6656]{1,0:T(8,128)(2,1)S(1)}, bf16[16,6656]{1,0:T(8,128)(2,1)S(1)}, u32[]{:S(2)}, u32[]{:S(2)}) collective-permute-start(bf16[16,6656]{1,0:T(8,128)(2,1)S(1)} %get-tuple-element.31), channel_id=1, source_target_pairs={{0,16},{8,24},{16,32},{24,40},{32,48},{40,56},{48,0},{56,8},{64,80... | collective-permute-start | bytes 638984 | tf_op jit(solution)/shard_map/ppermute | solution.py:27
  23.6 8.1 %collective-permute-start.6 = (bf16[16,6656]{1,0:T(8,128)(2,1)S(1)}, bf16[16,6656]{1,0:T(8,128)(2,1)S(1)}, u32[]{:S(2)}, u32[]{:S(2)}) collective-permute-start(bf16[16,6656]{1,0:T(8,128)(2,1)S(1)} %get-tuple-element.32), channel_id=1, source_target_pairs={{0,48},{8,56},{16,0},{24,8},{32,16},{40,24},{48,32},{56,40},{64,11... | collective-permute-start | bytes 638984 | tf_op jit(solution)/shard_map/ppermute | solution.py:27
  24.0 13.5 %collective-permute-start.7 = (bf16[16,6656]{1,0:T(8,128)(2,1)}, bf16[16,6656]{1,0:T(8,128)(2,1)}, u32[]{:S(2)}, u32[]{:S(2)}) collective-permute-start(bf16[16,6656]{1,0:T(8,128)(2,1)} %get-tuple-element.36), channel_id=1, source_target_pairs={{0,48},{8,56},{16,0},{24,8},{32,16},{40,24},{48,32},{56,40},{64,11... | collective-permute-start | bytes 638984 | tf_op jit(solution)/shard_map/ppermute | solution.py:27
  25.7 11.9 %collective-permute-start.8 = (bf16[16,6656]{1,0:T(8,128)(2,1)}, bf16[16,6656]{1,0:T(8,128)(2,1)}, u32[]{:S(2)}, u32[]{:S(2)}) collective-permute-start(bf16[16,6656]{1,0:T(8,128)(2,1)} %get-tuple-element.37), channel_id=1, source_target_pairs={{0,16},{8,24},{16,32},{24,40},{32,48},{40,56},{48,0},{56,8},{64,80... | collective-permute-start | bytes 638984 | tf_op jit(solution)/shard_map/ppermute | solution.py:27
  32.5 7.3 %collective-permute-start.10 = (bf16[16,6656]{1,0:T(8,128)(2,1)}, bf16[16,6656]{1,0:T(8,128)(2,1)}, u32[]{:S(2)}, u32[]{:S(2)}) collective-permute-start(bf16[16,6656]{1,0:T(8,128)(2,1)} %get-tuple-element.38), channel_id=1, source_target_pairs={{0,48},{8,56},{16,0},{24,8},{32,16},{40,24},{48,32},{56,40},{64,11... | collective-permute-start | bytes 638984 | tf_op jit(solution)/shard_map/ppermute | solution.py:27
  33.0 7.0 %collective-permute-start.9 = (bf16[16,6656]{1,0:T(8,128)(2,1)}, bf16[16,6656]{1,0:T(8,128)(2,1)}, u32[]{:S(2)}, u32[]{:S(2)}) collective-permute-start(bf16[16,6656]{1,0:T(8,128)(2,1)} %get-tuple-element.33), channel_id=1, source_target_pairs={{0,16},{8,24},{16,32},{24,40},{32,48},{40,56},{48,0},{56,8},{64,80... | collective-permute-start | bytes 638984 | tf_op jit(solution)/shard_map/ppermute | solution.py:27
  34.7 5.3 %copy-start.1 = (bf16[128,6656]{1,0:T(8,128)(2,1)S(1)}, bf16[128,6656]{1,0:T(8,128)(2,1)}, u32[]{:S(2)}) copy-start(bf16[128,6656]{1,0:T(8,128)(2,1)} %copy-done) | copy-start | bytes 5111812
  41.4 10.5 %collective-permute-start.11 = (bf16[8,6656]{1,0:T(8,128)(2,1)S(1)}, bf16[8,6656]{1,0:T(8,128)(2,1)S(1)}, u32[]{:S(2)}, u32[]{:S(2)}) collective-permute-start(bf16[8,6656]{1,0:T(8,128)(2,1)S(1)} %get-tuple-element.40), channel_id=1, source_target_pairs={{0,64},{8,72},{16,80},{24,88},{32,96},{40,104},{48,112},{56,120},{... | collective-permute-start | bytes 319496 | tf_op jit(solution)/shard_map/ppermute | solution.py:27
  44.8 10.3 %collective-permute-start.12 = (bf16[8,6656]{1,0:T(8,128)(2,1)S(1)}, bf16[8,6656]{1,0:T(8,128)(2,1)S(1)}, u32[]{:S(2)}, u32[]{:S(2)}) collective-permute-start(bf16[8,6656]{1,0:T(8,128)(2,1)S(1)} %get-tuple-element.41), channel_id=1, source_target_pairs={{0,128},{8,136},{16,144},{24,152},{32,160},{40,168},{48,176},{56,1... | collective-permute-start | bytes 319496 | tf_op jit(solution)/shard_map/ppermute | solution.py:27
  49.2 9.0 %collective-permute-start.13 = (bf16[8,6656]{1,0:T(8,128)(2,1)S(1)}, bf16[8,6656]{1,0:T(8,128)(2,1)S(1)}, u32[]{:S(2)}, u32[]{:S(2)}) collective-permute-start(bf16[8,6656]{1,0:T(8,128)(2,1)S(1)} %get-tuple-element.42), channel_id=1, source_target_pairs={{0,192},{8,200},{16,208},{24,216},{32,224},{40,232},{48,240},{56,2... | collective-permute-start | bytes 319496 | tf_op jit(solution)/shard_map/ppermute | solution.py:27
  58.3 7.3 %collective-permute-start.14 = (bf16[8,3328]{1,0:T(8,128)(2,1)S(1)}, bf16[8,3328]{1,0:T(8,128)(2,1)S(1)}, u32[]{:S(2)}, u32[]{:S(2)}) collective-permute-start(bf16[8,3328]{1,0:T(8,128)(2,1)S(1)} %shard_map.82.a), channel_id=1, source_target_pairs={{0,192},{8,200},{16,208},{24,216},{32,224},{40,232},{48,240},{56,2... | collective-permute-start | bytes 159752 | tf_op jit(solution)/shard_map/ppermute | solution.py:27
  61.9 9.1 %collective-permute-start.15 = (bf16[8,3328]{1,0:T(8,128)(2,1)S(1)}, bf16[8,3328]{1,0:T(8,128)(2,1)S(1)}, u32[]{:S(2)}, u32[]{:S(2)}) collective-permute-start(bf16[8,3328]{1,0:T(8,128)(2,1)S(1)} %shard_map.82.a), channel_id=1, source_target_pairs={{0,128},{8,136},{16,144},{24,152},{32,160},{40,168},{48,176},{56,1... | collective-permute-start | bytes 159752 | tf_op jit(solution)/shard_map/ppermute | solution.py:27
  64.1 6.9 %collective-permute-start.16 = (bf16[8,3328]{1,0:T(8,128)(2,1)S(1)}, bf16[8,3328]{1,0:T(8,128)(2,1)S(1)}, u32[]{:S(2)}, u32[]{:S(2)}) collective-permute-start(bf16[8,3328]{1,0:T(8,128)(2,1)S(1)} %shard_map.82.a), channel_id=1, source_target_pairs={{0,64},{8,72},{16,80},{24,88},{32,96},{40,104},{48,112},{56,120},{... | collective-permute-start | bytes 159752 | tf_op jit(solution)/shard_map/ppermute | solution.py:27
  71.0 8.2 %collective-permute-start.17 = (bf16[32,3328]{1,0:T(8,128)(2,1)S(1)}, bf16[32,3328]{1,0:T(8,128)(2,1)S(1)}, u32[]{:S(2)}, u32[]{:S(2)}) collective-permute-start(bf16[32,3328]{1,0:T(8,128)(2,1)S(1)} %shard_map.83.refs_0_), channel_id=1, source_target_pairs={{0,48},{8,56},{16,0},{24,8},{32,16},{40,24},{48,32},{56,40},{64,11... | collective-permute-start | bytes 638984 | tf_op jit(solution)/shard_map/ppermute | solution.py:27
  71.3 10.5 %collective-permute-start.18 = (bf16[32,3328]{1,0:T(8,128)(2,1)S(1)}, bf16[32,3328]{1,0:T(8,128)(2,1)S(1)}, u32[]{:S(2)}, u32[]{:S(2)}) collective-permute-start(bf16[32,3328]{1,0:T(8,128)(2,1)S(1)} %shard_map.83.refs_0_), channel_id=1, source_target_pairs={{0,32},{8,40},{16,48},{24,56},{32,0},{40,8},{48,16},{56,24},{64,96... | collective-permute-start | bytes 638984 | tf_op jit(solution)/shard_map/ppermute | solution.py:27
  74.2 8.5 %collective-permute-start.19 = (bf16[32,3328]{1,0:T(8,128)(2,1)S(1)}, bf16[32,3328]{1,0:T(8,128)(2,1)S(1)}, u32[]{:S(2)}, u32[]{:S(2)}) collective-permute-start(bf16[32,3328]{1,0:T(8,128)(2,1)S(1)} %shard_map.83.refs_0_), channel_id=1, source_target_pairs={{0,16},{8,24},{16,32},{24,40},{32,48},{40,56},{48,0},{56,8},{64,80... | collective-permute-start | bytes 638984 | tf_op jit(solution)/shard_map/ppermute | solution.py:27
  74.4 8.4 %collective-permute-start.20 = (bf16[32,3328]{1,0:T(8,128)(2,1)S(1)}, bf16[32,3328]{1,0:T(8,128)(2,1)S(1)}, u32[]{:S(2)}, u32[]{:S(2)}) collective-permute-start(bf16[32,3328]{1,0:T(8,128)(2,1)S(1)} %shard_map.83.refs_0_), channel_id=1, source_target_pairs={{0,8},{8,0},{16,24},{24,16},{32,40},{40,32},{48,56},{56,48},{64,72... | collective-permute-start | bytes 638984 | tf_op jit(solution)/shard_map/ppermute | solution.py:27
  79.2 3.6 %collective-permute-start.21 = (bf16[32,3328]{1,0:T(8,128)(2,1)S(1)}, bf16[32,3328]{1,0:T(8,128)(2,1)S(1)}, u32[]{:S(2)}, u32[]{:S(2)}) collective-permute-start(bf16[32,3328]{1,0:T(8,128)(2,1)S(1)} %collective-permute-done.17.refs_1_), channel_id=1, source_target_pairs={{0,8},{8,0},{16,24},{24,16},{32,40},{40,32},{48,56},{56,48},{64,72... | collective-permute-start | bytes 638984 | tf_op jit(solution)/shard_map/ppermute | solution.py:27
  81.8 1.5 %collective-permute-start.22 = (bf16[32,3328]{1,0:T(8,128)(2,1)S(1)}, bf16[32,3328]{1,0:T(8,128)(2,1)S(1)}, u32[]{:S(2)}, u32[]{:S(2)}) collective-permute-start(bf16[32,3328]{1,0:T(8,128)(2,1)S(1)} %collective-permute-done.18.refs_2_), channel_id=1, source_target_pairs={{0,8},{8,0},{16,24},{24,16},{32,40},{40,32},{48,56},{56,48},{64,72... | collective-permute-start | bytes 638984 | tf_op jit(solution)/shard_map/ppermute | solution.py:27
  82.7 1.5 %collective-permute-start.23 = (bf16[32,3328]{1,0:T(8,128)(2,1)S(1)}, bf16[32,3328]{1,0:T(8,128)(2,1)S(1)}, u32[]{:S(2)}, u32[]{:S(2)}) collective-permute-start(bf16[32,3328]{1,0:T(8,128)(2,1)S(1)} %collective-permute-done.19.refs_3_), channel_id=1, source_target_pairs={{0,8},{8,0},{16,24},{24,16},{32,40},{40,32},{48,56},{56,48},{64,72... | collective-permute-start | bytes 638984 | tf_op jit(solution)/shard_map/ppermute | solution.py:27
  85.8 6.0 %collective-permute-start.24 = (bf16[64,512]{1,0:T(8,128)(2,1)S(1)}, bf16[64,512]{1,0:T(8,128)(2,1)S(1)}, u32[]{:S(2)}, u32[]{:S(2)}) collective-permute-start(bf16[64,512]{1,0:T(8,128)(2,1)S(1)} %get-tuple-element.44), channel_id=1, source_target_pairs={{0,3},{1,0},{2,1},{3,2},{4,7},{5,4},{6,5},{7,6},{8,11},{9,8},{10,9... | collective-permute-start | bytes 196616 | tf_op jit(solution)/shard_map/ppermute | solution.py:35
  88.7 6.1 %collective-permute-start.25 = (bf16[64,512]{1,0:T(8,128)(2,1)S(1)}, bf16[64,512]{1,0:T(8,128)(2,1)S(1)}, u32[]{:S(2)}, u32[]{:S(2)}) collective-permute-start(bf16[64,512]{1,0:T(8,128)(2,1)S(1)} %get-tuple-element.45), channel_id=1, source_target_pairs={{0,2},{1,3},{2,0},{3,1},{4,6},{5,7},{6,4},{7,5},{8,10},{9,11},{10,... | collective-permute-start | bytes 196616 | tf_op jit(solution)/shard_map/ppermute | solution.py:35
  88.7 6.5 %collective-permute-start.26 = (bf16[64,512]{1,0:T(8,128)(2,1)S(1)}, bf16[64,512]{1,0:T(8,128)(2,1)S(1)}, u32[]{:S(2)}, u32[]{:S(2)}) collective-permute-start(bf16[64,512]{1,0:T(8,128)(2,1)S(1)} %get-tuple-element.46), channel_id=1, source_target_pairs={{0,1},{1,2},{2,3},{3,0},{4,5},{5,6},{6,7},{7,4},{8,9},{9,10},{10,1... | collective-permute-start | bytes 196616 | tf_op jit(solution)/shard_map/ppermute | solution.py:35
  95.2 4.0 %collective-permute-start.27 = (bf16[32,512]{1,0:T(8,128)(2,1)S(1)}, bf16[32,512]{1,0:T(8,128)(2,1)S(1)}, u32[]{:S(2)}, u32[]{:S(2)}) collective-permute-start(bf16[32,512]{1,0:T(8,128)(2,1)S(1)} %get-tuple-element.48), channel_id=1, source_target_pairs={{0,4},{1,5},{2,6},{3,7},{4,0},{5,1},{6,2},{7,3},{8,12},{9,13},{10,... | collective-permute-start | bytes 98312 | tf_op jit(solution)/shard_map/ppermute | solution.py:35

commit v3 on v2

v3 whole, which is shorter than its diff:
```python
import jax
import jax.numpy as jnp
from jax import lax
from jax.experimental import pallas as pl
from jax.experimental.pallas import tpu as pltpu
from jax.sharding import PartitionSpec as P

BLOCK = 128
F32 = jnp.float32
BF16 = jnp.bfloat16
NZ, NY, NC, NL, NX = 4, 4, 2, 2, 4
ROWS = 8
SMEM = pl.BlockSpec(memory_space=pltpu.SMEM)
VMEM = pl.BlockSpec(memory_space=pltpu.VMEM)
HBM = pl.BlockSpec(memory_space=pltpu.HBM)
MIB = 2**20


def move_gx(x, dz=0, dy=0, dc=0):
    pairs = []
    for z in range(NZ):
        for y in range(NY):
            for c in range(NC):
                src = (z * NY + y) * NC + c
                dst = (((z + dz) % NZ) * NY + (y + dy) % NY) * NC + (c + dc) % NC
                pairs.append((src, dst))
    return lax.ppermute(x, "gx", pairs)


def move_gy(x, dl=0, dx=0):
    pairs = []
    for l in range(NL):
        for i in range(NX):
            pairs.append((l * NX + i, (l + dl) % NL * NX + (i + dx) % NX))
    return lax.ppermute(x, "gy", pairs)


def after(x, *others):
    return lax.optimization_barrier((x, *others))[0]


def in_vmem(x):
    return pltpu.with_memory_space_constraint(x, pltpu.VMEM)


def local_call(kernel, outs, *arrays, scalars=(), scratch=(), limit=2, flops=0):
    moved = sum(a.size * a.dtype.itemsize for a in arrays)
    return pl.pallas_call(
        kernel,
        in_specs=[SMEM] * len(scalars) + [VMEM] * len(arrays),
        out_specs=[VMEM] * len(outs),
        out_shape=[pltpu.VMEM(shape, dtype) for shape, dtype in outs],
        scratch_shapes=list(scratch),
        compiler_params=pltpu.CompilerParams(vmem_limit_bytes=limit * MIB),
        cost_estimate=pl.CostEstimate(flops=flops, bytes_accessed=moved, transcendentals=0),
    )(*scalars, *[in_vmem(a) for a in arrays])


def weights_kernel(steps, flipped, payload, scales, out, held, factors, sems, sem):
    rows = payload.shape[0] // steps
    copies = [
        pltpu.make_async_copy(
            payload.at[pl.ds(i * rows, rows)], held.at[pl.ds(i * rows, rows)], sems.at[i]
        )
        for i in range(steps)
    ]
    small = pltpu.make_async_copy(scales, factors, sem)
    small.start()
    for copy in copies:
        copy.start()
    small.wait()
    for i, copy in enumerate(copies):
        copy.wait()
        for row in range(i * rows // BLOCK, (i + 1) * rows // BLOCK):
            for col in range(payload.shape[1] // BLOCK):
                at = (
                    slice(row * BLOCK, (row + 1) * BLOCK),
                    slice(col * BLOCK, (col + 1) * BLOCK),
                )
                factor = factors[col, row] if flipped else factors[row, col]
                out[at] = (held[at].astype(F32) * factor).astype(BF16)


def in_hbm(x):
    return pltpu.with_memory_space_constraint(x, pltpu.HBM)


def weights(payload, scales, steps, flipped=False):
    rows, cols = payload.shape
    return pl.pallas_call(
        lambda *refs: weights_kernel(steps, flipped, *refs),
        in_specs=[HBM, HBM],
        out_specs=VMEM,
        out_shape=pltpu.VMEM((rows, cols), BF16),
        scratch_shapes=[
            pltpu.VMEM((rows, cols), BF16),
            pltpu.SMEM(scales.shape, F32),
            pltpu.SemaphoreType.DMA((steps,)),
            pltpu.SemaphoreType.DMA,
        ],
        compiler_params=pltpu.CompilerParams(vmem_limit_bytes=5 * MIB),
        cost_estimate=pl.CostEstimate(
            flops=rows * cols, bytes_accessed=4 * rows * cols, transcendentals=0
        ),
    )(in_hbm(payload), in_hbm(scales))


def join_kernel(*refs):
    *pieces, out = refs
    at = 0
    for piece in pieces:
        rows = piece.shape[0]
        out[at : at + rows, :] = piece[...]
        at += rows


def join(*pieces):
    shape = (sum(p.shape[0] for p in pieces), pieces[0].shape[1])
    return local_call(join_kernel, [(shape, BF16)], *pieces)[0]


def order_kernel(where, out):
    row = lax.broadcasted_iota(jnp.int32, out.shape, 0)
    column = lax.broadcasted_iota(jnp.int32, out.shape, 1)
    block, inner = row // ROWS, row % ROWS
    c, y, z = block // (NY * NZ), block // NZ % NY, block % NZ
    c, y, z = (where[0] + c) % NC, (where[1] + y) % NY, (where[2] + z) % NZ
    chosen = ((c * NY + y) * NZ + z) * ROWS + inner
    out[...] = jnp.where(chosen == column, 1.0, 0.0).astype(BF16)


def turned_row(place, where):
    c, y, z = place // (NY * NZ), place // NZ % NY, place % NZ
    c, y, z = (where[0] + c) % NC, (where[1] + y) % NY, (where[2] + z) % NZ
    return pl.multiple_of(((c * NY + y) * NZ + z) * ROWS, ROWS)


def products(features, gate, up):
    width = gate.shape[1]
    for number, weight in ((0, gate), (1, up)):
        for col in range(0, width, 2 * BLOCK):
            out = slice(number * width + col, number * width + col + 2 * BLOCK)
            yield out, jnp.dot(
                features, weight[:, col : col + 2 * BLOCK], preferred_element_type=F32
            )


def sent_kernel(*refs):
    *pieces, order, gate, up, mine, sent = refs
    rows = jnp.concatenate([piece[...] for piece in pieces], axis=0)
    features = jnp.dot(order[...], rows, preferred_element_type=F32).astype(BF16)
    half = order.shape[0] // NC
    mine[...] = features[:half]
    for out, product in products(features[half:], gate, up):
        sent[:, out] = product.astype(BF16)


def kept_kernel(features, gate, up, kept):
    for out, product in products(features[...], gate, up):
        kept[:, out] = product


def columns(width, step):
    return [slice(i, i + step) for i in range(0, width, step)]


def over_columns(width, step, body):
    @pl.loop(0, width // step)
    def _(i):
        body(pl.multiple_of(i * step, step))


def summed(kept, received, part, cols):
    step = kept.shape[0] // 8
    rows = slice(part * step, (part + 1) * step)
    return kept[rows, cols] + received[rows, cols].astype(F32)


def leave_kernel(kept, received, far0, far1, next1, back0):
    def body(at):
        cols = pl.ds(at, 13 * BLOCK)
        for part, out in ((4, far0), (5, far1), (3, next1), (6, back0)):
            out[:, cols] = summed(kept, received, part, cols).astype(BF16)

    over_columns(kept.shape[1], 13 * BLOCK, body)


def relay_kernel(kept, received, relay0, relay1, through0, through1):
    def body(at):
        cols = pl.ds(at, 13 * BLOCK)
        for part, relay, out in ((2, relay0, through0), (7, relay1, through1)):
            value = summed(kept, received, part, cols) + relay[:, cols].astype(F32)
            out[:, cols] = value.astype(BF16)

    over_columns(kept.shape[1], 13 * BLOCK, body)


def over_y_kernel(part, kept, received, direct, through, first, second):
    width = kept.shape[1] // 2

    def body(at):
        values = []
        for place in (0, width):
            cols = pl.ds(pl.multiple_of(place + at, BLOCK), 13 * BLOCK)
            value = summed(kept, received, part, cols)
            values.append(value + direct[:, cols].astype(F32) + through[:, cols].astype(F32))
        for i, out in enumerate((first, second)):
            both = jnp.concatenate([v[i * ROWS : (i + 1) * ROWS] for v in values], axis=0)
            out[:, pl.ds(at, 13 * BLOCK)] = both.astype(out.dtype)

    over_columns(width, 13 * BLOCK, body)


def hidden_kernel(mine, one, two, three, hidden):
    for cols in columns(hidden.shape[1], 2 * BLOCK):
        total = mine[:, cols] + one[:, cols].astype(F32)
        total = total + two[:, cols].astype(F32) + three[:, cols].astype(F32)
        hidden[:, cols] = (jax.nn.silu(total[:ROWS]) * total[ROWS:]).astype(BF16)


def rows_kernel(a, b, c, d, out):
    for i, pair in ((0, (a, b)), (2, (c, d))):
        for cols in columns(out.shape[1], 2 * BLOCK):
            value = jnp.concatenate([piece[:, cols].astype(F32) for piece in pair], axis=0)
            out[i * ROWS : (i + 2) * ROWS, cols] = value.astype(BF16)


def mine_kernel(*refs):
    *hidden, weight, out = refs
    rows = jnp.concatenate([piece[...] for piece in hidden], axis=0)
    out[...] = jnp.dot(rows, weight[...], preferred_element_type=F32)


def last_kernel(where, mine, *refs):
    *hidden, weight, kept, one, two, three, terms = refs
    half = mine.shape[0]
    rows = jnp.concatenate([piece[...] for piece in hidden], axis=0)
    for place in range(half // ROWS):
        terms[pl.ds(turned_row(place, where), ROWS), :] = mine[place * ROWS : (place + 1) * ROWS, :]
    product = jnp.dot(rows, weight[...], preferred_element_type=F32)
    for place in range(half // ROWS):
        terms[pl.ds(turned_row(half // ROWS + place, where), ROWS), :] = product[
            place * ROWS : (place + 1) * ROWS
        ]
    for i, out in enumerate((kept, one, two, three)):
        rows = slice(i * 2 * half // NX, (i + 1) * 2 * half // NX)
        out[...] = terms[rows, :].astype(out.dtype)


def last_products(where, mine, theirs, weight):
    half = sum(p.shape[0] for p in mine)
    depth, cols = weight.shape
    flops = 2 * half * depth * cols
    (product,) = local_call(mine_kernel, [((half, cols), F32)], *mine, weight, flops=flops)
    shape = (2 * half // NX, cols)
    return local_call(
        last_kernel,
        [(shape, F32)] + [(shape, BF16)] * 3,
        product,
        *theirs,
        weight,
        scalars=[where],
        scratch=[pltpu.VMEM((2 * half, cols), F32)],
        limit=4,
        flops=flops,
    )


def over_x_kernel(total, one, two, three, kept, sent):
    half = total.shape[0] // NL
    for i, out in ((1, sent), (0, kept)):
        rows = slice(i * half, (i + 1) * half)
        value = total[rows, :] + one[rows, :].astype(F32)
        value = value + two[rows, :].astype(F32) + three[rows, :].astype(F32)
        out[...] = value.astype(out.dtype)


def local(tokens, gate_payload, gate_scales, up_payload, up_scales, down_payload, down_scales):
    index = lax.axis_index("gx")
    where = jnp.stack([index % NC, (index // NC) % NY, index // (NY * NC)]).astype(jnp.int32)

    count = tokens.shape[0] * NL * NX
    gate = weights(gate_payload, gate_scales, 4)
    (order,) = local_call(order_kernel, [((count, count), BF16)], scalars=[where])
    pair = after(join(tokens, move_gy(tokens, dl=1)), gate, order)
    up = weights(after(up_payload, pair), up_scales, 4)
    two, one, three = move_gy(pair, dx=2), move_gy(pair, dx=1), move_gy(pair, dx=3)
    pieces = [pair, one, two, after(three, up)]

    depth, cols = gate.shape[0], 2 * gate.shape[1]
    rows = count // NC
    flops = 2 * rows * depth * cols
    features, sent = local_call(
        sent_kernel,
        [((rows, depth), BF16), ((rows, cols), BF16)],
        *pieces,
        order,
        gate,
        up,
        flops=flops,
    )
    received = move_gx(sent, dc=1)
    (kept,) = local_call(kept_kernel, [((rows, cols), F32)], features, gate, up, flops=flops)

    step = (rows // 8, cols)
    far0, far1, next1, back0 = local_call(leave_kernel, [(step, BF16)] * 4, kept, received)
    relay0, relay1 = move_gx(far0, dy=1), move_gx(far1, dy=-1)
    direct1, direct0 = move_gx(next1, dy=1), move_gx(back0, dy=-1)
    through0, through1 = local_call(
        relay_kernel, [(step, BF16)] * 2, kept, received, relay0, relay1
    )
    down = weights(after(down_payload, through0), down_scales.T, 13, flipped=True)
    through0, through1 = move_gx(through0, dy=1), move_gx(through1, dy=-1)
    units = cols // 2
    piece = (2 * ROWS, units)
    kept = after(kept, down)
    two, three = local_call(
        lambda *refs: over_y_kernel(1, *refs),
        [(piece, BF16)] * 2,
        kept,
        received,
        direct1,
        through1,
    )
    two = move_gx(two, dz=2)
    mine, one = local_call(
        lambda *refs: over_y_kernel(0, *refs),
        [(piece, F32), (piece, BF16)],
        kept,
        received,
        direct0,
        through0,
    )
    one, three = move_gx(one, dz=1), move_gx(three, dz=3)
    (hidden,) = local_call(hidden_kernel, [((ROWS, units), BF16)], mine, one, two, three)

    two, one, three = move_gx(hidden, dz=-2), move_gx(hidden, dz=-1), move_gx(hidden, dz=-3)
    (hidden,) = local_call(rows_kernel, [((NZ * ROWS, units), BF16)], hidden, one, two, three)
    two, one, three = move_gx(hidden, dy=-2), move_gx(hidden, dy=-1), move_gx(hidden, dy=-3)
    mine = [hidden, one, two, three]
    theirs = [move_gx(hidden, dc=1)]
    theirs += [move_gx(after(block, one, two, three), dc=1) for block in mine[1:]]
    total, one, two, three = last_products(where, mine, theirs, down)

    two, one, three = move_gy(two, dx=-2), move_gy(one, dx=-1), move_gy(three, dx=-3)
    shape = (total.shape[0] // NL, total.shape[1])
    total, sent = local_call(over_x_kernel, [(shape, F32), (shape, BF16)], total, one, two, three)
    return (total + move_gy(sent, dl=1).astype(F32)).astype(BF16)


def solution(mesh):
    placed = (
        P("gy", "gx"),
        P("gx", "gy"),
        P("gx", "gy"),
        P("gx", "gy"),
        P("gx", "gy"),
        P("gy", "gx"),
        P("gy", "gx"),
    )
    return jax.shard_map(
        local, mesh=mesh, in_specs=placed, out_specs=P("gy", "gx"), check_vma=False
    )
```

time: 100 us -> 89.7 us (0.90)
  waiting for transfers between devices: 43.8 us -> 34.3 us
  Pallas kernels: 16.1 us -> 12 us
  starting transfers between devices: 38.4 us -> 42.3 us
    ppermute x20, waiting for transfers between devices: 33.2 us -> 24.1 us  [move_gx(): return lax.ppermute(x, 'gx', pairs)]
    ppermute x20, starting transfers between devices: 27.4 us -> 32 us  [move_gx(): return lax.ppermute(x, 'gx', pairs)]
    pallas_call x10 -> x13, Pallas kernels: 7.84 us -> 5.61 us  [local_call(): pl.pallas_call(kernel, in_specs=[SMEM] * len(scalars) + [VMEM] * len(arra...]
    pallas_call x3, Pallas kernels: 8.26 us -> 6.35 us  [weights(): pl.pallas_call(lambda *refs: weights_kernel(steps, flipped, *refs), in_sp...]
  transfers between devices with their start and end apart: 28 -> 28, of which waited for: 18 -> 20; matrix products, arithmetic and copies ran while one was open for 0% -> 0% of each run, Pallas kernels for 10% -> 10%
where the time goes in v3:
time: 89.7 us; the launch traced here: 89.4 us
  starting transfers between devices  42.3 us (47%)
  waiting for transfers between devices  34.3 us (38%)
  Pallas kernels  12 us (13%)
    ppermute x20, starting transfers between devices, move_gx(): return lax.ppermute(x, 'gx', pairs)  32 us
    ppermute x20, waiting for transfers between devices, move_gx(): return lax.ppermute(x, 'gx', pairs)  24.1 us
    ppermute x8, waiting for transfers between devices, move_gy(): return lax.ppermute(x, 'gy', pairs)  10.3 us
    ppermute x8, starting transfers between devices, move_gy(): return lax.ppermute(x, 'gy', pairs)  10.3 us
    pallas_call x3, Pallas kernels, weights(): pl.pallas_call(lambda *refs: weights_kernel(steps, flipped, *refs), in_sp...  6.35 us
    pallas_call x13, Pallas kernels, local_call(): pl.pallas_call(kernel, in_specs=[SMEM] * len(scalars) + [VMEM] * len(arra...  5.61 us
  transfers between devices with their start and end apart: 28, of which 20 were waited for; matrix products, arithmetic and copies ran while one was open for 0% of the time, Pallas kernels for 10%

profile of v3, /device:TPU:8, one launch (start us, length us, event | category | flops | bytes accessed | tf_op | source)
XLA Modules:
  0.0 89.4 jit_solution(17484133326558968929)
XLA Ops:
  0.0 1.9 %collective-permute-start = (bf16[32,512]{1,0:T(8,128)(2,1)}, bf16[32,512]{1,0:T(8,128)(2,1)S(1)}, u32[]{:S(2)}, u32[]{:S(2)}) collective-permute-start(bf16[32,512]{1,0:T(8,128)(2,1)} %refs_0_.2), channel_id=1, source_target_pairs={{0,4},{1,5},{2,6},{3,7},{4,0},{5,1},{6,2},{7,3},{8,12},{9,13},{10,... | collective-permute-start | bytes 98312 | tf_op jit(solution)/shard_map/ppermute | solution.py:35
  2.0 0.8 shard_map.75.refs_4_
  2.8 2.1 %shard_map.74.refs_5_.gate = bf16[512,3328]{1,0:T(8,128)(2,1)S(1)} custom-call(bf16[512,3328]{1,0:T(8,128)(2,1)} %refs_0_.3, f32[4,26]{1,0:T(4,128)} %refs_1_.2), custom_call_target="tpu_custom_call" | custom-call | flops 1703936 | bytes 6815744 | tf_op jit(solution)/shard_map/pallas_call | solution.py:90
  5.0 2.8 %collective-permute-start.3 = (bf16[64,512]{1,0:T(8,128)(2,1)S(1)}, bf16[64,512]{1,0:T(8,128)(2,1)S(1)}, u32[]{:S(2)}, u32[]{:S(2)}) collective-permute-start(bf16[64,512]{1,0:T(8,128)(2,1)S(1)} %shard_map.73.refs_0_), channel_id=1, source_target_pairs={{0,3},{1,0},{2,1},{3,2},{4,7},{5,4},{6,5},{7,6},{8,11},{9,8},{10,9... | collective-permute-start | bytes 196616 | tf_op jit(solution)/shard_map/ppermute | solution.py:35
  7.8 0.8 collective-permute-start.2
  8.6 0.9 collective-permute-start.1
  9.5 2.1 %shard_map.76.refs_6_.up = bf16[512,3328]{1,0:T(8,128)(2,1)S(1)} custom-call(bf16[512,3328]{1,0:T(8,128)(2,1)} %refs_0_.4, f32[4,26]{1,0:T(4,128)} %refs_1_.3), custom_call_target="tpu_custom_call" | custom-call | flops 1703936 | bytes 6815744 | tf_op jit(solution)/shard_map/pallas_call | solution.py:90
  11.7 1.9 %collective-permute-done.2.refs_2_ = bf16[64,512]{1,0:T(8,128)(2,1)S(1)} collective-permute-done((bf16[64,512]{1,0:T(8,128)(2,1)S(1)}, bf16[64,512]{1,0:T(8,128)(2,1)S(1)}, u32[]{:S(2)}, u32[]{:S(2)}) %collective-permute-start.2) | collective-permute-done | bytes 65568 | tf_op jit(solution)/shard_map/ppermute | solution.py:35
  13.6 0.7 collective-permute-done.1.refs_1_
  14.3 1.2 %shard_map.77 = (bf16[128,512]{1,0:T(8,128)(2,1)S(1)}, bf16[128,6656]{1,0:T(8,128)(2,1)S(1)}) custom-call(bf16[64,512]{1,0:T(8,128)(2,1)S(1)} %shard_map.73.refs_0_, bf16[64,512]{1,0:T(8,128)(2,1)S(1)} %collective-permute-done.1.refs_1_, bf16[64,512]{1,0:T(8,128)(2,1)S(1)} %collective-permute-done.2.refs_2_, ...), custom_call_target="tpu_custom_call" | custom-call | flops 872415232 | bytes 7208960 | tf_op jit(solution)/shard_map/pallas_call | solution.py:48
  15.7 1.1 %shard_map.78.kept.refs_0_ = f32[128,6656]{1,0:T(8,128)S(1)} custom-call(bf16[128,512]{1,0:T(8,128)(2,1)S(1)} %get-tuple-element.34.features, bf16[512,3328]{1,0:T(8,128)(2,1)S(1)} %shard_map.74.refs_5_.gate, bf16[512,3328]{1,0:T(8,128)(2,1)S(1)} %shard_map.76.refs_6_.up), custom_call_target="tpu_custom_call" | custom-call | flops 872415232 | bytes 6946816 | tf_op jit(solution)/shard_map/pallas_call | solution.py:48
  16.7 2.5 %collective-permute-done.4.received.refs_1_ = bf16[128,6656]{1,0:T(8,128)(2,1)S(1)} collective-permute-done((bf16[128,6656]{1,0:T(8,128)(2,1)S(1)}, bf16[128,6656]{1,0:T(8,128)(2,1)S(1)}, u32[]{:S(2)}, u32[]{:S(2)}) %collective-permute-start.4) | collective-permute-done | bytes 1703968 | tf_op jit(solution)/shard_map/ppermute | solution.py:27
  19.4 1.7 %collective-permute-start.5 = (bf16[16,6656]{1,0:T(8,128)(2,1)S(1)}, bf16[16,6656]{1,0:T(8,128)(2,1)S(1)}, u32[]{:S(2)}, u32[]{:S(2)}) collective-permute-start(bf16[16,6656]{1,0:T(8,128)(2,1)S(1)} %get-tuple-element.36), channel_id=1, source_target_pairs={{0,16},{8,24},{16,32},{24,40},{32,48},{40,56},{48,0},{56,8},{64,80... | collective-permute-start | bytes 638984 | tf_op jit(solution)/shard_map/ppermute | solution.py:27
  21.5 1.6 %collective-permute-start.10 = (bf16[16,6656]{1,0:T(8,128)(2,1)S(1)}, bf16[16,6656]{1,0:T(8,128)(2,1)S(1)}, u32[]{:S(2)}, u32[]{:S(2)}) collective-permute-start(bf16[16,6656]{1,0:T(8,128)(2,1)S(1)} %get-tuple-element.44), channel_id=1, source_target_pairs={{0,16},{8,24},{16,32},{24,40},{32,48},{40,56},{48,0},{56,8},{64,80... | collective-permute-start | bytes 638984 | tf_op jit(solution)/shard_map/ppermute | solution.py:27
  23.1 4.5 %collective-permute-done.5.relay0 = bf16[16,6656]{1,0:T(8,128)(2,1)S(1)} collective-permute-done((bf16[16,6656]{1,0:T(8,128)(2,1)S(1)}, bf16[16,6656]{1,0:T(8,128)(2,1)S(1)}, u32[]{:S(2)}, u32[]{:S(2)}) %collective-permute-start.5) | collective-permute-done | bytes 213024 | tf_op jit(solution)/shard_map/ppermute | solution.py:27
  27.6 0.5 collective-permute-done.6.relay1
  28.3 1.2 %collective-permute-start.11 = (bf16[16,6656]{1,0:T(8,128)(2,1)S(1)}, bf16[16,6656]{1,0:T(8,128)(2,1)S(1)}, u32[]{:S(2)}, u32[]{:S(2)}) collective-permute-start(bf16[16,6656]{1,0:T(8,128)(2,1)S(1)} %get-tuple-element.45), channel_id=1, source_target_pairs={{0,48},{8,56},{16,0},{24,8},{32,16},{40,24},{48,32},{56,40},{64,11... | collective-permute-start | bytes 638984 | tf_op jit(solution)/shard_map/ppermute | solution.py:27
  29.5 2.3 %collective-permute-start.7 = (bf16[16,6656]{1,0:T(8,128)(2,1)S(1)}, bf16[16,6656]{1,0:T(8,128)(2,1)S(1)}, u32[]{:S(2)}, u32[]{:S(2)}) collective-permute-start(bf16[16,6656]{1,0:T(8,128)(2,1)S(1)} %get-tuple-element.41), channel_id=1, source_target_pairs={{0,48},{8,56},{16,0},{24,8},{32,16},{40,24},{48,32},{56,40},{64,11... | collective-permute-start | bytes 638984 | tf_op jit(solution)/shard_map/ppermute | solution.py:27
  31.8 2.1 %shard_map.81.refs_4_ = bf16[3328,512]{1,0:T(8,128)(2,1)S(1)} custom-call(bf16[3328,512]{1,0:T(8,128)(2,1)} %refs_0_.5, f32[4,26]{1,0:T(4,128)} %bitcast.4), custom_call_target="tpu_custom_call" | custom-call | flops 1703936 | bytes 6815744 | tf_op jit(solution)/shard_map/pallas_call | solution.py:90
  33.9 2.6 %collective-permute-done.11.refs_3_ = bf16[16,6656]{1,0:T(8,128)(2,1)S(1)} collective-permute-done((bf16[16,6656]{1,0:T(8,128)(2,1)S(1)}, bf16[16,6656]{1,0:T(8,128)(2,1)S(1)}, u32[]{:S(2)}, u32[]{:S(2)}) %collective-permute-start.11) | collective-permute-done | bytes 213024 | tf_op jit(solution)/shard_map/ppermute | solution.py:27
  36.7 6.4 %collective-permute-start.12 = (bf16[16,3328]{1,0:T(8,128)(2,1)S(1)}, bf16[16,3328]{1,0:T(8,128)(2,1)S(1)}, u32[]{:S(2)}, u32[]{:S(2)}) collective-permute-start(bf16[16,3328]{1,0:T(8,128)(2,1)S(1)} %get-tuple-element.46), channel_id=1, source_target_pairs={{0,128},{8,136},{16,144},{24,152},{32,160},{40,168},{48,176},{56,1... | collective-permute-start | bytes 319496 | tf_op jit(solution)/shard_map/ppermute | solution.py:27
  43.1 0.5 collective-permute-start.13
  43.7 2.5 %collective-permute-start.9 = (bf16[16,3328]{1,0:T(8,128)(2,1)S(1)}, bf16[16,3328]{1,0:T(8,128)(2,1)S(1)}, u32[]{:S(2)}, u32[]{:S(2)}) collective-permute-start(bf16[16,3328]{1,0:T(8,128)(2,1)S(1)} %get-tuple-element.43), channel_id=1, source_target_pairs={{0,64},{8,72},{16,80},{24,88},{32,96},{40,104},{48,112},{56,120},{... | collective-permute-start | bytes 319496 | tf_op jit(solution)/shard_map/ppermute | solution.py:27
  46.2 0.9 collective-permute-done.12.two
  47.1 3.5 %collective-permute-done.13.three = bf16[16,3328]{1,0:T(8,128)(2,1)S(1)} collective-permute-done((bf16[16,3328]{1,0:T(8,128)(2,1)S(1)}, bf16[16,3328]{1,0:T(8,128)(2,1)S(1)}, u32[]{:S(2)}, u32[]{:S(2)}) %collective-permute-start.13) | collective-permute-done | bytes 106528 | tf_op jit(solution)/shard_map/ppermute | solution.py:27
  50.6 0.5 collective-permute-done.9.one
  51.2 2.1 %collective-permute-start.16 = (bf16[8,3328]{1,0:T(8,128)(2,1)S(1)}, bf16[8,3328]{1,0:T(8,128)(2,1)S(1)}, u32[]{:S(2)}, u32[]{:S(2)}) collective-permute-start(bf16[8,3328]{1,0:T(8,128)(2,1)S(1)} %shard_map.84.a), channel_id=1, source_target_pairs={{0,64},{8,72},{16,80},{24,88},{32,96},{40,104},{48,112},{56,120},{... | collective-permute-start | bytes 159752 | tf_op jit(solution)/shard_map/ppermute | solution.py:27
  53.2 3.1 %collective-permute-start.15 = (bf16[8,3328]{1,0:T(8,128)(2,1)S(1)}, bf16[8,3328]{1,0:T(8,128)(2,1)S(1)}, u32[]{:S(2)}, u32[]{:S(2)}) collective-permute-start(bf16[8,3328]{1,0:T(8,128)(2,1)S(1)} %shard_map.84.a), channel_id=1, source_target_pairs={{0,128},{8,136},{16,144},{24,152},{32,160},{40,168},{48,176},{56,1... | collective-permute-start | bytes 159752 | tf_op jit(solution)/shard_map/ppermute | solution.py:27
  56.3 3.7 %collective-permute-start.14 = (bf16[8,3328]{1,0:T(8,128)(2,1)S(1)}, bf16[8,3328]{1,0:T(8,128)(2,1)S(1)}, u32[]{:S(2)}, u32[]{:S(2)}) collective-permute-start(bf16[8,3328]{1,0:T(8,128)(2,1)S(1)} %shard_map.84.a), channel_id=1, source_target_pairs={{0,192},{8,200},{16,208},{24,216},{32,224},{40,232},{48,240},{56,2... | collective-permute-start | bytes 159752 | tf_op jit(solution)/shard_map/ppermute | solution.py:27
  60.0 1.2 %collective-permute-done.15.c = bf16[8,3328]{1,0:T(8,128)(2,1)S(1)} collective-permute-done((bf16[8,3328]{1,0:T(8,128)(2,1)S(1)}, bf16[8,3328]{1,0:T(8,128)(2,1)S(1)}, u32[]{:S(2)}, u32[]{:S(2)}) %collective-permute-start.15) | collective-permute-done | bytes 53280 | tf_op jit(solution)/shard_map/ppermute | solution.py:27
  61.3 1.8 %collective-permute-done.14.b = bf16[8,3328]{1,0:T(8,128)(2,1)S(1)} collective-permute-done((bf16[8,3328]{1,0:T(8,128)(2,1)S(1)}, bf16[8,3328]{1,0:T(8,128)(2,1)S(1)}, u32[]{:S(2)}, u32[]{:S(2)}) %collective-permute-start.14) | collective-permute-done | bytes 53280 | tf_op jit(solution)/shard_map/ppermute | solution.py:27
  63.1 1.4 %collective-permute-start.19 = (bf16[32,3328]{1,0:T(8,128)(2,1)S(1)}, bf16[32,3328]{1,0:T(8,128)(2,1)S(1)}, u32[]{:S(2)}, u32[]{:S(2)}) collective-permute-start(bf16[32,3328]{1,0:T(8,128)(2,1)S(1)} %shard_map.85.refs_0_), channel_id=1, source_target_pairs={{0,16},{8,24},{16,32},{24,40},{32,48},{40,56},{48,0},{56,8},{64,80... | collective-permute-start | bytes 638984 | tf_op jit(solution)/shard_map/ppermute | solution.py:27
  64.4 2.0 %collective-permute-start.18 = (bf16[32,3328]{1,0:T(8,128)(2,1)S(1)}, bf16[32,3328]{1,0:T(8,128)(2,1)S(1)}, u32[]{:S(2)}, u32[]{:S(2)}) collective-permute-start(bf16[32,3328]{1,0:T(8,128)(2,1)S(1)} %shard_map.85.refs_0_), channel_id=1, source_target_pairs={{0,32},{8,40},{16,48},{24,56},{32,0},{40,8},{48,16},{56,24},{64,96... | collective-permute-start | bytes 638984 | tf_op jit(solution)/shard_map/ppermute | solution.py:27
  66.4 2.5 %collective-permute-start.17 = (bf16[32,3328]{1,0:T(8,128)(2,1)S(1)}, bf16[32,3328]{1,0:T(8,128)(2,1)S(1)}, u32[]{:S(2)}, u32[]{:S(2)}) collective-permute-start(bf16[32,3328]{1,0:T(8,128)(2,1)S(1)} %shard_map.85.refs_0_), channel_id=1, source_target_pairs={{0,48},{8,56},{16,0},{24,8},{32,16},{40,24},{48,32},{56,40},{64,11... | collective-permute-start | bytes 638984 | tf_op jit(solution)/shard_map/ppermute | solution.py:27
  69.0 2.9 %collective-permute-done.18.refs_2_ = bf16[32,3328]{1,0:T(8,128)(2,1)S(1)} collective-permute-done((bf16[32,3328]{1,0:T(8,128)(2,1)S(1)}, bf16[32,3328]{1,0:T(8,128)(2,1)S(1)}, u32[]{:S(2)}, u32[]{:S(2)}) %collective-permute-start.18) | collective-permute-done | bytes 213024 | tf_op jit(solution)/shard_map/ppermute | solution.py:27
  71.9 2.2 %collective-permute-done.17.refs_1_ = bf16[32,3328]{1,0:T(8,128)(2,1)S(1)} collective-permute-done((bf16[32,3328]{1,0:T(8,128)(2,1)S(1)}, bf16[32,3328]{1,0:T(8,128)(2,1)S(1)}, u32[]{:S(2)}, u32[]{:S(2)}) %collective-permute-start.17) | collective-permute-done | bytes 213024 | tf_op jit(solution)/shard_map/ppermute | solution.py:27
  74.0 0.5 collective-permute-start.22
  74.6 0.6 shard_map.86.mine
  76.1 1.2 %shard_map.87 = (f32[64,512]{1,0:T(8,128)S(1)}, bf16[64,512]{1,0:T(8,128)(2,1)S(1)}, bf16[64,512]{1,0:T(8,128)(2,1)S(1)}, bf16[64,512]{1,0:T(8,128)(2,1)S(1)}) custom-call(s32[3]{0:T(128)S(1)} %pad_add_fusion.where, f32[128,512]{1,0:T(8,128)S(1)} %shard_map.86.mine, bf16[32,3328]{1,0:T(8,128)(2,1)S(1)} %collective-permute-done.20.refs_0_, ...), custom_call_target="tpu_custom_call" | custom-call | flops 436207616 | bytes 4521984 | tf_op jit(solution)/shard_map/pallas_call | solution.py:48
  77.3 0.6 collective-permute-start.24
  77.9 0.9 %collective-permute-start.25 = (bf16[64,512]{1,0:T(8,128)(2,1)S(1)}, bf16[64,512]{1,0:T(8,128)(2,1)S(1)}, u32[]{:S(2)}, u32[]{:S(2)}) collective-permute-start(bf16[64,512]{1,0:T(8,128)(2,1)S(1)} %get-tuple-element.53), channel_id=1, source_target_pairs={{0,2},{1,3},{2,0},{3,1},{4,6},{5,7},{6,4},{7,5},{8,10},{9,11},{10,... | collective-permute-start | bytes 196616 | tf_op jit(solution)/shard_map/ppermute | solution.py:35
  78.9 1.3 %collective-permute-start.26 = (bf16[64,512]{1,0:T(8,128)(2,1)S(1)}, bf16[64,512]{1,0:T(8,128)(2,1)S(1)}, u32[]{:S(2)}, u32[]{:S(2)}) collective-permute-start(bf16[64,512]{1,0:T(8,128)(2,1)S(1)} %get-tuple-element.54), channel_id=1, source_target_pairs={{0,1},{1,2},{2,3},{3,0},{4,5},{5,6},{6,7},{7,4},{8,9},{9,10},{10,1... | collective-permute-start | bytes 196616 | tf_op jit(solution)/shard_map/ppermute | solution.py:35
  80.1 2.2 %collective-permute-done.24.one = bf16[64,512]{1,0:T(8,128)(2,1)S(1)} collective-permute-done((bf16[64,512]{1,0:T(8,128)(2,1)S(1)}, bf16[64,512]{1,0:T(8,128)(2,1)S(1)}, u32[]{:S(2)}, u32[]{:S(2)}) %collective-permute-start.24) | collective-permute-done | bytes 65568 | tf_op jit(solution)/shard_map/ppermute | solution.py:35
  82.3 1.5 %collective-permute-done.25.two = bf16[64,512]{1,0:T(8,128)(2,1)S(1)} collective-permute-done((bf16[64,512]{1,0:T(8,128)(2,1)S(1)}, bf16[64,512]{1,0:T(8,128)(2,1)S(1)}, u32[]{:S(2)}, u32[]{:S(2)}) %collective-permute-start.25) | collective-permute-done | bytes 65568 | tf_op jit(solution)/shard_map/ppermute | solution.py:35
  83.8 1.0 %collective-permute-done.26.three = bf16[64,512]{1,0:T(8,128)(2,1)S(1)} collective-permute-done((bf16[64,512]{1,0:T(8,128)(2,1)S(1)}, bf16[64,512]{1,0:T(8,128)(2,1)S(1)}, u32[]{:S(2)}, u32[]{:S(2)}) %collective-permute-start.26) | collective-permute-done | bytes 65568 | tf_op jit(solution)/shard_map/ppermute | solution.py:35
  84.8 1.0 %collective-permute-start.27 = (bf16[32,512]{1,0:T(8,128)(2,1)S(1)}, bf16[32,512]{1,0:T(8,128)(2,1)S(1)}, u32[]{:S(2)}, u32[]{:S(2)}) collective-permute-start(bf16[32,512]{1,0:T(8,128)(2,1)S(1)} %get-tuple-element.56), channel_id=1, source_target_pairs={{0,4},{1,5},{2,6},{3,7},{4,0},{5,1},{6,2},{7,3},{8,12},{9,13},{10,... | collective-permute-start | bytes 98312 | tf_op jit(solution)/shard_map/ppermute | solution.py:35
  85.8 3.0 %collective-permute-done.27 = bf16[32,512]{1,0:T(8,128)(2,1)S(1)} collective-permute-done((bf16[32,512]{1,0:T(8,128)(2,1)S(1)}, bf16[32,512]{1,0:T(8,128)(2,1)S(1)}, u32[]{:S(2)}, u32[]{:S(2)}) %collective-permute-start.27) | collective-permute-done | bytes 32800 | tf_op jit(solution)/shard_map/ppermute | solution.py:35
  88.8 0.6 add_convert_fusion
  (28 shorter events, 2.3 us)
Async XLA Ops:
  0.0 5.0 %collective-permute-start = (bf16[32,512]{1,0:T(8,128)(2,1)}, bf16[32,512]{1,0:T(8,128)(2,1)S(1)}, u32[]{:S(2)}, u32[]{:S(2)}) collective-permute-start(bf16[32,512]{1,0:T(8,128)(2,1)} %refs_0_.2), channel_id=1, source_target_pairs={{0,4},{1,5},{2,6},{3,7},{4,0},{5,1},{6,2},{7,3},{8,12},{9,13},{10,... | collective-permute-start | bytes 98312 | tf_op jit(solution)/shard_map/ppermute | solution.py:35
  2.8 2.2 %copy-start = (bf16[32,512]{1,0:T(8,128)(2,1)S(1)}, bf16[32,512]{1,0:T(8,128)(2,1)}, u32[]{:S(2)}) copy-start(bf16[32,512]{1,0:T(8,128)(2,1)} %refs_0_.2) | copy-start | bytes 98308
  5.0 6.7 %collective-permute-start.3 = (bf16[64,512]{1,0:T(8,128)(2,1)S(1)}, bf16[64,512]{1,0:T(8,128)(2,1)S(1)}, u32[]{:S(2)}, u32[]{:S(2)}) collective-permute-start(bf16[64,512]{1,0:T(8,128)(2,1)S(1)} %shard_map.73.refs_0_), channel_id=1, source_target_pairs={{0,3},{1,0},{2,1},{3,2},{4,7},{5,4},{6,5},{7,6},{8,11},{9,8},{10,9... | collective-permute-start | bytes 196616 | tf_op jit(solution)/shard_map/ppermute | solution.py:35
  7.8 5.8 %collective-permute-start.2 = (bf16[64,512]{1,0:T(8,128)(2,1)S(1)}, bf16[64,512]{1,0:T(8,128)(2,1)S(1)}, u32[]{:S(2)}, u32[]{:S(2)}) collective-permute-start(bf16[64,512]{1,0:T(8,128)(2,1)S(1)} %shard_map.73.refs_0_), channel_id=1, source_target_pairs={{0,2},{1,3},{2,0},{3,1},{4,6},{5,7},{6,4},{7,5},{8,10},{9,11},{10,... | collective-permute-start | bytes 196616 | tf_op jit(solution)/shard_map/ppermute | solution.py:35
  8.6 5.7 %collective-permute-start.1 = (bf16[64,512]{1,0:T(8,128)(2,1)S(1)}, bf16[64,512]{1,0:T(8,128)(2,1)S(1)}, u32[]{:S(2)}, u32[]{:S(2)}) collective-permute-start(bf16[64,512]{1,0:T(8,128)(2,1)S(1)} %shard_map.73.refs_0_), channel_id=1, source_target_pairs={{0,1},{1,2},{2,3},{3,0},{4,5},{5,6},{6,7},{7,4},{8,9},{9,10},{10,1... | collective-permute-start | bytes 196616 | tf_op jit(solution)/shard_map/ppermute | solution.py:35
  15.6 3.7 %collective-permute-start.4 = (bf16[128,6656]{1,0:T(8,128)(2,1)S(1)}, bf16[128,6656]{1,0:T(8,128)(2,1)S(1)}, u32[]{:S(2)}, u32[]{:S(2)}) collective-permute-start(bf16[128,6656]{1,0:T(8,128)(2,1)S(1)} %get-tuple-element.35), channel_id=1, source_target_pairs={{0,8},{8,0},{16,24},{24,16},{32,40},{40,32},{48,56},{56,48},{64,72... | collective-permute-start | bytes 5111816 | tf_op jit(solution)/shard_map/ppermute | solution.py:27
  19.4 8.2 %collective-permute-start.5 = (bf16[16,6656]{1,0:T(8,128)(2,1)S(1)}, bf16[16,6656]{1,0:T(8,128)(2,1)S(1)}, u32[]{:S(2)}, u32[]{:S(2)}) collective-permute-start(bf16[16,6656]{1,0:T(8,128)(2,1)S(1)} %get-tuple-element.36), channel_id=1, source_target_pairs={{0,16},{8,24},{16,32},{24,40},{32,48},{40,56},{48,0},{56,8},{64,80... | collective-permute-start | bytes 638984 | tf_op jit(solution)/shard_map/ppermute | solution.py:27
  21.1 7.0 %collective-permute-start.6 = (bf16[16,6656]{1,0:T(8,128)(2,1)S(1)}, bf16[16,6656]{1,0:T(8,128)(2,1)S(1)}, u32[]{:S(2)}, u32[]{:S(2)}) collective-permute-start(bf16[16,6656]{1,0:T(8,128)(2,1)S(1)} %get-tuple-element.37), channel_id=1, source_target_pairs={{0,48},{8,56},{16,0},{24,8},{32,16},{40,24},{48,32},{56,40},{64,11... | collective-permute-start | bytes 638984 | tf_op jit(solution)/shard_map/ppermute | solution.py:27
  21.5 12.4 %collective-permute-start.10 = (bf16[16,6656]{1,0:T(8,128)(2,1)S(1)}, bf16[16,6656]{1,0:T(8,128)(2,1)S(1)}, u32[]{:S(2)}, u32[]{:S(2)}) collective-permute-start(bf16[16,6656]{1,0:T(8,128)(2,1)S(1)} %get-tuple-element.44), channel_id=1, source_target_pairs={{0,16},{8,24},{16,32},{24,40},{32,48},{40,56},{48,0},{56,8},{64,80... | collective-permute-start | bytes 638984 | tf_op jit(solution)/shard_map/ppermute | solution.py:27
  28.3 8.3 %collective-permute-start.11 = (bf16[16,6656]{1,0:T(8,128)(2,1)S(1)}, bf16[16,6656]{1,0:T(8,128)(2,1)S(1)}, u32[]{:S(2)}, u32[]{:S(2)}) collective-permute-start(bf16[16,6656]{1,0:T(8,128)(2,1)S(1)} %get-tuple-element.45), channel_id=1, source_target_pairs={{0,48},{8,56},{16,0},{24,8},{32,16},{40,24},{48,32},{56,40},{64,11... | collective-permute-start | bytes 638984 | tf_op jit(solution)/shard_map/ppermute | solution.py:27
  29.5 14.1 %collective-permute-start.7 = (bf16[16,6656]{1,0:T(8,128)(2,1)S(1)}, bf16[16,6656]{1,0:T(8,128)(2,1)S(1)}, u32[]{:S(2)}, u32[]{:S(2)}) collective-permute-start(bf16[16,6656]{1,0:T(8,128)(2,1)S(1)} %get-tuple-element.41), channel_id=1, source_target_pairs={{0,48},{8,56},{16,0},{24,8},{32,16},{40,24},{48,32},{56,40},{64,11... | collective-permute-start | bytes 638984 | tf_op jit(solution)/shard_map/ppermute | solution.py:27
  31.8 11.8 %collective-permute-start.8 = (bf16[16,6656]{1,0:T(8,128)(2,1)S(1)}, bf16[16,6656]{1,0:T(8,128)(2,1)S(1)}, u32[]{:S(2)}, u32[]{:S(2)}) collective-permute-start(bf16[16,6656]{1,0:T(8,128)(2,1)S(1)} %get-tuple-element.38), channel_id=1, source_target_pairs={{0,16},{8,24},{16,32},{24,40},{32,48},{40,56},{48,0},{56,8},{64,80... | collective-permute-start | bytes 638984 | tf_op jit(solution)/shard_map/ppermute | solution.py:27
  36.7 10.4 %collective-permute-start.12 = (bf16[16,3328]{1,0:T(8,128)(2,1)S(1)}, bf16[16,3328]{1,0:T(8,128)(2,1)S(1)}, u32[]{:S(2)}, u32[]{:S(2)}) collective-permute-start(bf16[16,3328]{1,0:T(8,128)(2,1)S(1)} %get-tuple-element.46), channel_id=1, source_target_pairs={{0,128},{8,136},{16,144},{24,152},{32,160},{40,168},{48,176},{56,1... | collective-permute-start | bytes 319496 | tf_op jit(solution)/shard_map/ppermute | solution.py:27
  43.1 7.5 %collective-permute-start.13 = (bf16[16,3328]{1,0:T(8,128)(2,1)S(1)}, bf16[16,3328]{1,0:T(8,128)(2,1)S(1)}, u32[]{:S(2)}, u32[]{:S(2)}) collective-permute-start(bf16[16,3328]{1,0:T(8,128)(2,1)S(1)} %get-tuple-element.47), channel_id=1, source_target_pairs={{0,192},{8,200},{16,208},{24,216},{32,224},{40,232},{48,240},{56,2... | collective-permute-start | bytes 319496 | tf_op jit(solution)/shard_map/ppermute | solution.py:27
  43.7 7.4 %collective-permute-start.9 = (bf16[16,3328]{1,0:T(8,128)(2,1)S(1)}, bf16[16,3328]{1,0:T(8,128)(2,1)S(1)}, u32[]{:S(2)}, u32[]{:S(2)}) collective-permute-start(bf16[16,3328]{1,0:T(8,128)(2,1)S(1)} %get-tuple-element.43), channel_id=1, source_target_pairs={{0,64},{8,72},{16,80},{24,88},{32,96},{40,104},{48,112},{56,120},{... | collective-permute-start | bytes 319496 | tf_op jit(solution)/shard_map/ppermute | solution.py:27
  51.2 8.9 %collective-permute-start.16 = (bf16[8,3328]{1,0:T(8,128)(2,1)S(1)}, bf16[8,3328]{1,0:T(8,128)(2,1)S(1)}, u32[]{:S(2)}, u32[]{:S(2)}) collective-permute-start(bf16[8,3328]{1,0:T(8,128)(2,1)S(1)} %shard_map.84.a), channel_id=1, source_target_pairs={{0,64},{8,72},{16,80},{24,88},{32,96},{40,104},{48,112},{56,120},{... | collective-permute-start | bytes 159752 | tf_op jit(solution)/shard_map/ppermute | solution.py:27
  53.2 8.0 %collective-permute-start.15 = (bf16[8,3328]{1,0:T(8,128)(2,1)S(1)}, bf16[8,3328]{1,0:T(8,128)(2,1)S(1)}, u32[]{:S(2)}, u32[]{:S(2)}) collective-permute-start(bf16[8,3328]{1,0:T(8,128)(2,1)S(1)} %shard_map.84.a), channel_id=1, source_target_pairs={{0,128},{8,136},{16,144},{24,152},{32,160},{40,168},{48,176},{56,1... | collective-permute-start | bytes 159752 | tf_op jit(solution)/shard_map/ppermute | solution.py:27
  56.3 6.7 %collective-permute-start.14 = (bf16[8,3328]{1,0:T(8,128)(2,1)S(1)}, bf16[8,3328]{1,0:T(8,128)(2,1)S(1)}, u32[]{:S(2)}, u32[]{:S(2)}) collective-permute-start(bf16[8,3328]{1,0:T(8,128)(2,1)S(1)} %shard_map.84.a), channel_id=1, source_target_pairs={{0,192},{8,200},{16,208},{24,216},{32,224},{40,232},{48,240},{56,2... | collective-permute-start | bytes 159752 | tf_op jit(solution)/shard_map/ppermute | solution.py:27
  63.1 5.9 %collective-permute-start.19 = (bf16[32,3328]{1,0:T(8,128)(2,1)S(1)}, bf16[32,3328]{1,0:T(8,128)(2,1)S(1)}, u32[]{:S(2)}, u32[]{:S(2)}) collective-permute-start(bf16[32,3328]{1,0:T(8,128)(2,1)S(1)} %shard_map.85.refs_0_), channel_id=1, source_target_pairs={{0,16},{8,24},{16,32},{24,40},{32,48},{40,56},{48,0},{56,8},{64,80... | collective-permute-start | bytes 638984 | tf_op jit(solution)/shard_map/ppermute | solution.py:27
  64.4 7.5 %collective-permute-start.18 = (bf16[32,3328]{1,0:T(8,128)(2,1)S(1)}, bf16[32,3328]{1,0:T(8,128)(2,1)S(1)}, u32[]{:S(2)}, u32[]{:S(2)}) collective-permute-start(bf16[32,3328]{1,0:T(8,128)(2,1)S(1)} %shard_map.85.refs_0_), channel_id=1, source_target_pairs={{0,32},{8,40},{16,48},{24,56},{32,0},{40,8},{48,16},{56,24},{64,96... | collective-permute-start | bytes 638984 | tf_op jit(solution)/shard_map/ppermute | solution.py:27
  66.4 7.6 %collective-permute-start.17 = (bf16[32,3328]{1,0:T(8,128)(2,1)S(1)}, bf16[32,3328]{1,0:T(8,128)(2,1)S(1)}, u32[]{:S(2)}, u32[]{:S(2)}) collective-permute-start(bf16[32,3328]{1,0:T(8,128)(2,1)S(1)} %shard_map.85.refs_0_), channel_id=1, source_target_pairs={{0,48},{8,56},{16,0},{24,8},{32,16},{40,24},{48,32},{56,40},{64,11... | collective-permute-start | bytes 638984 | tf_op jit(solution)/shard_map/ppermute | solution.py:27
  68.9 6.2 %collective-permute-start.20 = (bf16[32,3328]{1,0:T(8,128)(2,1)S(1)}, bf16[32,3328]{1,0:T(8,128)(2,1)S(1)}, u32[]{:S(2)}, u32[]{:S(2)}) collective-permute-start(bf16[32,3328]{1,0:T(8,128)(2,1)S(1)} %shard_map.85.refs_0_), channel_id=1, source_target_pairs={{0,8},{8,0},{16,24},{24,16},{32,40},{40,32},{48,56},{56,48},{64,72... | collective-permute-start | bytes 638984 | tf_op jit(solution)/shard_map/ppermute | solution.py:27
  74.0 1.5 %collective-permute-start.21 = (bf16[32,3328]{1,0:T(8,128)(2,1)S(1)}, bf16[32,3328]{1,0:T(8,128)(2,1)S(1)}, u32[]{:S(2)}, u32[]{:S(2)}) collective-permute-start(bf16[32,3328]{1,0:T(8,128)(2,1)S(1)} %collective-permute-done.17.refs_1_), channel_id=1, source_target_pairs={{0,8},{8,0},{16,24},{24,16},{32,40},{40,32},{48,56},{56,48},{64,72... | collective-permute-start | bytes 638984 | tf_op jit(solution)/shard_map/ppermute | solution.py:27
  74.0 1.8 %collective-permute-start.22 = (bf16[32,3328]{1,0:T(8,128)(2,1)S(1)}, bf16[32,3328]{1,0:T(8,128)(2,1)S(1)}, u32[]{:S(2)}, u32[]{:S(2)}) collective-permute-start(bf16[32,3328]{1,0:T(8,128)(2,1)S(1)} %collective-permute-done.18.refs_2_), channel_id=1, source_target_pairs={{0,8},{8,0},{16,24},{24,16},{32,40},{40,32},{48,56},{56,48},{64,72... | collective-permute-start | bytes 638984 | tf_op jit(solution)/shard_map/ppermute | solution.py:27
  74.6 1.6 %collective-permute-start.23 = (bf16[32,3328]{1,0:T(8,128)(2,1)S(1)}, bf16[32,3328]{1,0:T(8,128)(2,1)S(1)}, u32[]{:S(2)}, u32[]{:S(2)}) collective-permute-start(bf16[32,3328]{1,0:T(8,128)(2,1)S(1)} %collective-permute-done.19.refs_3_), channel_id=1, source_target_pairs={{0,8},{8,0},{16,24},{24,16},{32,40},{40,32},{48,56},{56,48},{64,72... | collective-permute-start | bytes 638984 | tf_op jit(solution)/shard_map/ppermute | solution.py:27
  77.3 5.0 %collective-permute-start.24 = (bf16[64,512]{1,0:T(8,128)(2,1)S(1)}, bf16[64,512]{1,0:T(8,128)(2,1)S(1)}, u32[]{:S(2)}, u32[]{:S(2)}) collective-permute-start(bf16[64,512]{1,0:T(8,128)(2,1)S(1)} %get-tuple-element.52), channel_id=1, source_target_pairs={{0,3},{1,0},{2,1},{3,2},{4,7},{5,4},{6,5},{7,6},{8,11},{9,8},{10,9... | collective-permute-start | bytes 196616 | tf_op jit(solution)/shard_map/ppermute | solution.py:35
  77.9 5.8 %collective-permute-start.25 = (bf16[64,512]{1,0:T(8,128)(2,1)S(1)}, bf16[64,512]{1,0:T(8,128)(2,1)S(1)}, u32[]{:S(2)}, u32[]{:S(2)}) collective-permute-start(bf16[64,512]{1,0:T(8,128)(2,1)S(1)} %get-tuple-element.53), channel_id=1, source_target_pairs={{0,2},{1,3},{2,0},{3,1},{4,6},{5,7},{6,4},{7,5},{8,10},{9,11},{10,... | collective-permute-start | bytes 196616 | tf_op jit(solution)/shard_map/ppermute | solution.py:35
  78.9 5.9 %collective-permute-start.26 = (bf16[64,512]{1,0:T(8,128)(2,1)S(1)}, bf16[64,512]{1,0:T(8,128)(2,1)S(1)}, u32[]{:S(2)}, u32[]{:S(2)}) collective-permute-start(bf16[64,512]{1,0:T(8,128)(2,1)S(1)} %get-tuple-element.54), channel_id=1, source_target_pairs={{0,1},{1,2},{2,3},{3,0},{4,5},{5,6},{6,7},{7,4},{8,9},{9,10},{10,1... | collective-permute-start | bytes 196616 | tf_op jit(solution)/shard_map/ppermute | solution.py:35
  84.8 4.0 %collective-permute-start.27 = (bf16[32,512]{1,0:T(8,128)(2,1)S(1)}, bf16[32,512]{1,0:T(8,128)(2,1)S(1)}, u32[]{:S(2)}, u32[]{:S(2)}) collective-permute-start(bf16[32,512]{1,0:T(8,128)(2,1)S(1)} %get-tuple-element.56), channel_id=1, source_target_pairs={{0,4},{1,5},{2,6},{3,7},{4,0},{5,1},{6,2},{7,3},{8,12},{9,13},{10,... | collective-permute-start | bytes 98312 | tf_op jit(solution)/shard_map/ppermute | solution.py:35

commit v4 on v3

--- a/solution.py
+++ b/solution.py
@@ -10,7 +10,6 @@
 BF16 = jnp.bfloat16
 NZ, NY, NC, NL, NX = 4, 4, 2, 2, 4
 ROWS = 8
-SMEM = pl.BlockSpec(memory_space=pltpu.SMEM)
 VMEM = pl.BlockSpec(memory_space=pltpu.VMEM)
 HBM = pl.BlockSpec(memory_space=pltpu.HBM)
 MIB = 2**20
@@ -43,17 +42,17 @@
     return pltpu.with_memory_space_constraint(x, pltpu.VMEM)
 
 
-def local_call(kernel, outs, *arrays, scalars=(), scratch=(), limit=2, flops=0):
+def local_call(kernel, outs, *arrays, scratch=(), limit=2, flops=0):
     moved = sum(a.size * a.dtype.itemsize for a in arrays)
     return pl.pallas_call(
         kernel,
-        in_specs=[SMEM] * len(scalars) + [VMEM] * len(arrays),
+        in_specs=[VMEM] * len(arrays),
         out_specs=[VMEM] * len(outs),
         out_shape=[pltpu.VMEM(shape, dtype) for shape, dtype in outs],
         scratch_shapes=list(scratch),
         compiler_params=pltpu.CompilerParams(vmem_limit_bytes=limit * MIB),
         cost_estimate=pl.CostEstimate(flops=flops, bytes_accessed=moved, transcendentals=0),
-    )(*scalars, *[in_vmem(a) for a in arrays])
+    )(*[in_vmem(a) for a in arrays])
 
 
 def weights_kernel(steps, flipped, payload, scales, out, held, factors, sems, sem):
@@ -119,14 +118,20 @@
     return local_call(join_kernel, [(shape, BF16)], *pieces)[0]
 
 
-def order_kernel(where, out):
-    row = lax.broadcasted_iota(jnp.int32, out.shape, 0)
-    column = lax.broadcasted_iota(jnp.int32, out.shape, 1)
-    block, inner = row // ROWS, row % ROWS
-    c, y, z = block // (NY * NZ), block // NZ % NY, block % NZ
-    c, y, z = (where[0] + c) % NC, (where[1] + y) % NY, (where[2] + z) % NZ
-    chosen = ((c * NY + y) * NZ + z) * ROWS + inner
-    out[...] = jnp.where(chosen == column, 1.0, 0.0).astype(BF16)
+def position():
+    index = lax.axis_index("gx")
+    return index % NC, index // NC % NY, index // (NY * NC)
+
+
+def order_kernel(out):
+    where = position()
+    step = 2 * ROWS
+    for at in range(0, out.shape[0], step):
+        row = lax.broadcasted_iota(jnp.int32, (step, out.shape[1]), 0)
+        column = lax.broadcasted_iota(jnp.int32, (step, out.shape[1]), 1)
+        first, second = (turned_row(at // ROWS + i, where) for i in (0, 1))
+        chosen = jnp.where(row < ROWS, first, second - ROWS) + row
+        out[at : at + step, :] = jnp.where(chosen == column, 1.0, 0.0).astype(BF16)
 
 
 def turned_row(place, where):
@@ -185,12 +190,11 @@
     over_columns(kept.shape[1], 13 * BLOCK, body)
 
 
-def relay_kernel(kept, received, relay0, relay1, through0, through1):
+def relay_kernel(part, kept, received, relay, through):
     def body(at):
         cols = pl.ds(at, 13 * BLOCK)
-        for part, relay, out in ((2, relay0, through0), (7, relay1, through1)):
-            value = summed(kept, received, part, cols) + relay[:, cols].astype(F32)
-            out[:, cols] = value.astype(BF16)
+        value = summed(kept, received, part, cols) + relay[:, cols].astype(F32)
+        through[:, cols] = value.astype(BF16)
 
     over_columns(kept.shape[1], 13 * BLOCK, body)
 
@@ -231,7 +235,8 @@
     out[...] = jnp.dot(rows, weight[...], preferred_element_type=F32)
 
 
-def last_kernel(where, mine, *refs):
+def last_kernel(mine, *refs):
+    where = position()
     *hidden, weight, kept, one, two, three, terms = refs
     half = mine.shape[0]
     rows = jnp.concatenate([piece[...] for piece in hidden], axis=0)
@@ -247,7 +252,7 @@
         out[...] = terms[rows, :].astype(out.dtype)
 
 
-def last_products(where, mine, theirs, weight):
+def last_products(mine, theirs, weight):
     half = sum(p.shape[0] for p in mine)
     depth, cols = weight.shape
     flops = 2 * half * depth * cols
@@ -259,7 +264,6 @@
         product,
         *theirs,
         weight,
-        scalars=[where],
         scratch=[pltpu.VMEM((2 * half, cols), F32)],
         limit=4,
         flops=flops,
@@ -276,12 +280,9 @@
 
 
 def local(tokens, gate_payload, gate_scales, up_payload, up_scales, down_payload, down_scales):
-    index = lax.axis_index("gx")
-    where = jnp.stack([index % NC, (index // NC) % NY, index // (NY * NC)]).astype(jnp.int32)
-
     count = tokens.shape[0] * NL * NX
     gate = weights(gate_payload, gate_scales, 4)
-    (order,) = local_call(order_kernel, [((count, count), BF16)], scalars=[where])
+    (order,) = local_call(order_kernel, [((count, count), BF16)])
     pair = after(join(tokens, move_gy(tokens, dl=1)), gate, order)
     up = weights(after(up_payload, pair), up_scales, 4)
     two, one, three = move_gy(pair, dx=2), move_gy(pair, dx=1), move_gy(pair, dx=3)
@@ -306,11 +307,14 @@
     far0, far1, next1, back0 = local_call(leave_kernel, [(step, BF16)] * 4, kept, received)
     relay0, relay1 = move_gx(far0, dy=1), move_gx(far1, dy=-1)
     direct1, direct0 = move_gx(next1, dy=1), move_gx(back0, dy=-1)
-    through0, through1 = local_call(
-        relay_kernel, [(step, BF16)] * 2, kept, received, relay0, relay1
+    (through1,) = local_call(
+        lambda *refs: relay_kernel(7, *refs), [(step, BF16)], kept, received, relay1
+    )
+    (through0,) = local_call(
+        lambda *refs: relay_kernel(2, *refs), [(step, BF16)], kept, received, after(relay0, through1)
     )
     down = weights(after(down_payload, through0), down_scales.T, 13, flipped=True)
-    through0, through1 = move_gx(through0, dy=1), move_gx(through1, dy=-1)
+    through1, through0 = move_gx(through1, dy=-1), move_gx(through0, dy=1)
     units = cols // 2
     piece = (2 * ROWS, units)
     kept = after(kept, down)
@@ -339,8 +343,8 @@
     two, one, three = move_gx(hidden, dy=-2), move_gx(hidden, dy=-1), move_gx(hidden, dy=-3)
     mine = [hidden, one, two, three]
     theirs = [move_gx(hidden, dc=1)]
-    theirs += [move_gx(after(block, one, two, three), dc=1) for block in mine[1:]]
-    total, one, two, three = last_products(where, mine, theirs, down)
+    theirs += [move_gx(block, dc=1) for block in mine[1:]]
+    total, one, two, three = last_products(mine, theirs, down)
 
     two, one, three = move_gy(two, dx=-2), move_gy(one, dx=-1), move_gy(three, dx=-3)
     shape = (total.shape[0] // NL, total.shape[1])

time: 89.7 us -> 88.7 us (0.989)
  starting transfers between devices: 42.3 us -> 43.8 us
  Pallas kernels: 12 us -> 10.7 us
  waiting for transfers between devices: 34.3 us -> 33.2 us
    ppermute x20, starting transfers between devices: 32 us -> 33.7 us  [move_gx(): return lax.ppermute(x, 'gx', pairs)]
    pallas_call x13 -> x14, Pallas kernels: 5.61 us -> 4.33 us  [local_call(): pl.pallas_call(kernel, in_specs=[VMEM] * len(arrays), out_specs=[VMEM] *...]
    ppermute x20, waiting for transfers between devices: 24.1 us -> 22.8 us  [move_gx(): return lax.ppermute(x, 'gx', pairs)]
  transfers between devices with their start and end apart: 28 -> 28, of which waited for: 20 -> 17; matrix products, arithmetic and copies ran while one was open for 0% -> 0% of each run, Pallas kernels for 10% -> 10%
where the time goes in v4:
time: 88.7 us; the launch traced here: 88.5 us
  starting transfers between devices  43.8 us (49%)
  waiting for transfers between devices  33.2 us (37%)
  Pallas kernels  10.7 us (12%)
    ppermute x20, starting transfers between devices, move_gx(): return lax.ppermute(x, 'gx', pairs)  33.7 us
    ppermute x20, waiting for transfers between devices, move_gx(): return lax.ppermute(x, 'gx', pairs)  22.8 us
    ppermute x8, waiting for transfers between devices, move_gy(): return lax.ppermute(x, 'gy', pairs)  10.4 us
    ppermute x8, starting transfers between devices, move_gy(): return lax.ppermute(x, 'gy', pairs)  10.1 us
    pallas_call x3, Pallas kernels, weights(): pl.pallas_call(lambda *refs: weights_kernel(steps, flipped, *refs), in_sp...  6.36 us
    pallas_call x14, Pallas kernels, local_call(): pl.pallas_call(kernel, in_specs=[VMEM] * len(arrays), out_specs=[VMEM] *...  4.33 us
  transfers between devices with their start and end apart: 28, of which 17 were waited for; matrix products, arithmetic and copies ran while one was open for 0% of the time, Pallas kernels for 10%

profile of v4, /device:TPU:8, one launch (start us, length us, event | category | flops | bytes accessed | tf_op | source)
XLA Modules:
  0.0 88.5 jit_solution(4484230333433036393)
XLA Ops:
  0.0 1.9 %collective-permute-start = (bf16[32,512]{1,0:T(8,128)(2,1)}, bf16[32,512]{1,0:T(8,128)(2,1)S(1)}, u32[]{:S(2)}, u32[]{:S(2)}) collective-permute-start(bf16[32,512]{1,0:T(8,128)(2,1)} %refs_0_.2), channel_id=1, source_target_pairs={{0,4},{1,5},{2,6},{3,7},{4,0},{5,1},{6,2},{7,3},{8,12},{9,13},{10,... | collective-permute-start | bytes 98312 | tf_op jit(solution)/shard_map/ppermute | solution.py:34
  2.0 2.1 %shard_map.74.refs_5_.gate = bf16[512,3328]{1,0:T(8,128)(2,1)S(1)} custom-call(bf16[512,3328]{1,0:T(8,128)(2,1)} %refs_0_.3, f32[4,26]{1,0:T(4,128)} %refs_1_.2), custom_call_target="tpu_custom_call" | custom-call | flops 1703936 | bytes 6815744 | tf_op jit(solution)/shard_map/pallas_call | solution.py:89
  4.2 2.8 %collective-permute-start.3 = (bf16[64,512]{1,0:T(8,128)(2,1)S(1)}, bf16[64,512]{1,0:T(8,128)(2,1)S(1)}, u32[]{:S(2)}, u32[]{:S(2)}) collective-permute-start(bf16[64,512]{1,0:T(8,128)(2,1)S(1)} %shard_map.73.refs_0_), channel_id=1, source_target_pairs={{0,3},{1,0},{2,1},{3,2},{4,7},{5,4},{6,5},{7,6},{8,11},{9,8},{10,9... | collective-permute-start | bytes 196616 | tf_op jit(solution)/shard_map/ppermute | solution.py:34
  7.0 0.8 collective-permute-start.2
  7.8 0.9 %collective-permute-start.1 = (bf16[64,512]{1,0:T(8,128)(2,1)S(1)}, bf16[64,512]{1,0:T(8,128)(2,1)S(1)}, u32[]{:S(2)}, u32[]{:S(2)}) collective-permute-start(bf16[64,512]{1,0:T(8,128)(2,1)S(1)} %shard_map.73.refs_0_), channel_id=1, source_target_pairs={{0,1},{1,2},{2,3},{3,0},{4,5},{5,6},{6,7},{7,4},{8,9},{9,10},{10,1... | collective-permute-start | bytes 196616 | tf_op jit(solution)/shard_map/ppermute | solution.py:34
  8.7 2.1 %shard_map.76.refs_6_.up = bf16[512,3328]{1,0:T(8,128)(2,1)S(1)} custom-call(bf16[512,3328]{1,0:T(8,128)(2,1)} %refs_0_.4, f32[4,26]{1,0:T(4,128)} %refs_1_.3), custom_call_target="tpu_custom_call" | custom-call | flops 1703936 | bytes 6815744 | tf_op jit(solution)/shard_map/pallas_call | solution.py:89
  10.8 1.9 %collective-permute-done.2.refs_2_ = bf16[64,512]{1,0:T(8,128)(2,1)S(1)} collective-permute-done((bf16[64,512]{1,0:T(8,128)(2,1)S(1)}, bf16[64,512]{1,0:T(8,128)(2,1)S(1)}, u32[]{:S(2)}, u32[]{:S(2)}) %collective-permute-start.2) | collective-permute-done | bytes 65568 | tf_op jit(solution)/shard_map/ppermute | solution.py:34
  12.8 0.7 collective-permute-done.1.refs_1_
  13.5 1.2 %shard_map.77 = (bf16[128,512]{1,0:T(8,128)(2,1)S(1)}, bf16[128,6656]{1,0:T(8,128)(2,1)S(1)}) custom-call(bf16[64,512]{1,0:T(8,128)(2,1)S(1)} %shard_map.73.refs_0_, bf16[64,512]{1,0:T(8,128)(2,1)S(1)} %collective-permute-done.1.refs_1_, bf16[64,512]{1,0:T(8,128)(2,1)S(1)} %collective-permute-done.2.refs_2_, ...), custom_call_target="tpu_custom_call" | custom-call | flops 872415232 | bytes 7208960 | tf_op jit(solution)/shard_map/pallas_call | solution.py:47
  14.8 1.1 %shard_map.78.kept.refs_0_ = f32[128,6656]{1,0:T(8,128)S(1)} custom-call(bf16[128,512]{1,0:T(8,128)(2,1)S(1)} %get-tuple-element.30.features, bf16[512,3328]{1,0:T(8,128)(2,1)S(1)} %shard_map.74.refs_5_.gate, bf16[512,3328]{1,0:T(8,128)(2,1)S(1)} %shard_map.76.refs_6_.up), custom_call_target="tpu_custom_call" | custom-call | flops 872415232 | bytes 6946816 | tf_op jit(solution)/shard_map/pallas_call | solution.py:47
  15.9 2.5 %collective-permute-done.4.received.refs_1_ = bf16[128,6656]{1,0:T(8,128)(2,1)S(1)} collective-permute-done((bf16[128,6656]{1,0:T(8,128)(2,1)S(1)}, bf16[128,6656]{1,0:T(8,128)(2,1)S(1)}, u32[]{:S(2)}, u32[]{:S(2)}) %collective-permute-start.4) | collective-permute-done | bytes 1703968 | tf_op jit(solution)/shard_map/ppermute | solution.py:26
  18.4 0.2 shard_map.79
  18.6 0.5 collective-permute-start.6
  19.1 1.6 %collective-permute-start.5 = (bf16[16,6656]{1,0:T(8,128)(2,1)S(1)}, bf16[16,6656]{1,0:T(8,128)(2,1)S(1)}, u32[]{:S(2)}, u32[]{:S(2)}) collective-permute-start(bf16[16,6656]{1,0:T(8,128)(2,1)S(1)} %get-tuple-element.32), channel_id=1, source_target_pairs={{0,16},{8,24},{16,32},{24,40},{32,48},{40,56},{48,0},{56,8},{64,80... | collective-permute-start | bytes 638984 | tf_op jit(solution)/shard_map/ppermute | solution.py:26
  20.7 1.6 %collective-permute-start.10 = (bf16[16,6656]{1,0:T(8,128)(2,1)S(1)}, bf16[16,6656]{1,0:T(8,128)(2,1)S(1)}, u32[]{:S(2)}, u32[]{:S(2)}) collective-permute-start(bf16[16,6656]{1,0:T(8,128)(2,1)S(1)} %get-tuple-element.40), channel_id=1, source_target_pairs={{0,16},{8,24},{16,32},{24,40},{32,48},{40,56},{48,0},{56,8},{64,80... | collective-permute-start | bytes 638984 | tf_op jit(solution)/shard_map/ppermute | solution.py:26
  22.3 3.7 %collective-permute-done.6.refs_2_ = bf16[16,6656]{1,0:T(8,128)(2,1)S(1)} collective-permute-done((bf16[16,6656]{1,0:T(8,128)(2,1)S(1)}, bf16[16,6656]{1,0:T(8,128)(2,1)S(1)}, u32[]{:S(2)}, u32[]{:S(2)}) %collective-permute-start.6) | collective-permute-done | bytes 213024 | tf_op jit(solution)/shard_map/ppermute | solution.py:26
  26.1 1.1 %collective-permute-start.11 = (bf16[16,6656]{1,0:T(8,128)(2,1)S(1)}, bf16[16,6656]{1,0:T(8,128)(2,1)S(1)}, u32[]{:S(2)}, u32[]{:S(2)}) collective-permute-start(bf16[16,6656]{1,0:T(8,128)(2,1)S(1)} %shard_map.80), channel_id=1, source_target_pairs={{0,48},{8,56},{16,0},{24,8},{32,16},{40,24},{48,32},{56,40},{64,11... | collective-permute-start | bytes 638984 | tf_op jit(solution)/shard_map/ppermute | solution.py:26
  27.1 3.7 %collective-permute-start.7 = (bf16[16,6656]{1,0:T(8,128)(2,1)S(1)}, bf16[16,6656]{1,0:T(8,128)(2,1)S(1)}, u32[]{:S(2)}, u32[]{:S(2)}) collective-permute-start(bf16[16,6656]{1,0:T(8,128)(2,1)S(1)} %get-tuple-element.37), channel_id=1, source_target_pairs={{0,48},{8,56},{16,0},{24,8},{32,16},{40,24},{48,32},{56,40},{64,11... | collective-permute-start | bytes 638984 | tf_op jit(solution)/shard_map/ppermute | solution.py:26
  30.9 0.3 collective-permute-start.8
  31.2 2.1 %shard_map.82.refs_4_ = bf16[3328,512]{1,0:T(8,128)(2,1)S(1)} custom-call(bf16[3328,512]{1,0:T(8,128)(2,1)} %refs_0_.5, f32[4,26]{1,0:T(4,128)} %bitcast.1), custom_call_target="tpu_custom_call" | custom-call | flops 1703936 | bytes 6815744 | tf_op jit(solution)/shard_map/pallas_call | solution.py:89
  33.3 1.0 %collective-permute-done.11.refs_3_ = bf16[16,6656]{1,0:T(8,128)(2,1)S(1)} collective-permute-done((bf16[16,6656]{1,0:T(8,128)(2,1)S(1)}, bf16[16,6656]{1,0:T(8,128)(2,1)S(1)}, u32[]{:S(2)}, u32[]{:S(2)}) %collective-permute-start.11) | collective-permute-done | bytes 213024 | tf_op jit(solution)/shard_map/ppermute | solution.py:26
  34.5 7.2 %collective-permute-start.12 = (bf16[16,3328]{1,0:T(8,128)(2,1)S(1)}, bf16[16,3328]{1,0:T(8,128)(2,1)S(1)}, u32[]{:S(2)}, u32[]{:S(2)}) collective-permute-start(bf16[16,3328]{1,0:T(8,128)(2,1)S(1)} %get-tuple-element.41), channel_id=1, source_target_pairs={{0,128},{8,136},{16,144},{24,152},{32,160},{40,168},{48,176},{56,1... | collective-permute-start | bytes 319496 | tf_op jit(solution)/shard_map/ppermute | solution.py:26
  41.8 3.0 %collective-permute-start.9 = (bf16[16,3328]{1,0:T(8,128)(2,1)S(1)}, bf16[16,3328]{1,0:T(8,128)(2,1)S(1)}, u32[]{:S(2)}, u32[]{:S(2)}) collective-permute-start(bf16[16,3328]{1,0:T(8,128)(2,1)S(1)} %get-tuple-element.39), channel_id=1, source_target_pairs={{0,64},{8,72},{16,80},{24,88},{32,96},{40,104},{48,112},{56,120},{... | collective-permute-start | bytes 319496 | tf_op jit(solution)/shard_map/ppermute | solution.py:26
  44.8 0.7 collective-permute-done.12.two
  45.5 4.5 %collective-permute-done.13.three = bf16[16,3328]{1,0:T(8,128)(2,1)S(1)} collective-permute-done((bf16[16,3328]{1,0:T(8,128)(2,1)S(1)}, bf16[16,3328]{1,0:T(8,128)(2,1)S(1)}, u32[]{:S(2)}, u32[]{:S(2)}) %collective-permute-start.13) | collective-permute-done | bytes 106528 | tf_op jit(solution)/shard_map/ppermute | solution.py:26
  50.1 1.5 %collective-permute-start.16 = (bf16[8,3328]{1,0:T(8,128)(2,1)S(1)}, bf16[8,3328]{1,0:T(8,128)(2,1)S(1)}, u32[]{:S(2)}, u32[]{:S(2)}) collective-permute-start(bf16[8,3328]{1,0:T(8,128)(2,1)S(1)} %shard_map.85.a), channel_id=1, source_target_pairs={{0,64},{8,72},{16,80},{24,88},{32,96},{40,104},{48,112},{56,120},{... | collective-permute-start | bytes 159752 | tf_op jit(solution)/shard_map/ppermute | solution.py:26
  51.6 4.0 %collective-permute-start.15 = (bf16[8,3328]{1,0:T(8,128)(2,1)S(1)}, bf16[8,3328]{1,0:T(8,128)(2,1)S(1)}, u32[]{:S(2)}, u32[]{:S(2)}) collective-permute-start(bf16[8,3328]{1,0:T(8,128)(2,1)S(1)} %shard_map.85.a), channel_id=1, source_target_pairs={{0,128},{8,136},{16,144},{24,152},{32,160},{40,168},{48,176},{56,1... | collective-permute-start | bytes 159752 | tf_op jit(solution)/shard_map/ppermute | solution.py:26
  55.6 3.1 %collective-permute-start.14 = (bf16[8,3328]{1,0:T(8,128)(2,1)S(1)}, bf16[8,3328]{1,0:T(8,128)(2,1)S(1)}, u32[]{:S(2)}, u32[]{:S(2)}) collective-permute-start(bf16[8,3328]{1,0:T(8,128)(2,1)S(1)} %shard_map.85.a), channel_id=1, source_target_pairs={{0,192},{8,200},{16,208},{24,216},{32,224},{40,232},{48,240},{56,2... | collective-permute-start | bytes 159752 | tf_op jit(solution)/shard_map/ppermute | solution.py:26
  58.7 2.1 %collective-permute-done.15.c = bf16[8,3328]{1,0:T(8,128)(2,1)S(1)} collective-permute-done((bf16[8,3328]{1,0:T(8,128)(2,1)S(1)}, bf16[8,3328]{1,0:T(8,128)(2,1)S(1)}, u32[]{:S(2)}, u32[]{:S(2)}) %collective-permute-start.15) | collective-permute-done | bytes 53280 | tf_op jit(solution)/shard_map/ppermute | solution.py:26
  60.8 2.0 %collective-permute-done.14.b = bf16[8,3328]{1,0:T(8,128)(2,1)S(1)} collective-permute-done((bf16[8,3328]{1,0:T(8,128)(2,1)S(1)}, bf16[8,3328]{1,0:T(8,128)(2,1)S(1)}, u32[]{:S(2)}, u32[]{:S(2)}) %collective-permute-start.14) | collective-permute-done | bytes 53280 | tf_op jit(solution)/shard_map/ppermute | solution.py:26
  62.9 1.1 %collective-permute-start.19 = (bf16[32,3328]{1,0:T(8,128)(2,1)S(1)}, bf16[32,3328]{1,0:T(8,128)(2,1)S(1)}, u32[]{:S(2)}, u32[]{:S(2)}) collective-permute-start(bf16[32,3328]{1,0:T(8,128)(2,1)S(1)} %shard_map.86.refs_0_), channel_id=1, source_target_pairs={{0,16},{8,24},{16,32},{24,40},{32,48},{40,56},{48,0},{56,8},{64,80... | collective-permute-start | bytes 638984 | tf_op jit(solution)/shard_map/ppermute | solution.py:26
  64.0 2.3 %collective-permute-start.18 = (bf16[32,3328]{1,0:T(8,128)(2,1)S(1)}, bf16[32,3328]{1,0:T(8,128)(2,1)S(1)}, u32[]{:S(2)}, u32[]{:S(2)}) collective-permute-start(bf16[32,3328]{1,0:T(8,128)(2,1)S(1)} %shard_map.86.refs_0_), channel_id=1, source_target_pairs={{0,32},{8,40},{16,48},{24,56},{32,0},{40,8},{48,16},{56,24},{64,96... | collective-permute-start | bytes 638984 | tf_op jit(solution)/shard_map/ppermute | solution.py:26
  66.2 2.5 %collective-permute-start.17 = (bf16[32,3328]{1,0:T(8,128)(2,1)S(1)}, bf16[32,3328]{1,0:T(8,128)(2,1)S(1)}, u32[]{:S(2)}, u32[]{:S(2)}) collective-permute-start(bf16[32,3328]{1,0:T(8,128)(2,1)S(1)} %shard_map.86.refs_0_), channel_id=1, source_target_pairs={{0,48},{8,56},{16,0},{24,8},{32,16},{40,24},{48,32},{56,40},{64,11... | collective-permute-start | bytes 638984 | tf_op jit(solution)/shard_map/ppermute | solution.py:26
  68.8 0.4 collective-permute-done.19.refs_3_
  69.3 3.3 %collective-permute-done.18.refs_2_ = bf16[32,3328]{1,0:T(8,128)(2,1)S(1)} collective-permute-done((bf16[32,3328]{1,0:T(8,128)(2,1)S(1)}, bf16[32,3328]{1,0:T(8,128)(2,1)S(1)}, u32[]{:S(2)}, u32[]{:S(2)}) %collective-permute-start.18) | collective-permute-done | bytes 213024 | tf_op jit(solution)/shard_map/ppermute | solution.py:26
  72.6 1.7 %collective-permute-done.17.refs_1_ = bf16[32,3328]{1,0:T(8,128)(2,1)S(1)} collective-permute-done((bf16[32,3328]{1,0:T(8,128)(2,1)S(1)}, bf16[32,3328]{1,0:T(8,128)(2,1)S(1)}, u32[]{:S(2)}, u32[]{:S(2)}) %collective-permute-start.17) | collective-permute-done | bytes 213024 | tf_op jit(solution)/shard_map/ppermute | solution.py:26
  74.4 0.6 shard_map.87.mine
  75.0 0.8 collective-permute-done.21.refs_1_
  75.8 0.6 shard_map.88
  76.5 0.6 collective-permute-start.24
  77.1 1.0 %collective-permute-start.25 = (bf16[64,512]{1,0:T(8,128)(2,1)S(1)}, bf16[64,512]{1,0:T(8,128)(2,1)S(1)}, u32[]{:S(2)}, u32[]{:S(2)}) collective-permute-start(bf16[64,512]{1,0:T(8,128)(2,1)S(1)} %get-tuple-element.45), channel_id=1, source_target_pairs={{0,2},{1,3},{2,0},{3,1},{4,6},{5,7},{6,4},{7,5},{8,10},{9,11},{10,... | collective-permute-start | bytes 196616 | tf_op jit(solution)/shard_map/ppermute | solution.py:34
  78.1 1.2 %collective-permute-start.26 = (bf16[64,512]{1,0:T(8,128)(2,1)S(1)}, bf16[64,512]{1,0:T(8,128)(2,1)S(1)}, u32[]{:S(2)}, u32[]{:S(2)}) collective-permute-start(bf16[64,512]{1,0:T(8,128)(2,1)S(1)} %get-tuple-element.46), channel_id=1, source_target_pairs={{0,1},{1,2},{2,3},{3,0},{4,5},{5,6},{6,7},{7,4},{8,9},{9,10},{10,1... | collective-permute-start | bytes 196616 | tf_op jit(solution)/shard_map/ppermute | solution.py:34
  79.3 2.1 %collective-permute-done.24.one = bf16[64,512]{1,0:T(8,128)(2,1)S(1)} collective-permute-done((bf16[64,512]{1,0:T(8,128)(2,1)S(1)}, bf16[64,512]{1,0:T(8,128)(2,1)S(1)}, u32[]{:S(2)}, u32[]{:S(2)}) %collective-permute-start.24) | collective-permute-done | bytes 65568 | tf_op jit(solution)/shard_map/ppermute | solution.py:34
  81.4 1.5 %collective-permute-done.25.two = bf16[64,512]{1,0:T(8,128)(2,1)S(1)} collective-permute-done((bf16[64,512]{1,0:T(8,128)(2,1)S(1)}, bf16[64,512]{1,0:T(8,128)(2,1)S(1)}, u32[]{:S(2)}, u32[]{:S(2)}) %collective-permute-start.25) | collective-permute-done | bytes 65568 | tf_op jit(solution)/shard_map/ppermute | solution.py:34
  82.9 0.9 %collective-permute-done.26.three = bf16[64,512]{1,0:T(8,128)(2,1)S(1)} collective-permute-done((bf16[64,512]{1,0:T(8,128)(2,1)S(1)}, bf16[64,512]{1,0:T(8,128)(2,1)S(1)}, u32[]{:S(2)}, u32[]{:S(2)}) %collective-permute-start.26) | collective-permute-done | bytes 65568 | tf_op jit(solution)/shard_map/ppermute | solution.py:34
  83.9 0.9 collective-permute-start.27
  84.8 3.1 %collective-permute-done.27 = bf16[32,512]{1,0:T(8,128)(2,1)S(1)} collective-permute-done((bf16[32,512]{1,0:T(8,128)(2,1)S(1)}, bf16[32,512]{1,0:T(8,128)(2,1)S(1)}, u32[]{:S(2)}, u32[]{:S(2)}) %collective-permute-start.27) | collective-permute-done | bytes 32800 | tf_op jit(solution)/shard_map/ppermute | solution.py:34
  87.9 0.6 add_convert_fusion
  (28 shorter events, 0.9 us)
Async XLA Ops:
  0.0 4.1 %collective-permute-start = (bf16[32,512]{1,0:T(8,128)(2,1)}, bf16[32,512]{1,0:T(8,128)(2,1)S(1)}, u32[]{:S(2)}, u32[]{:S(2)}) collective-permute-start(bf16[32,512]{1,0:T(8,128)(2,1)} %refs_0_.2), channel_id=1, source_target_pairs={{0,4},{1,5},{2,6},{3,7},{4,0},{5,1},{6,2},{7,3},{8,12},{9,13},{10,... | collective-permute-start | bytes 98312 | tf_op jit(solution)/shard_map/ppermute | solution.py:34
  2.0 2.2 %copy-start = (bf16[32,512]{1,0:T(8,128)(2,1)S(1)}, bf16[32,512]{1,0:T(8,128)(2,1)}, u32[]{:S(2)}) copy-start(bf16[32,512]{1,0:T(8,128)(2,1)} %refs_0_.2) | copy-start | bytes 98308
  4.2 6.7 %collective-permute-start.3 = (bf16[64,512]{1,0:T(8,128)(2,1)S(1)}, bf16[64,512]{1,0:T(8,128)(2,1)S(1)}, u32[]{:S(2)}, u32[]{:S(2)}) collective-permute-start(bf16[64,512]{1,0:T(8,128)(2,1)S(1)} %shard_map.73.refs_0_), channel_id=1, source_target_pairs={{0,3},{1,0},{2,1},{3,2},{4,7},{5,4},{6,5},{7,6},{8,11},{9,8},{10,9... | collective-permute-start | bytes 196616 | tf_op jit(solution)/shard_map/ppermute | solution.py:34
  7.0 5.8 %collective-permute-start.2 = (bf16[64,512]{1,0:T(8,128)(2,1)S(1)}, bf16[64,512]{1,0:T(8,128)(2,1)S(1)}, u32[]{:S(2)}, u32[]{:S(2)}) collective-permute-start(bf16[64,512]{1,0:T(8,128)(2,1)S(1)} %shard_map.73.refs_0_), channel_id=1, source_target_pairs={{0,2},{1,3},{2,0},{3,1},{4,6},{5,7},{6,4},{7,5},{8,10},{9,11},{10,... | collective-permute-start | bytes 196616 | tf_op jit(solution)/shard_map/ppermute | solution.py:34
  7.8 5.7 %collective-permute-start.1 = (bf16[64,512]{1,0:T(8,128)(2,1)S(1)}, bf16[64,512]{1,0:T(8,128)(2,1)S(1)}, u32[]{:S(2)}, u32[]{:S(2)}) collective-permute-start(bf16[64,512]{1,0:T(8,128)(2,1)S(1)} %shard_map.73.refs_0_), channel_id=1, source_target_pairs={{0,1},{1,2},{2,3},{3,0},{4,5},{5,6},{6,7},{7,4},{8,9},{9,10},{10,1... | collective-permute-start | bytes 196616 | tf_op jit(solution)/shard_map/ppermute | solution.py:34
  14.7 3.7 %collective-permute-start.4 = (bf16[128,6656]{1,0:T(8,128)(2,1)S(1)}, bf16[128,6656]{1,0:T(8,128)(2,1)S(1)}, u32[]{:S(2)}, u32[]{:S(2)}) collective-permute-start(bf16[128,6656]{1,0:T(8,128)(2,1)S(1)} %get-tuple-element.31), channel_id=1, source_target_pairs={{0,8},{8,0},{16,24},{24,16},{32,40},{40,32},{48,56},{56,48},{64,72... | collective-permute-start | bytes 5111816 | tf_op jit(solution)/shard_map/ppermute | solution.py:26
  18.6 7.4 %collective-permute-start.6 = (bf16[16,6656]{1,0:T(8,128)(2,1)S(1)}, bf16[16,6656]{1,0:T(8,128)(2,1)S(1)}, u32[]{:S(2)}, u32[]{:S(2)}) collective-permute-start(bf16[16,6656]{1,0:T(8,128)(2,1)S(1)} %get-tuple-element.33), channel_id=1, source_target_pairs={{0,48},{8,56},{16,0},{24,8},{32,16},{40,24},{48,32},{56,40},{64,11... | collective-permute-start | bytes 638984 | tf_op jit(solution)/shard_map/ppermute | solution.py:26
  19.1 11.7 %collective-permute-start.5 = (bf16[16,6656]{1,0:T(8,128)(2,1)S(1)}, bf16[16,6656]{1,0:T(8,128)(2,1)S(1)}, u32[]{:S(2)}, u32[]{:S(2)}) collective-permute-start(bf16[16,6656]{1,0:T(8,128)(2,1)S(1)} %get-tuple-element.32), channel_id=1, source_target_pairs={{0,16},{8,24},{16,32},{24,40},{32,48},{40,56},{48,0},{56,8},{64,80... | collective-permute-start | bytes 638984 | tf_op jit(solution)/shard_map/ppermute | solution.py:26
  20.7 12.6 %collective-permute-start.10 = (bf16[16,6656]{1,0:T(8,128)(2,1)S(1)}, bf16[16,6656]{1,0:T(8,128)(2,1)S(1)}, u32[]{:S(2)}, u32[]{:S(2)}) collective-permute-start(bf16[16,6656]{1,0:T(8,128)(2,1)S(1)} %get-tuple-element.40), channel_id=1, source_target_pairs={{0,16},{8,24},{16,32},{24,40},{32,48},{40,56},{48,0},{56,8},{64,80... | collective-permute-start | bytes 638984 | tf_op jit(solution)/shard_map/ppermute | solution.py:26
  26.1 8.3 %collective-permute-start.11 = (bf16[16,6656]{1,0:T(8,128)(2,1)S(1)}, bf16[16,6656]{1,0:T(8,128)(2,1)S(1)}, u32[]{:S(2)}, u32[]{:S(2)}) collective-permute-start(bf16[16,6656]{1,0:T(8,128)(2,1)S(1)} %shard_map.80), channel_id=1, source_target_pairs={{0,48},{8,56},{16,0},{24,8},{32,16},{40,24},{48,32},{56,40},{64,11... | collective-permute-start | bytes 638984 | tf_op jit(solution)/shard_map/ppermute | solution.py:26
  27.1 14.6 %collective-permute-start.7 = (bf16[16,6656]{1,0:T(8,128)(2,1)S(1)}, bf16[16,6656]{1,0:T(8,128)(2,1)S(1)}, u32[]{:S(2)}, u32[]{:S(2)}) collective-permute-start(bf16[16,6656]{1,0:T(8,128)(2,1)S(1)} %get-tuple-element.37), channel_id=1, source_target_pairs={{0,48},{8,56},{16,0},{24,8},{32,16},{40,24},{48,32},{56,40},{64,11... | collective-permute-start | bytes 638984 | tf_op jit(solution)/shard_map/ppermute | solution.py:26
  30.9 10.8 %collective-permute-start.8 = (bf16[16,6656]{1,0:T(8,128)(2,1)S(1)}, bf16[16,6656]{1,0:T(8,128)(2,1)S(1)}, u32[]{:S(2)}, u32[]{:S(2)}) collective-permute-start(bf16[16,6656]{1,0:T(8,128)(2,1)S(1)} %shard_map.81), channel_id=1, source_target_pairs={{0,16},{8,24},{16,32},{24,40},{32,48},{40,56},{48,0},{56,8},{64,80... | collective-permute-start | bytes 638984 | tf_op jit(solution)/shard_map/ppermute | solution.py:26
  34.5 11.0 %collective-permute-start.12 = (bf16[16,3328]{1,0:T(8,128)(2,1)S(1)}, bf16[16,3328]{1,0:T(8,128)(2,1)S(1)}, u32[]{:S(2)}, u32[]{:S(2)}) collective-permute-start(bf16[16,3328]{1,0:T(8,128)(2,1)S(1)} %get-tuple-element.41), channel_id=1, source_target_pairs={{0,128},{8,136},{16,144},{24,152},{32,160},{40,168},{48,176},{56,1... | collective-permute-start | bytes 319496 | tf_op jit(solution)/shard_map/ppermute | solution.py:26
  41.7 8.3 %collective-permute-start.13 = (bf16[16,3328]{1,0:T(8,128)(2,1)S(1)}, bf16[16,3328]{1,0:T(8,128)(2,1)S(1)}, u32[]{:S(2)}, u32[]{:S(2)}) collective-permute-start(bf16[16,3328]{1,0:T(8,128)(2,1)S(1)} %get-tuple-element.42), channel_id=1, source_target_pairs={{0,192},{8,200},{16,208},{24,216},{32,224},{40,232},{48,240},{56,2... | collective-permute-start | bytes 319496 | tf_op jit(solution)/shard_map/ppermute | solution.py:26
  41.8 8.2 %collective-permute-start.9 = (bf16[16,3328]{1,0:T(8,128)(2,1)S(1)}, bf16[16,3328]{1,0:T(8,128)(2,1)S(1)}, u32[]{:S(2)}, u32[]{:S(2)}) collective-permute-start(bf16[16,3328]{1,0:T(8,128)(2,1)S(1)} %get-tuple-element.39), channel_id=1, source_target_pairs={{0,64},{8,72},{16,80},{24,88},{32,96},{40,104},{48,112},{56,120},{... | collective-permute-start | bytes 319496 | tf_op jit(solution)/shard_map/ppermute | solution.py:26
  50.1 8.6 %collective-permute-start.16 = (bf16[8,3328]{1,0:T(8,128)(2,1)S(1)}, bf16[8,3328]{1,0:T(8,128)(2,1)S(1)}, u32[]{:S(2)}, u32[]{:S(2)}) collective-permute-start(bf16[8,3328]{1,0:T(8,128)(2,1)S(1)} %shard_map.85.a), channel_id=1, source_target_pairs={{0,64},{8,72},{16,80},{24,88},{32,96},{40,104},{48,112},{56,120},{... | collective-permute-start | bytes 159752 | tf_op jit(solution)/shard_map/ppermute | solution.py:26
  51.6 9.2 %collective-permute-start.15 = (bf16[8,3328]{1,0:T(8,128)(2,1)S(1)}, bf16[8,3328]{1,0:T(8,128)(2,1)S(1)}, u32[]{:S(2)}, u32[]{:S(2)}) collective-permute-start(bf16[8,3328]{1,0:T(8,128)(2,1)S(1)} %shard_map.85.a), channel_id=1, source_target_pairs={{0,128},{8,136},{16,144},{24,152},{32,160},{40,168},{48,176},{56,1... | collective-permute-start | bytes 159752 | tf_op jit(solution)/shard_map/ppermute | solution.py:26
  55.6 7.3 %collective-permute-start.14 = (bf16[8,3328]{1,0:T(8,128)(2,1)S(1)}, bf16[8,3328]{1,0:T(8,128)(2,1)S(1)}, u32[]{:S(2)}, u32[]{:S(2)}) collective-permute-start(bf16[8,3328]{1,0:T(8,128)(2,1)S(1)} %shard_map.85.a), channel_id=1, source_target_pairs={{0,192},{8,200},{16,208},{24,216},{32,224},{40,232},{48,240},{56,2... | collective-permute-start | bytes 159752 | tf_op jit(solution)/shard_map/ppermute | solution.py:26
  62.9 6.3 %collective-permute-start.19 = (bf16[32,3328]{1,0:T(8,128)(2,1)S(1)}, bf16[32,3328]{1,0:T(8,128)(2,1)S(1)}, u32[]{:S(2)}, u32[]{:S(2)}) collective-permute-start(bf16[32,3328]{1,0:T(8,128)(2,1)S(1)} %shard_map.86.refs_0_), channel_id=1, source_target_pairs={{0,16},{8,24},{16,32},{24,40},{32,48},{40,56},{48,0},{56,8},{64,80... | collective-permute-start | bytes 638984 | tf_op jit(solution)/shard_map/ppermute | solution.py:26
  64.0 8.6 %collective-permute-start.18 = (bf16[32,3328]{1,0:T(8,128)(2,1)S(1)}, bf16[32,3328]{1,0:T(8,128)(2,1)S(1)}, u32[]{:S(2)}, u32[]{:S(2)}) collective-permute-start(bf16[32,3328]{1,0:T(8,128)(2,1)S(1)} %shard_map.86.refs_0_), channel_id=1, source_target_pairs={{0,32},{8,40},{16,48},{24,56},{32,0},{40,8},{48,16},{56,24},{64,96... | collective-permute-start | bytes 638984 | tf_op jit(solution)/shard_map/ppermute | solution.py:26
  66.2 8.1 %collective-permute-start.17 = (bf16[32,3328]{1,0:T(8,128)(2,1)S(1)}, bf16[32,3328]{1,0:T(8,128)(2,1)S(1)}, u32[]{:S(2)}, u32[]{:S(2)}) collective-permute-start(bf16[32,3328]{1,0:T(8,128)(2,1)S(1)} %shard_map.86.refs_0_), channel_id=1, source_target_pairs={{0,48},{8,56},{16,0},{24,8},{32,16},{40,24},{48,32},{56,40},{64,11... | collective-permute-start | bytes 638984 | tf_op jit(solution)/shard_map/ppermute | solution.py:26
  68.8 6.2 %collective-permute-start.20 = (bf16[32,3328]{1,0:T(8,128)(2,1)S(1)}, bf16[32,3328]{1,0:T(8,128)(2,1)S(1)}, u32[]{:S(2)}, u32[]{:S(2)}) collective-permute-start(bf16[32,3328]{1,0:T(8,128)(2,1)S(1)} %shard_map.86.refs_0_), channel_id=1, source_target_pairs={{0,8},{8,0},{16,24},{24,16},{32,40},{40,32},{48,56},{56,48},{64,72... | collective-permute-start | bytes 638984 | tf_op jit(solution)/shard_map/ppermute | solution.py:26
  69.2 5.8 %collective-permute-start.23 = (bf16[32,3328]{1,0:T(8,128)(2,1)S(1)}, bf16[32,3328]{1,0:T(8,128)(2,1)S(1)}, u32[]{:S(2)}, u32[]{:S(2)}) collective-permute-start(bf16[32,3328]{1,0:T(8,128)(2,1)S(1)} %collective-permute-done.19.refs_3_), channel_id=1, source_target_pairs={{0,8},{8,0},{16,24},{24,16},{32,40},{40,32},{48,56},{56,48},{64,72... | collective-permute-start | bytes 638984 | tf_op jit(solution)/shard_map/ppermute | solution.py:26
  72.6 2.4 %collective-permute-start.22 = (bf16[32,3328]{1,0:T(8,128)(2,1)S(1)}, bf16[32,3328]{1,0:T(8,128)(2,1)S(1)}, u32[]{:S(2)}, u32[]{:S(2)}) collective-permute-start(bf16[32,3328]{1,0:T(8,128)(2,1)S(1)} %collective-permute-done.18.refs_2_), channel_id=1, source_target_pairs={{0,8},{8,0},{16,24},{24,16},{32,40},{40,32},{48,56},{56,48},{64,72... | collective-permute-start | bytes 638984 | tf_op jit(solution)/shard_map/ppermute | solution.py:26
  74.4 1.5 %collective-permute-start.21 = (bf16[32,3328]{1,0:T(8,128)(2,1)S(1)}, bf16[32,3328]{1,0:T(8,128)(2,1)S(1)}, u32[]{:S(2)}, u32[]{:S(2)}) collective-permute-start(bf16[32,3328]{1,0:T(8,128)(2,1)S(1)} %collective-permute-done.17.refs_1_), channel_id=1, source_target_pairs={{0,8},{8,0},{16,24},{24,16},{32,40},{40,32},{48,56},{56,48},{64,72... | collective-permute-start | bytes 638984 | tf_op jit(solution)/shard_map/ppermute | solution.py:26
  76.5 4.9 %collective-permute-start.24 = (bf16[64,512]{1,0:T(8,128)(2,1)S(1)}, bf16[64,512]{1,0:T(8,128)(2,1)S(1)}, u32[]{:S(2)}, u32[]{:S(2)}) collective-permute-start(bf16[64,512]{1,0:T(8,128)(2,1)S(1)} %get-tuple-element.44), channel_id=1, source_target_pairs={{0,3},{1,0},{2,1},{3,2},{4,7},{5,4},{6,5},{7,6},{8,11},{9,8},{10,9... | collective-permute-start | bytes 196616 | tf_op jit(solution)/shard_map/ppermute | solution.py:34
  77.1 5.8 %collective-permute-start.25 = (bf16[64,512]{1,0:T(8,128)(2,1)S(1)}, bf16[64,512]{1,0:T(8,128)(2,1)S(1)}, u32[]{:S(2)}, u32[]{:S(2)}) collective-permute-start(bf16[64,512]{1,0:T(8,128)(2,1)S(1)} %get-tuple-element.45), channel_id=1, source_target_pairs={{0,2},{1,3},{2,0},{3,1},{4,6},{5,7},{6,4},{7,5},{8,10},{9,11},{10,... | collective-permute-start | bytes 196616 | tf_op jit(solution)/shard_map/ppermute | solution.py:34
  78.1 5.8 %collective-permute-start.26 = (bf16[64,512]{1,0:T(8,128)(2,1)S(1)}, bf16[64,512]{1,0:T(8,128)(2,1)S(1)}, u32[]{:S(2)}, u32[]{:S(2)}) collective-permute-start(bf16[64,512]{1,0:T(8,128)(2,1)S(1)} %get-tuple-element.46), channel_id=1, source_target_pairs={{0,1},{1,2},{2,3},{3,0},{4,5},{5,6},{6,7},{7,4},{8,9},{9,10},{10,1... | collective-permute-start | bytes 196616 | tf_op jit(solution)/shard_map/ppermute | solution.py:34
  83.9 4.0 %collective-permute-start.27 = (bf16[32,512]{1,0:T(8,128)(2,1)S(1)}, bf16[32,512]{1,0:T(8,128)(2,1)S(1)}, u32[]{:S(2)}, u32[]{:S(2)}) collective-permute-start(bf16[32,512]{1,0:T(8,128)(2,1)S(1)} %get-tuple-element.48), channel_id=1, source_target_pairs={{0,4},{1,5},{2,6},{3,7},{4,0},{5,1},{6,2},{7,3},{8,12},{9,13},{10,... | collective-permute-start | bytes 98312 | tf_op jit(solution)/shard_map/ppermute | solution.py:34

commit v5 on v4

--- a/solution.py
+++ b/solution.py
@@ -222,6 +222,15 @@
         hidden[:, cols] = (jax.nn.silu(total[:ROWS]) * total[ROWS:]).astype(BF16)
 
 
+def corner_kernel(x, out):
+    out[...] = x[: out.shape[0], : out.shape[1]]
+
+
+def first_awaited(first, *others):
+    (corner,) = local_call(corner_kernel, [((8, BLOCK), first.dtype)], first)
+    return [after(x, corner) for x in others]
+
+
 def rows_kernel(a, b, c, d, out):
     for i, pair in ((0, (a, b)), (2, (c, d))):
         for cols in columns(out.shape[1], 2 * BLOCK):
@@ -339,6 +348,7 @@
     (hidden,) = local_call(hidden_kernel, [((ROWS, units), BF16)], mine, one, two, three)
 
     two, one, three = move_gx(hidden, dz=-2), move_gx(hidden, dz=-1), move_gx(hidden, dz=-3)
+    one, three = first_awaited(two, one, three)
     (hidden,) = local_call(rows_kernel, [((NZ * ROWS, units), BF16)], hidden, one, two, three)
     two, one, three = move_gx(hidden, dy=-2), move_gx(hidden, dy=-1), move_gx(hidden, dy=-3)
     mine = [hidden, one, two, three]
@@ -347,6 +357,7 @@
     total, one, two, three = last_products(mine, theirs, down)
 
     two, one, three = move_gy(two, dx=-2), move_gy(one, dx=-1), move_gy(three, dx=-3)
+    one, three = first_awaited(two, one, three)
     shape = (total.shape[0] // NL, total.shape[1])
     total, sent = local_call(over_x_kernel, [(shape, F32), (shape, BF16)], total, one, two, three)
     return (total + move_gy(sent, dl=1).astype(F32)).astype(BF16)

time: 88.7 us -> 89.3 us (level)
  waiting for transfers between devices: 33.2 us -> 30.9 us
  starting transfers between devices: 43.8 us -> 45.9 us
    ppermute x8, starting transfers between devices: 10.1 us -> 11.9 us  [move_gy(): return lax.ppermute(x, 'gy', pairs)]
    ppermute x8, waiting for transfers between devices: 10.4 us -> 8.87 us  [move_gy(): return lax.ppermute(x, 'gy', pairs)]
  transfers between devices with their start and end apart: 28 -> 28, of which waited for: 17 -> 16; matrix products, arithmetic and copies ran while one was open for 0% -> 0% of each run, Pallas kernels for 10% -> 10%
where the time goes in v5:
time: 89.3 us; the launch traced here: 88.3 us
  starting transfers between devices  45.9 us (51%)
  waiting for transfers between devices  30.9 us (35%)
  Pallas kernels  10.7 us (12%)
    ppermute x20, starting transfers between devices, move_gx(): return lax.ppermute(x, 'gx', pairs)  34 us
    ppermute x20, waiting for transfers between devices, move_gx(): return lax.ppermute(x, 'gx', pairs)  22.1 us
    ppermute x8, starting transfers between devices, move_gy(): return lax.ppermute(x, 'gy', pairs)  11.9 us
    ppermute x8, waiting for transfers between devices, move_gy(): return lax.ppermute(x, 'gy', pairs)  8.87 us
    pallas_call x3, Pallas kernels, weights(): pl.pallas_call(lambda *refs: weights_kernel(steps, flipped, *refs), in_sp...  6.36 us
    pallas_call x14, Pallas kernels, local_call(): pl.pallas_call(kernel, in_specs=[VMEM] * len(arrays), out_specs=[VMEM] *...  4.32 us
  transfers between devices with their start and end apart: 28, of which 16 were waited for; matrix products, arithmetic and copies ran while one was open for 0% of the time, Pallas kernels for 10%

profile of v5, /device:TPU:8, one launch (start us, length us, event | category | flops | bytes accessed | tf_op | source)
XLA Modules:
  0.0 88.3 jit_solution(13282580279186195327)
XLA Ops:
  0.0 1.9 %collective-permute-start = (bf16[32,512]{1,0:T(8,128)(2,1)}, bf16[32,512]{1,0:T(8,128)(2,1)S(1)}, u32[]{:S(2)}, u32[]{:S(2)}) collective-permute-start(bf16[32,512]{1,0:T(8,128)(2,1)} %refs_0_.2), channel_id=1, source_target_pairs={{0,4},{1,5},{2,6},{3,7},{4,0},{5,1},{6,2},{7,3},{8,12},{9,13},{10,... | collective-permute-start | bytes 98312 | tf_op jit(solution)/shard_map/ppermute | solution.py:34
  2.0 2.1 %shard_map.74.refs_5_.gate = bf16[512,3328]{1,0:T(8,128)(2,1)S(1)} custom-call(bf16[512,3328]{1,0:T(8,128)(2,1)} %refs_0_.3, f32[4,26]{1,0:T(4,128)} %refs_1_.2), custom_call_target="tpu_custom_call" | custom-call | flops 1703936 | bytes 6815744 | tf_op jit(solution)/shard_map/pallas_call | solution.py:89
  4.2 2.8 %collective-permute-start.3 = (bf16[64,512]{1,0:T(8,128)(2,1)S(1)}, bf16[64,512]{1,0:T(8,128)(2,1)S(1)}, u32[]{:S(2)}, u32[]{:S(2)}) collective-permute-start(bf16[64,512]{1,0:T(8,128)(2,1)S(1)} %shard_map.73.refs_0_), channel_id=1, source_target_pairs={{0,3},{1,0},{2,1},{3,2},{4,7},{5,4},{6,5},{7,6},{8,11},{9,8},{10,9... | collective-permute-start | bytes 196616 | tf_op jit(solution)/shard_map/ppermute | solution.py:34
  7.0 0.8 collective-permute-start.2
  7.8 0.9 %collective-permute-start.1 = (bf16[64,512]{1,0:T(8,128)(2,1)S(1)}, bf16[64,512]{1,0:T(8,128)(2,1)S(1)}, u32[]{:S(2)}, u32[]{:S(2)}) collective-permute-start(bf16[64,512]{1,0:T(8,128)(2,1)S(1)} %shard_map.73.refs_0_), channel_id=1, source_target_pairs={{0,1},{1,2},{2,3},{3,0},{4,5},{5,6},{6,7},{7,4},{8,9},{9,10},{10,1... | collective-permute-start | bytes 196616 | tf_op jit(solution)/shard_map/ppermute | solution.py:34
  8.7 2.1 %shard_map.76.refs_6_.up = bf16[512,3328]{1,0:T(8,128)(2,1)S(1)} custom-call(bf16[512,3328]{1,0:T(8,128)(2,1)} %refs_0_.4, f32[4,26]{1,0:T(4,128)} %refs_1_.3), custom_call_target="tpu_custom_call" | custom-call | flops 1703936 | bytes 6815744 | tf_op jit(solution)/shard_map/pallas_call | solution.py:89
  10.8 1.9 %collective-permute-done.2.refs_2_ = bf16[64,512]{1,0:T(8,128)(2,1)S(1)} collective-permute-done((bf16[64,512]{1,0:T(8,128)(2,1)S(1)}, bf16[64,512]{1,0:T(8,128)(2,1)S(1)}, u32[]{:S(2)}, u32[]{:S(2)}) %collective-permute-start.2) | collective-permute-done | bytes 65568 | tf_op jit(solution)/shard_map/ppermute | solution.py:34
  12.8 0.7 collective-permute-done.1.refs_1_
  13.5 1.2 %shard_map.77 = (bf16[128,512]{1,0:T(8,128)(2,1)S(1)}, bf16[128,6656]{1,0:T(8,128)(2,1)S(1)}) custom-call(bf16[64,512]{1,0:T(8,128)(2,1)S(1)} %shard_map.73.refs_0_, bf16[64,512]{1,0:T(8,128)(2,1)S(1)} %collective-permute-done.1.refs_1_, bf16[64,512]{1,0:T(8,128)(2,1)S(1)} %collective-permute-done.2.refs_2_, ...), custom_call_target="tpu_custom_call" | custom-call | flops 872415232 | bytes 7208960 | tf_op jit(solution)/shard_map/pallas_call | solution.py:47
  14.8 1.1 %shard_map.78.kept.refs_0_ = f32[128,6656]{1,0:T(8,128)S(1)} custom-call(bf16[128,512]{1,0:T(8,128)(2,1)S(1)} %get-tuple-element.34.features, bf16[512,3328]{1,0:T(8,128)(2,1)S(1)} %shard_map.74.refs_5_.gate, bf16[512,3328]{1,0:T(8,128)(2,1)S(1)} %shard_map.76.refs_6_.up), custom_call_target="tpu_custom_call" | custom-call | flops 872415232 | bytes 6946816 | tf_op jit(solution)/shard_map/pallas_call | solution.py:47
  15.9 2.5 %collective-permute-done.4.received.refs_1_ = bf16[128,6656]{1,0:T(8,128)(2,1)S(1)} collective-permute-done((bf16[128,6656]{1,0:T(8,128)(2,1)S(1)}, bf16[128,6656]{1,0:T(8,128)(2,1)S(1)}, u32[]{:S(2)}, u32[]{:S(2)}) %collective-permute-start.4) | collective-permute-done | bytes 1703968 | tf_op jit(solution)/shard_map/ppermute | solution.py:26
  18.4 0.2 shard_map.79
  18.6 0.5 collective-permute-start.6
  19.1 1.6 %collective-permute-start.5 = (bf16[16,6656]{1,0:T(8,128)(2,1)S(1)}, bf16[16,6656]{1,0:T(8,128)(2,1)S(1)}, u32[]{:S(2)}, u32[]{:S(2)}) collective-permute-start(bf16[16,6656]{1,0:T(8,128)(2,1)S(1)} %get-tuple-element.36), channel_id=1, source_target_pairs={{0,16},{8,24},{16,32},{24,40},{32,48},{40,56},{48,0},{56,8},{64,80... | collective-permute-start | bytes 638984 | tf_op jit(solution)/shard_map/ppermute | solution.py:26
  20.7 1.6 %collective-permute-start.10 = (bf16[16,6656]{1,0:T(8,128)(2,1)S(1)}, bf16[16,6656]{1,0:T(8,128)(2,1)S(1)}, u32[]{:S(2)}, u32[]{:S(2)}) collective-permute-start(bf16[16,6656]{1,0:T(8,128)(2,1)S(1)} %get-tuple-element.44), channel_id=1, source_target_pairs={{0,16},{8,24},{16,32},{24,40},{32,48},{40,56},{48,0},{56,8},{64,80... | collective-permute-start | bytes 638984 | tf_op jit(solution)/shard_map/ppermute | solution.py:26
  22.3 3.7 %collective-permute-done.6.refs_2_ = bf16[16,6656]{1,0:T(8,128)(2,1)S(1)} collective-permute-done((bf16[16,6656]{1,0:T(8,128)(2,1)S(1)}, bf16[16,6656]{1,0:T(8,128)(2,1)S(1)}, u32[]{:S(2)}, u32[]{:S(2)}) %collective-permute-start.6) | collective-permute-done | bytes 213024 | tf_op jit(solution)/shard_map/ppermute | solution.py:26
  26.1 1.1 %collective-permute-start.11 = (bf16[16,6656]{1,0:T(8,128)(2,1)S(1)}, bf16[16,6656]{1,0:T(8,128)(2,1)S(1)}, u32[]{:S(2)}, u32[]{:S(2)}) collective-permute-start(bf16[16,6656]{1,0:T(8,128)(2,1)S(1)} %shard_map.80), channel_id=1, source_target_pairs={{0,48},{8,56},{16,0},{24,8},{32,16},{40,24},{48,32},{56,40},{64,11... | collective-permute-start | bytes 638984 | tf_op jit(solution)/shard_map/ppermute | solution.py:26
  27.1 3.7 %collective-permute-start.7 = (bf16[16,6656]{1,0:T(8,128)(2,1)S(1)}, bf16[16,6656]{1,0:T(8,128)(2,1)S(1)}, u32[]{:S(2)}, u32[]{:S(2)}) collective-permute-start(bf16[16,6656]{1,0:T(8,128)(2,1)S(1)} %get-tuple-element.41), channel_id=1, source_target_pairs={{0,48},{8,56},{16,0},{24,8},{32,16},{40,24},{48,32},{56,40},{64,11... | collective-permute-start | bytes 638984 | tf_op jit(solution)/shard_map/ppermute | solution.py:26
  30.9 0.3 collective-permute-start.8
  31.2 2.1 %shard_map.82.refs_4_ = bf16[3328,512]{1,0:T(8,128)(2,1)S(1)} custom-call(bf16[3328,512]{1,0:T(8,128)(2,1)} %refs_0_.5, f32[4,26]{1,0:T(4,128)} %bitcast.1), custom_call_target="tpu_custom_call" | custom-call | flops 1703936 | bytes 6815744 | tf_op jit(solution)/shard_map/pallas_call | solution.py:89
  33.3 1.0 %collective-permute-done.11.refs_3_ = bf16[16,6656]{1,0:T(8,128)(2,1)S(1)} collective-permute-done((bf16[16,6656]{1,0:T(8,128)(2,1)S(1)}, bf16[16,6656]{1,0:T(8,128)(2,1)S(1)}, u32[]{:S(2)}, u32[]{:S(2)}) %collective-permute-start.11) | collective-permute-done | bytes 213024 | tf_op jit(solution)/shard_map/ppermute | solution.py:26
  34.5 7.2 %collective-permute-start.12 = (bf16[16,3328]{1,0:T(8,128)(2,1)S(1)}, bf16[16,3328]{1,0:T(8,128)(2,1)S(1)}, u32[]{:S(2)}, u32[]{:S(2)}) collective-permute-start(bf16[16,3328]{1,0:T(8,128)(2,1)S(1)} %get-tuple-element.45), channel_id=1, source_target_pairs={{0,128},{8,136},{16,144},{24,152},{32,160},{40,168},{48,176},{56,1... | collective-permute-start | bytes 319496 | tf_op jit(solution)/shard_map/ppermute | solution.py:26
  41.7 0.1 shard_map.83
  41.8 3.0 %collective-permute-start.9 = (bf16[16,3328]{1,0:T(8,128)(2,1)S(1)}, bf16[16,3328]{1,0:T(8,128)(2,1)S(1)}, u32[]{:S(2)}, u32[]{:S(2)}) collective-permute-start(bf16[16,3328]{1,0:T(8,128)(2,1)S(1)} %get-tuple-element.43), channel_id=1, source_target_pairs={{0,64},{8,72},{16,80},{24,88},{32,96},{40,104},{48,112},{56,120},{... | collective-permute-start | bytes 319496 | tf_op jit(solution)/shard_map/ppermute | solution.py:26
  44.8 0.7 collective-permute-done.12.two
  45.5 4.5 %collective-permute-done.13.three = bf16[16,3328]{1,0:T(8,128)(2,1)S(1)} collective-permute-done((bf16[16,3328]{1,0:T(8,128)(2,1)S(1)}, bf16[16,3328]{1,0:T(8,128)(2,1)S(1)}, u32[]{:S(2)}, u32[]{:S(2)}) %collective-permute-start.13) | collective-permute-done | bytes 106528 | tf_op jit(solution)/shard_map/ppermute | solution.py:26
  50.1 4.5 %collective-permute-start.15 = (bf16[8,3328]{1,0:T(8,128)(2,1)S(1)}, bf16[8,3328]{1,0:T(8,128)(2,1)S(1)}, u32[]{:S(2)}, u32[]{:S(2)}) collective-permute-start(bf16[8,3328]{1,0:T(8,128)(2,1)S(1)} %shard_map.85.a), channel_id=1, source_target_pairs={{0,128},{8,136},{16,144},{24,152},{32,160},{40,168},{48,176},{56,1... | collective-permute-start | bytes 159752 | tf_op jit(solution)/shard_map/ppermute | solution.py:26
  54.6 1.0 %collective-permute-start.16 = (bf16[8,3328]{1,0:T(8,128)(2,1)S(1)}, bf16[8,3328]{1,0:T(8,128)(2,1)S(1)}, u32[]{:S(2)}, u32[]{:S(2)}) collective-permute-start(bf16[8,3328]{1,0:T(8,128)(2,1)S(1)} %shard_map.85.a), channel_id=1, source_target_pairs={{0,64},{8,72},{16,80},{24,88},{32,96},{40,104},{48,112},{56,120},{... | collective-permute-start | bytes 159752 | tf_op jit(solution)/shard_map/ppermute | solution.py:26
  55.6 3.1 %collective-permute-start.14 = (bf16[8,3328]{1,0:T(8,128)(2,1)S(1)}, bf16[8,3328]{1,0:T(8,128)(2,1)S(1)}, u32[]{:S(2)}, u32[]{:S(2)}) collective-permute-start(bf16[8,3328]{1,0:T(8,128)(2,1)S(1)} %shard_map.85.a), channel_id=1, source_target_pairs={{0,192},{8,200},{16,208},{24,216},{32,224},{40,232},{48,240},{56,2... | collective-permute-start | bytes 159752 | tf_op jit(solution)/shard_map/ppermute | solution.py:26
  58.7 2.3 %collective-permute-done.16.d = bf16[8,3328]{1,0:T(8,128)(2,1)S(1)} collective-permute-done((bf16[8,3328]{1,0:T(8,128)(2,1)S(1)}, bf16[8,3328]{1,0:T(8,128)(2,1)S(1)}, u32[]{:S(2)}, u32[]{:S(2)}) %collective-permute-start.16) | collective-permute-done | bytes 53280 | tf_op jit(solution)/shard_map/ppermute | solution.py:26
  61.1 0.7 collective-permute-done.14.b
  61.7 1.6 %collective-permute-start.19 = (bf16[32,3328]{1,0:T(8,128)(2,1)S(1)}, bf16[32,3328]{1,0:T(8,128)(2,1)S(1)}, u32[]{:S(2)}, u32[]{:S(2)}) collective-permute-start(bf16[32,3328]{1,0:T(8,128)(2,1)S(1)} %shard_map.86.refs_0_), channel_id=1, source_target_pairs={{0,16},{8,24},{16,32},{24,40},{32,48},{40,56},{48,0},{56,8},{64,80... | collective-permute-start | bytes 638984 | tf_op jit(solution)/shard_map/ppermute | solution.py:26
  63.4 2.2 %collective-permute-start.18 = (bf16[32,3328]{1,0:T(8,128)(2,1)S(1)}, bf16[32,3328]{1,0:T(8,128)(2,1)S(1)}, u32[]{:S(2)}, u32[]{:S(2)}) collective-permute-start(bf16[32,3328]{1,0:T(8,128)(2,1)S(1)} %shard_map.86.refs_0_), channel_id=1, source_target_pairs={{0,32},{8,40},{16,48},{24,56},{32,0},{40,8},{48,16},{56,24},{64,96... | collective-permute-start | bytes 638984 | tf_op jit(solution)/shard_map/ppermute | solution.py:26
  65.5 2.5 %collective-permute-start.17 = (bf16[32,3328]{1,0:T(8,128)(2,1)S(1)}, bf16[32,3328]{1,0:T(8,128)(2,1)S(1)}, u32[]{:S(2)}, u32[]{:S(2)}) collective-permute-start(bf16[32,3328]{1,0:T(8,128)(2,1)S(1)} %shard_map.86.refs_0_), channel_id=1, source_target_pairs={{0,48},{8,56},{16,0},{24,8},{32,16},{40,24},{48,32},{56,40},{64,11... | collective-permute-start | bytes 638984 | tf_op jit(solution)/shard_map/ppermute | solution.py:26
  68.1 1.1 %collective-permute-done.19.refs_3_ = bf16[32,3328]{1,0:T(8,128)(2,1)S(1)} collective-permute-done((bf16[32,3328]{1,0:T(8,128)(2,1)S(1)}, bf16[32,3328]{1,0:T(8,128)(2,1)S(1)}, u32[]{:S(2)}, u32[]{:S(2)}) %collective-permute-start.19) | collective-permute-done | bytes 213024 | tf_op jit(solution)/shard_map/ppermute | solution.py:26
  69.2 2.5 %collective-permute-done.18.refs_2_ = bf16[32,3328]{1,0:T(8,128)(2,1)S(1)} collective-permute-done((bf16[32,3328]{1,0:T(8,128)(2,1)S(1)}, bf16[32,3328]{1,0:T(8,128)(2,1)S(1)}, u32[]{:S(2)}, u32[]{:S(2)}) %collective-permute-start.18) | collective-permute-done | bytes 213024 | tf_op jit(solution)/shard_map/ppermute | solution.py:26
  71.7 2.2 %collective-permute-done.17.refs_1_ = bf16[32,3328]{1,0:T(8,128)(2,1)S(1)} collective-permute-done((bf16[32,3328]{1,0:T(8,128)(2,1)S(1)}, bf16[32,3328]{1,0:T(8,128)(2,1)S(1)}, u32[]{:S(2)}, u32[]{:S(2)}) %collective-permute-start.17) | collective-permute-done | bytes 213024 | tf_op jit(solution)/shard_map/ppermute | solution.py:26
  73.9 0.6 shard_map.87.mine
  74.5 0.8 collective-permute-done.21.refs_1_
  75.3 0.6 shard_map.88
  76.0 1.7 %collective-permute-start.25 = (bf16[64,512]{1,0:T(8,128)(2,1)S(1)}, bf16[64,512]{1,0:T(8,128)(2,1)S(1)}, u32[]{:S(2)}, u32[]{:S(2)}) collective-permute-start(bf16[64,512]{1,0:T(8,128)(2,1)S(1)} %get-tuple-element.51), channel_id=1, source_target_pairs={{0,2},{1,3},{2,0},{3,1},{4,6},{5,7},{6,4},{7,5},{8,10},{9,11},{10,... | collective-permute-start | bytes 196616 | tf_op jit(solution)/shard_map/ppermute | solution.py:34
  77.7 0.5 collective-permute-start.24
  78.2 1.5 %collective-permute-start.26 = (bf16[64,512]{1,0:T(8,128)(2,1)S(1)}, bf16[64,512]{1,0:T(8,128)(2,1)S(1)}, u32[]{:S(2)}, u32[]{:S(2)}) collective-permute-start(bf16[64,512]{1,0:T(8,128)(2,1)S(1)} %get-tuple-element.53), channel_id=1, source_target_pairs={{0,1},{1,2},{2,3},{3,0},{4,5},{5,6},{6,7},{7,4},{8,9},{9,10},{10,1... | collective-permute-start | bytes 196616 | tf_op jit(solution)/shard_map/ppermute | solution.py:34
  79.7 2.2 %collective-permute-done.25.two = bf16[64,512]{1,0:T(8,128)(2,1)S(1)} collective-permute-done((bf16[64,512]{1,0:T(8,128)(2,1)S(1)}, bf16[64,512]{1,0:T(8,128)(2,1)S(1)}, u32[]{:S(2)}, u32[]{:S(2)}) %collective-permute-start.25) | collective-permute-done | bytes 65568 | tf_op jit(solution)/shard_map/ppermute | solution.py:34
  82.0 1.7 %collective-permute-done.26.three = bf16[64,512]{1,0:T(8,128)(2,1)S(1)} collective-permute-done((bf16[64,512]{1,0:T(8,128)(2,1)S(1)}, bf16[64,512]{1,0:T(8,128)(2,1)S(1)}, u32[]{:S(2)}, u32[]{:S(2)}) %collective-permute-start.26) | collective-permute-done | bytes 65568 | tf_op jit(solution)/shard_map/ppermute | solution.py:34
  83.7 1.7 %collective-permute-start.27 = (bf16[32,512]{1,0:T(8,128)(2,1)S(1)}, bf16[32,512]{1,0:T(8,128)(2,1)S(1)}, u32[]{:S(2)}, u32[]{:S(2)}) collective-permute-start(bf16[32,512]{1,0:T(8,128)(2,1)S(1)} %get-tuple-element.56), channel_id=1, source_target_pairs={{0,4},{1,5},{2,6},{3,7},{4,0},{5,1},{6,2},{7,3},{8,12},{9,13},{10,... | collective-permute-start | bytes 98312 | tf_op jit(solution)/shard_map/ppermute | solution.py:34
  85.4 2.3 %collective-permute-done.27 = bf16[32,512]{1,0:T(8,128)(2,1)S(1)} collective-permute-done((bf16[32,512]{1,0:T(8,128)(2,1)S(1)}, bf16[32,512]{1,0:T(8,128)(2,1)S(1)}, u32[]{:S(2)}, u32[]{:S(2)}) %collective-permute-start.27) | collective-permute-done | bytes 32800 | tf_op jit(solution)/shard_map/ppermute | solution.py:34
  87.7 0.6 add_convert_fusion
  (28 shorter events, 0.6 us)
Async XLA Ops:
  0.0 4.1 %collective-permute-start = (bf16[32,512]{1,0:T(8,128)(2,1)}, bf16[32,512]{1,0:T(8,128)(2,1)S(1)}, u32[]{:S(2)}, u32[]{:S(2)}) collective-permute-start(bf16[32,512]{1,0:T(8,128)(2,1)} %refs_0_.2), channel_id=1, source_target_pairs={{0,4},{1,5},{2,6},{3,7},{4,0},{5,1},{6,2},{7,3},{8,12},{9,13},{10,... | collective-permute-start | bytes 98312 | tf_op jit(solution)/shard_map/ppermute | solution.py:34
  2.0 2.2 %copy-start = (bf16[32,512]{1,0:T(8,128)(2,1)S(1)}, bf16[32,512]{1,0:T(8,128)(2,1)}, u32[]{:S(2)}) copy-start(bf16[32,512]{1,0:T(8,128)(2,1)} %refs_0_.2) | copy-start | bytes 98308
  4.2 6.7 %collective-permute-start.3 = (bf16[64,512]{1,0:T(8,128)(2,1)S(1)}, bf16[64,512]{1,0:T(8,128)(2,1)S(1)}, u32[]{:S(2)}, u32[]{:S(2)}) collective-permute-start(bf16[64,512]{1,0:T(8,128)(2,1)S(1)} %shard_map.73.refs_0_), channel_id=1, source_target_pairs={{0,3},{1,0},{2,1},{3,2},{4,7},{5,4},{6,5},{7,6},{8,11},{9,8},{10,9... | collective-permute-start | bytes 196616 | tf_op jit(solution)/shard_map/ppermute | solution.py:34
  7.0 5.8 %collective-permute-start.2 = (bf16[64,512]{1,0:T(8,128)(2,1)S(1)}, bf16[64,512]{1,0:T(8,128)(2,1)S(1)}, u32[]{:S(2)}, u32[]{:S(2)}) collective-permute-start(bf16[64,512]{1,0:T(8,128)(2,1)S(1)} %shard_map.73.refs_0_), channel_id=1, source_target_pairs={{0,2},{1,3},{2,0},{3,1},{4,6},{5,7},{6,4},{7,5},{8,10},{9,11},{10,... | collective-permute-start | bytes 196616 | tf_op jit(solution)/shard_map/ppermute | solution.py:34
  7.8 5.7 %collective-permute-start.1 = (bf16[64,512]{1,0:T(8,128)(2,1)S(1)}, bf16[64,512]{1,0:T(8,128)(2,1)S(1)}, u32[]{:S(2)}, u32[]{:S(2)}) collective-permute-start(bf16[64,512]{1,0:T(8,128)(2,1)S(1)} %shard_map.73.refs_0_), channel_id=1, source_target_pairs={{0,1},{1,2},{2,3},{3,0},{4,5},{5,6},{6,7},{7,4},{8,9},{9,10},{10,1... | collective-permute-start | bytes 196616 | tf_op jit(solution)/shard_map/ppermute | solution.py:34
  14.7 3.7 %collective-permute-start.4 = (bf16[128,6656]{1,0:T(8,128)(2,1)S(1)}, bf16[128,6656]{1,0:T(8,128)(2,1)S(1)}, u32[]{:S(2)}, u32[]{:S(2)}) collective-permute-start(bf16[128,6656]{1,0:T(8,128)(2,1)S(1)} %get-tuple-element.35), channel_id=1, source_target_pairs={{0,8},{8,0},{16,24},{24,16},{32,40},{40,32},{48,56},{56,48},{64,72... | collective-permute-start | bytes 5111816 | tf_op jit(solution)/shard_map/ppermute | solution.py:26
  18.6 7.4 %collective-permute-start.6 = (bf16[16,6656]{1,0:T(8,128)(2,1)S(1)}, bf16[16,6656]{1,0:T(8,128)(2,1)S(1)}, u32[]{:S(2)}, u32[]{:S(2)}) collective-permute-start(bf16[16,6656]{1,0:T(8,128)(2,1)S(1)} %get-tuple-element.37), channel_id=1, source_target_pairs={{0,48},{8,56},{16,0},{24,8},{32,16},{40,24},{48,32},{56,40},{64,11... | collective-permute-start | bytes 638984 | tf_op jit(solution)/shard_map/ppermute | solution.py:26
  19.1 11.7 %collective-permute-start.5 = (bf16[16,6656]{1,0:T(8,128)(2,1)S(1)}, bf16[16,6656]{1,0:T(8,128)(2,1)S(1)}, u32[]{:S(2)}, u32[]{:S(2)}) collective-permute-start(bf16[16,6656]{1,0:T(8,128)(2,1)S(1)} %get-tuple-element.36), channel_id=1, source_target_pairs={{0,16},{8,24},{16,32},{24,40},{32,48},{40,56},{48,0},{56,8},{64,80... | collective-permute-start | bytes 638984 | tf_op jit(solution)/shard_map/ppermute | solution.py:26
  20.7 12.6 %collective-permute-start.10 = (bf16[16,6656]{1,0:T(8,128)(2,1)S(1)}, bf16[16,6656]{1,0:T(8,128)(2,1)S(1)}, u32[]{:S(2)}, u32[]{:S(2)}) collective-permute-start(bf16[16,6656]{1,0:T(8,128)(2,1)S(1)} %get-tuple-element.44), channel_id=1, source_target_pairs={{0,16},{8,24},{16,32},{24,40},{32,48},{40,56},{48,0},{56,8},{64,80... | collective-permute-start | bytes 638984 | tf_op jit(solution)/shard_map/ppermute | solution.py:26
  26.1 8.3 %collective-permute-start.11 = (bf16[16,6656]{1,0:T(8,128)(2,1)S(1)}, bf16[16,6656]{1,0:T(8,128)(2,1)S(1)}, u32[]{:S(2)}, u32[]{:S(2)}) collective-permute-start(bf16[16,6656]{1,0:T(8,128)(2,1)S(1)} %shard_map.80), channel_id=1, source_target_pairs={{0,48},{8,56},{16,0},{24,8},{32,16},{40,24},{48,32},{56,40},{64,11... | collective-permute-start | bytes 638984 | tf_op jit(solution)/shard_map/ppermute | solution.py:26
  27.1 14.6 %collective-permute-start.7 = (bf16[16,6656]{1,0:T(8,128)(2,1)S(1)}, bf16[16,6656]{1,0:T(8,128)(2,1)S(1)}, u32[]{:S(2)}, u32[]{:S(2)}) collective-permute-start(bf16[16,6656]{1,0:T(8,128)(2,1)S(1)} %get-tuple-element.41), channel_id=1, source_target_pairs={{0,48},{8,56},{16,0},{24,8},{32,16},{40,24},{48,32},{56,40},{64,11... | collective-permute-start | bytes 638984 | tf_op jit(solution)/shard_map/ppermute | solution.py:26
  30.9 10.8 %collective-permute-start.8 = (bf16[16,6656]{1,0:T(8,128)(2,1)S(1)}, bf16[16,6656]{1,0:T(8,128)(2,1)S(1)}, u32[]{:S(2)}, u32[]{:S(2)}) collective-permute-start(bf16[16,6656]{1,0:T(8,128)(2,1)S(1)} %shard_map.81), channel_id=1, source_target_pairs={{0,16},{8,24},{16,32},{24,40},{32,48},{40,56},{48,0},{56,8},{64,80... | collective-permute-start | bytes 638984 | tf_op jit(solution)/shard_map/ppermute | solution.py:26
  34.5 11.0 %collective-permute-start.12 = (bf16[16,3328]{1,0:T(8,128)(2,1)S(1)}, bf16[16,3328]{1,0:T(8,128)(2,1)S(1)}, u32[]{:S(2)}, u32[]{:S(2)}) collective-permute-start(bf16[16,3328]{1,0:T(8,128)(2,1)S(1)} %get-tuple-element.45), channel_id=1, source_target_pairs={{0,128},{8,136},{16,144},{24,152},{32,160},{40,168},{48,176},{56,1... | collective-permute-start | bytes 319496 | tf_op jit(solution)/shard_map/ppermute | solution.py:26
  41.7 8.3 %collective-permute-start.13 = (bf16[16,3328]{1,0:T(8,128)(2,1)S(1)}, bf16[16,3328]{1,0:T(8,128)(2,1)S(1)}, u32[]{:S(2)}, u32[]{:S(2)}) collective-permute-start(bf16[16,3328]{1,0:T(8,128)(2,1)S(1)} %get-tuple-element.46), channel_id=1, source_target_pairs={{0,192},{8,200},{16,208},{24,216},{32,224},{40,232},{48,240},{56,2... | collective-permute-start | bytes 319496 | tf_op jit(solution)/shard_map/ppermute | solution.py:26
  41.8 8.2 %collective-permute-start.9 = (bf16[16,3328]{1,0:T(8,128)(2,1)S(1)}, bf16[16,3328]{1,0:T(8,128)(2,1)S(1)}, u32[]{:S(2)}, u32[]{:S(2)}) collective-permute-start(bf16[16,3328]{1,0:T(8,128)(2,1)S(1)} %get-tuple-element.43), channel_id=1, source_target_pairs={{0,64},{8,72},{16,80},{24,88},{32,96},{40,104},{48,112},{56,120},{... | collective-permute-start | bytes 319496 | tf_op jit(solution)/shard_map/ppermute | solution.py:26
  50.1 8.7 %collective-permute-start.15 = (bf16[8,3328]{1,0:T(8,128)(2,1)S(1)}, bf16[8,3328]{1,0:T(8,128)(2,1)S(1)}, u32[]{:S(2)}, u32[]{:S(2)}) collective-permute-start(bf16[8,3328]{1,0:T(8,128)(2,1)S(1)} %shard_map.85.a), channel_id=1, source_target_pairs={{0,128},{8,136},{16,144},{24,152},{32,160},{40,168},{48,176},{56,1... | collective-permute-start | bytes 159752 | tf_op jit(solution)/shard_map/ppermute | solution.py:26
  54.6 6.5 %collective-permute-start.16 = (bf16[8,3328]{1,0:T(8,128)(2,1)S(1)}, bf16[8,3328]{1,0:T(8,128)(2,1)S(1)}, u32[]{:S(2)}, u32[]{:S(2)}) collective-permute-start(bf16[8,3328]{1,0:T(8,128)(2,1)S(1)} %shard_map.85.a), channel_id=1, source_target_pairs={{0,64},{8,72},{16,80},{24,88},{32,96},{40,104},{48,112},{56,120},{... | collective-permute-start | bytes 159752 | tf_op jit(solution)/shard_map/ppermute | solution.py:26
  55.6 6.1 %collective-permute-start.14 = (bf16[8,3328]{1,0:T(8,128)(2,1)S(1)}, bf16[8,3328]{1,0:T(8,128)(2,1)S(1)}, u32[]{:S(2)}, u32[]{:S(2)}) collective-permute-start(bf16[8,3328]{1,0:T(8,128)(2,1)S(1)} %shard_map.85.a), channel_id=1, source_target_pairs={{0,192},{8,200},{16,208},{24,216},{32,224},{40,232},{48,240},{56,2... | collective-permute-start | bytes 159752 | tf_op jit(solution)/shard_map/ppermute | solution.py:26
  61.7 7.4 %collective-permute-start.19 = (bf16[32,3328]{1,0:T(8,128)(2,1)S(1)}, bf16[32,3328]{1,0:T(8,128)(2,1)S(1)}, u32[]{:S(2)}, u32[]{:S(2)}) collective-permute-start(bf16[32,3328]{1,0:T(8,128)(2,1)S(1)} %shard_map.86.refs_0_), channel_id=1, source_target_pairs={{0,16},{8,24},{16,32},{24,40},{32,48},{40,56},{48,0},{56,8},{64,80... | collective-permute-start | bytes 638984 | tf_op jit(solution)/shard_map/ppermute | solution.py:26
  63.4 8.3 %collective-permute-start.18 = (bf16[32,3328]{1,0:T(8,128)(2,1)S(1)}, bf16[32,3328]{1,0:T(8,128)(2,1)S(1)}, u32[]{:S(2)}, u32[]{:S(2)}) collective-permute-start(bf16[32,3328]{1,0:T(8,128)(2,1)S(1)} %shard_map.86.refs_0_), channel_id=1, source_target_pairs={{0,32},{8,40},{16,48},{24,56},{32,0},{40,8},{48,16},{56,24},{64,96... | collective-permute-start | bytes 638984 | tf_op jit(solution)/shard_map/ppermute | solution.py:26
  65.5 8.3 %collective-permute-start.17 = (bf16[32,3328]{1,0:T(8,128)(2,1)S(1)}, bf16[32,3328]{1,0:T(8,128)(2,1)S(1)}, u32[]{:S(2)}, u32[]{:S(2)}) collective-permute-start(bf16[32,3328]{1,0:T(8,128)(2,1)S(1)} %shard_map.86.refs_0_), channel_id=1, source_target_pairs={{0,48},{8,56},{16,0},{24,8},{32,16},{40,24},{48,32},{56,40},{64,11... | collective-permute-start | bytes 638984 | tf_op jit(solution)/shard_map/ppermute | solution.py:26
  68.1 6.4 %collective-permute-start.20 = (bf16[32,3328]{1,0:T(8,128)(2,1)S(1)}, bf16[32,3328]{1,0:T(8,128)(2,1)S(1)}, u32[]{:S(2)}, u32[]{:S(2)}) collective-permute-start(bf16[32,3328]{1,0:T(8,128)(2,1)S(1)} %shard_map.86.refs_0_), channel_id=1, source_target_pairs={{0,8},{8,0},{16,24},{24,16},{32,40},{40,32},{48,56},{56,48},{64,72... | collective-permute-start | bytes 638984 | tf_op jit(solution)/shard_map/ppermute | solution.py:26
  69.2 5.3 %collective-permute-start.23 = (bf16[32,3328]{1,0:T(8,128)(2,1)S(1)}, bf16[32,3328]{1,0:T(8,128)(2,1)S(1)}, u32[]{:S(2)}, u32[]{:S(2)}) collective-permute-start(bf16[32,3328]{1,0:T(8,128)(2,1)S(1)} %collective-permute-done.19.refs_3_), channel_id=1, source_target_pairs={{0,8},{8,0},{16,24},{24,16},{32,40},{40,32},{48,56},{56,48},{64,72... | collective-permute-start | bytes 638984 | tf_op jit(solution)/shard_map/ppermute | solution.py:26
  71.7 2.8 %collective-permute-start.22 = (bf16[32,3328]{1,0:T(8,128)(2,1)S(1)}, bf16[32,3328]{1,0:T(8,128)(2,1)S(1)}, u32[]{:S(2)}, u32[]{:S(2)}) collective-permute-start(bf16[32,3328]{1,0:T(8,128)(2,1)S(1)} %collective-permute-done.18.refs_2_), channel_id=1, source_target_pairs={{0,8},{8,0},{16,24},{24,16},{32,40},{40,32},{48,56},{56,48},{64,72... | collective-permute-start | bytes 638984 | tf_op jit(solution)/shard_map/ppermute | solution.py:26
  73.9 1.5 %collective-permute-start.21 = (bf16[32,3328]{1,0:T(8,128)(2,1)S(1)}, bf16[32,3328]{1,0:T(8,128)(2,1)S(1)}, u32[]{:S(2)}, u32[]{:S(2)}) collective-permute-start(bf16[32,3328]{1,0:T(8,128)(2,1)S(1)} %collective-permute-done.17.refs_1_), channel_id=1, source_target_pairs={{0,8},{8,0},{16,24},{24,16},{32,40},{40,32},{48,56},{56,48},{64,72... | collective-permute-start | bytes 638984 | tf_op jit(solution)/shard_map/ppermute | solution.py:26
  76.0 6.0 %collective-permute-start.25 = (bf16[64,512]{1,0:T(8,128)(2,1)S(1)}, bf16[64,512]{1,0:T(8,128)(2,1)S(1)}, u32[]{:S(2)}, u32[]{:S(2)}) collective-permute-start(bf16[64,512]{1,0:T(8,128)(2,1)S(1)} %get-tuple-element.51), channel_id=1, source_target_pairs={{0,2},{1,3},{2,0},{3,1},{4,6},{5,7},{6,4},{7,5},{8,10},{9,11},{10,... | collective-permute-start | bytes 196616 | tf_op jit(solution)/shard_map/ppermute | solution.py:34
  77.7 4.3 %collective-permute-start.24 = (bf16[64,512]{1,0:T(8,128)(2,1)S(1)}, bf16[64,512]{1,0:T(8,128)(2,1)S(1)}, u32[]{:S(2)}, u32[]{:S(2)}) collective-permute-start(bf16[64,512]{1,0:T(8,128)(2,1)S(1)} %get-tuple-element.50), channel_id=1, source_target_pairs={{0,3},{1,0},{2,1},{3,2},{4,7},{5,4},{6,5},{7,6},{8,11},{9,8},{10,9... | collective-permute-start | bytes 196616 | tf_op jit(solution)/shard_map/ppermute | solution.py:34
  78.2 5.5 %collective-permute-start.26 = (bf16[64,512]{1,0:T(8,128)(2,1)S(1)}, bf16[64,512]{1,0:T(8,128)(2,1)S(1)}, u32[]{:S(2)}, u32[]{:S(2)}) collective-permute-start(bf16[64,512]{1,0:T(8,128)(2,1)S(1)} %get-tuple-element.53), channel_id=1, source_target_pairs={{0,1},{1,2},{2,3},{3,0},{4,5},{5,6},{6,7},{7,4},{8,9},{9,10},{10,1... | collective-permute-start | bytes 196616 | tf_op jit(solution)/shard_map/ppermute | solution.py:34
  83.7 4.0 %collective-permute-start.27 = (bf16[32,512]{1,0:T(8,128)(2,1)S(1)}, bf16[32,512]{1,0:T(8,128)(2,1)S(1)}, u32[]{:S(2)}, u32[]{:S(2)}) collective-permute-start(bf16[32,512]{1,0:T(8,128)(2,1)S(1)} %get-tuple-element.56), channel_id=1, source_target_pairs={{0,4},{1,5},{2,6},{3,7},{4,0},{5,1},{6,2},{7,3},{8,12},{9,13},{10,... | collective-permute-start | bytes 98312 | tf_op jit(solution)/shard_map/ppermute | solution.py:34

commit v6 on v4

--- a/solution.py
+++ b/solution.py
@@ -222,6 +222,10 @@
         hidden[:, cols] = (jax.nn.silu(total[:ROWS]) * total[ROWS:]).astype(BF16)
 
 
+def corner_kernel(x, out):
+    out[...] = x[: out.shape[0], : out.shape[1]]
+
+
 def rows_kernel(a, b, c, d, out):
     for i, pair in ((0, (a, b)), (2, (c, d))):
         for cols in columns(out.shape[1], 2 * BLOCK):
@@ -341,6 +345,8 @@
     two, one, three = move_gx(hidden, dz=-2), move_gx(hidden, dz=-1), move_gx(hidden, dz=-3)
     (hidden,) = local_call(rows_kernel, [((NZ * ROWS, units), BF16)], hidden, one, two, three)
     two, one, three = move_gx(hidden, dy=-2), move_gx(hidden, dy=-1), move_gx(hidden, dy=-3)
+    (corner,) = local_call(corner_kernel, [((8, BLOCK), BF16)], two)
+    one, three = after(one, corner), after(three, corner)
     mine = [hidden, one, two, three]
     theirs = [move_gx(hidden, dc=1)]
     theirs += [move_gx(block, dc=1) for block in mine[1:]]

time: 88.7 us -> 88.6 us (level)
  transfers between devices with their start and end apart: 28 -> 28, of which waited for: 17 -> 18; matrix products, arithmetic and copies ran while one was open for 0% -> 0% of each run, Pallas kernels for 10% -> 10%
where the time goes in v6:
time: 88.6 us; the launch traced here: 88.5 us
  starting transfers between devices  44.4 us (50%)
  waiting for transfers between devices  32.6 us (37%)
  Pallas kernels  10.7 us (12%)
    ppermute x20, starting transfers between devices, move_gx(): return lax.ppermute(x, 'gx', pairs)  33.5 us
    ppermute x20, waiting for transfers between devices, move_gx(): return lax.ppermute(x, 'gx', pairs)  22.9 us
    ppermute x8, starting transfers between devices, move_gy(): return lax.ppermute(x, 'gy', pairs)  10.8 us
    ppermute x8, waiting for transfers between devices, move_gy(): return lax.ppermute(x, 'gy', pairs)  9.72 us
    pallas_call x3, Pallas kernels, weights(): pl.pallas_call(lambda *refs: weights_kernel(steps, flipped, *refs), in_sp...  6.36 us
    pallas_call x14, Pallas kernels, local_call(): pl.pallas_call(kernel, in_specs=[VMEM] * len(arrays), out_specs=[VMEM] *...  4.32 us
  transfers between devices with their start and end apart: 28, of which 18 were waited for; matrix products, arithmetic and copies ran while one was open for 0% of the time, Pallas kernels for 10%

profile of v6, /device:TPU:8, one launch (start us, length us, event | category | flops | bytes accessed | tf_op | source)
XLA Modules:
  0.0 88.5 jit_solution(10295202447513027141)
XLA Ops:
  0.0 1.9 %collective-permute-start = (bf16[32,512]{1,0:T(8,128)(2,1)}, bf16[32,512]{1,0:T(8,128)(2,1)S(1)}, u32[]{:S(2)}, u32[]{:S(2)}) collective-permute-start(bf16[32,512]{1,0:T(8,128)(2,1)} %refs_0_.2), channel_id=1, source_target_pairs={{0,4},{1,5},{2,6},{3,7},{4,0},{5,1},{6,2},{7,3},{8,12},{9,13},{10,... | collective-permute-start | bytes 98312 | tf_op jit(solution)/shard_map/ppermute | solution.py:34
  2.0 2.1 %shard_map.74.refs_5_.gate = bf16[512,3328]{1,0:T(8,128)(2,1)S(1)} custom-call(bf16[512,3328]{1,0:T(8,128)(2,1)} %refs_0_.3, f32[4,26]{1,0:T(4,128)} %refs_1_.2), custom_call_target="tpu_custom_call" | custom-call | flops 1703936 | bytes 6815744 | tf_op jit(solution)/shard_map/pallas_call | solution.py:89
  4.2 2.8 %collective-permute-start.3 = (bf16[64,512]{1,0:T(8,128)(2,1)S(1)}, bf16[64,512]{1,0:T(8,128)(2,1)S(1)}, u32[]{:S(2)}, u32[]{:S(2)}) collective-permute-start(bf16[64,512]{1,0:T(8,128)(2,1)S(1)} %shard_map.73.refs_0_), channel_id=1, source_target_pairs={{0,3},{1,0},{2,1},{3,2},{4,7},{5,4},{6,5},{7,6},{8,11},{9,8},{10,9... | collective-permute-start | bytes 196616 | tf_op jit(solution)/shard_map/ppermute | solution.py:34
  7.0 0.8 collective-permute-start.2
  7.8 0.9 %collective-permute-start.1 = (bf16[64,512]{1,0:T(8,128)(2,1)S(1)}, bf16[64,512]{1,0:T(8,128)(2,1)S(1)}, u32[]{:S(2)}, u32[]{:S(2)}) collective-permute-start(bf16[64,512]{1,0:T(8,128)(2,1)S(1)} %shard_map.73.refs_0_), channel_id=1, source_target_pairs={{0,1},{1,2},{2,3},{3,0},{4,5},{5,6},{6,7},{7,4},{8,9},{9,10},{10,1... | collective-permute-start | bytes 196616 | tf_op jit(solution)/shard_map/ppermute | solution.py:34
  8.7 2.1 %shard_map.76.refs_6_.up = bf16[512,3328]{1,0:T(8,128)(2,1)S(1)} custom-call(bf16[512,3328]{1,0:T(8,128)(2,1)} %refs_0_.4, f32[4,26]{1,0:T(4,128)} %refs_1_.3), custom_call_target="tpu_custom_call" | custom-call | flops 1703936 | bytes 6815744 | tf_op jit(solution)/shard_map/pallas_call | solution.py:89
  10.8 1.9 %collective-permute-done.2.refs_2_ = bf16[64,512]{1,0:T(8,128)(2,1)S(1)} collective-permute-done((bf16[64,512]{1,0:T(8,128)(2,1)S(1)}, bf16[64,512]{1,0:T(8,128)(2,1)S(1)}, u32[]{:S(2)}, u32[]{:S(2)}) %collective-permute-start.2) | collective-permute-done | bytes 65568 | tf_op jit(solution)/shard_map/ppermute | solution.py:34
  12.8 0.7 collective-permute-done.1.refs_1_
  13.5 1.2 %shard_map.77 = (bf16[128,512]{1,0:T(8,128)(2,1)S(1)}, bf16[128,6656]{1,0:T(8,128)(2,1)S(1)}) custom-call(bf16[64,512]{1,0:T(8,128)(2,1)S(1)} %shard_map.73.refs_0_, bf16[64,512]{1,0:T(8,128)(2,1)S(1)} %collective-permute-done.1.refs_1_, bf16[64,512]{1,0:T(8,128)(2,1)S(1)} %collective-permute-done.2.refs_2_, ...), custom_call_target="tpu_custom_call" | custom-call | flops 872415232 | bytes 7208960 | tf_op jit(solution)/shard_map/pallas_call | solution.py:47
  14.8 1.1 %shard_map.78.kept.refs_0_ = f32[128,6656]{1,0:T(8,128)S(1)} custom-call(bf16[128,512]{1,0:T(8,128)(2,1)S(1)} %get-tuple-element.32.features, bf16[512,3328]{1,0:T(8,128)(2,1)S(1)} %shard_map.74.refs_5_.gate, bf16[512,3328]{1,0:T(8,128)(2,1)S(1)} %shard_map.76.refs_6_.up), custom_call_target="tpu_custom_call" | custom-call | flops 872415232 | bytes 6946816 | tf_op jit(solution)/shard_map/pallas_call | solution.py:47
  15.9 2.5 %collective-permute-done.4.received.refs_1_ = bf16[128,6656]{1,0:T(8,128)(2,1)S(1)} collective-permute-done((bf16[128,6656]{1,0:T(8,128)(2,1)S(1)}, bf16[128,6656]{1,0:T(8,128)(2,1)S(1)}, u32[]{:S(2)}, u32[]{:S(2)}) %collective-permute-start.4) | collective-permute-done | bytes 1703968 | tf_op jit(solution)/shard_map/ppermute | solution.py:26
  18.6 0.5 collective-permute-start.6
  19.1 1.6 %collective-permute-start.5 = (bf16[16,6656]{1,0:T(8,128)(2,1)S(1)}, bf16[16,6656]{1,0:T(8,128)(2,1)S(1)}, u32[]{:S(2)}, u32[]{:S(2)}) collective-permute-start(bf16[16,6656]{1,0:T(8,128)(2,1)S(1)} %get-tuple-element.34), channel_id=1, source_target_pairs={{0,16},{8,24},{16,32},{24,40},{32,48},{40,56},{48,0},{56,8},{64,80... | collective-permute-start | bytes 638984 | tf_op jit(solution)/shard_map/ppermute | solution.py:26
  20.7 1.6 %collective-permute-start.10 = (bf16[16,6656]{1,0:T(8,128)(2,1)S(1)}, bf16[16,6656]{1,0:T(8,128)(2,1)S(1)}, u32[]{:S(2)}, u32[]{:S(2)}) collective-permute-start(bf16[16,6656]{1,0:T(8,128)(2,1)S(1)} %get-tuple-element.42), channel_id=1, source_target_pairs={{0,16},{8,24},{16,32},{24,40},{32,48},{40,56},{48,0},{56,8},{64,80... | collective-permute-start | bytes 638984 | tf_op jit(solution)/shard_map/ppermute | solution.py:26
  22.3 3.7 %collective-permute-done.6.refs_2_ = bf16[16,6656]{1,0:T(8,128)(2,1)S(1)} collective-permute-done((bf16[16,6656]{1,0:T(8,128)(2,1)S(1)}, bf16[16,6656]{1,0:T(8,128)(2,1)S(1)}, u32[]{:S(2)}, u32[]{:S(2)}) %collective-permute-start.6) | collective-permute-done | bytes 213024 | tf_op jit(solution)/shard_map/ppermute | solution.py:26
  26.1 1.1 %collective-permute-start.11 = (bf16[16,6656]{1,0:T(8,128)(2,1)S(1)}, bf16[16,6656]{1,0:T(8,128)(2,1)S(1)}, u32[]{:S(2)}, u32[]{:S(2)}) collective-permute-start(bf16[16,6656]{1,0:T(8,128)(2,1)S(1)} %shard_map.80), channel_id=1, source_target_pairs={{0,48},{8,56},{16,0},{24,8},{32,16},{40,24},{48,32},{56,40},{64,11... | collective-permute-start | bytes 638984 | tf_op jit(solution)/shard_map/ppermute | solution.py:26
  27.1 3.7 %collective-permute-start.7 = (bf16[16,6656]{1,0:T(8,128)(2,1)S(1)}, bf16[16,6656]{1,0:T(8,128)(2,1)S(1)}, u32[]{:S(2)}, u32[]{:S(2)}) collective-permute-start(bf16[16,6656]{1,0:T(8,128)(2,1)S(1)} %get-tuple-element.39), channel_id=1, source_target_pairs={{0,48},{8,56},{16,0},{24,8},{32,16},{40,24},{48,32},{56,40},{64,11... | collective-permute-start | bytes 638984 | tf_op jit(solution)/shard_map/ppermute | solution.py:26
  30.9 0.3 collective-permute-start.8
  31.2 2.1 %shard_map.82.refs_4_ = bf16[3328,512]{1,0:T(8,128)(2,1)S(1)} custom-call(bf16[3328,512]{1,0:T(8,128)(2,1)} %refs_0_.5, f32[4,26]{1,0:T(4,128)} %bitcast.1), custom_call_target="tpu_custom_call" | custom-call | flops 1703936 | bytes 6815744 | tf_op jit(solution)/shard_map/pallas_call | solution.py:89
  33.3 1.0 %collective-permute-done.11.refs_3_ = bf16[16,6656]{1,0:T(8,128)(2,1)S(1)} collective-permute-done((bf16[16,6656]{1,0:T(8,128)(2,1)S(1)}, bf16[16,6656]{1,0:T(8,128)(2,1)S(1)}, u32[]{:S(2)}, u32[]{:S(2)}) %collective-permute-start.11) | collective-permute-done | bytes 213024 | tf_op jit(solution)/shard_map/ppermute | solution.py:26
  34.5 7.2 %collective-permute-start.12 = (bf16[16,3328]{1,0:T(8,128)(2,1)S(1)}, bf16[16,3328]{1,0:T(8,128)(2,1)S(1)}, u32[]{:S(2)}, u32[]{:S(2)}) collective-permute-start(bf16[16,3328]{1,0:T(8,128)(2,1)S(1)} %get-tuple-element.43), channel_id=1, source_target_pairs={{0,128},{8,136},{16,144},{24,152},{32,160},{40,168},{48,176},{56,1... | collective-permute-start | bytes 319496 | tf_op jit(solution)/shard_map/ppermute | solution.py:26
  41.8 3.0 %collective-permute-start.9 = (bf16[16,3328]{1,0:T(8,128)(2,1)S(1)}, bf16[16,3328]{1,0:T(8,128)(2,1)S(1)}, u32[]{:S(2)}, u32[]{:S(2)}) collective-permute-start(bf16[16,3328]{1,0:T(8,128)(2,1)S(1)} %get-tuple-element.41), channel_id=1, source_target_pairs={{0,64},{8,72},{16,80},{24,88},{32,96},{40,104},{48,112},{56,120},{... | collective-permute-start | bytes 319496 | tf_op jit(solution)/shard_map/ppermute | solution.py:26
  44.8 0.7 collective-permute-done.12.two
  45.5 4.5 %collective-permute-done.13.three = bf16[16,3328]{1,0:T(8,128)(2,1)S(1)} collective-permute-done((bf16[16,3328]{1,0:T(8,128)(2,1)S(1)}, bf16[16,3328]{1,0:T(8,128)(2,1)S(1)}, u32[]{:S(2)}, u32[]{:S(2)}) %collective-permute-start.13) | collective-permute-done | bytes 106528 | tf_op jit(solution)/shard_map/ppermute | solution.py:26
  50.1 1.5 %collective-permute-start.16 = (bf16[8,3328]{1,0:T(8,128)(2,1)S(1)}, bf16[8,3328]{1,0:T(8,128)(2,1)S(1)}, u32[]{:S(2)}, u32[]{:S(2)}) collective-permute-start(bf16[8,3328]{1,0:T(8,128)(2,1)S(1)} %shard_map.85.a), channel_id=1, source_target_pairs={{0,64},{8,72},{16,80},{24,88},{32,96},{40,104},{48,112},{56,120},{... | collective-permute-start | bytes 159752 | tf_op jit(solution)/shard_map/ppermute | solution.py:26
  51.6 4.0 %collective-permute-start.15 = (bf16[8,3328]{1,0:T(8,128)(2,1)S(1)}, bf16[8,3328]{1,0:T(8,128)(2,1)S(1)}, u32[]{:S(2)}, u32[]{:S(2)}) collective-permute-start(bf16[8,3328]{1,0:T(8,128)(2,1)S(1)} %shard_map.85.a), channel_id=1, source_target_pairs={{0,128},{8,136},{16,144},{24,152},{32,160},{40,168},{48,176},{56,1... | collective-permute-start | bytes 159752 | tf_op jit(solution)/shard_map/ppermute | solution.py:26
  55.6 3.1 %collective-permute-start.14 = (bf16[8,3328]{1,0:T(8,128)(2,1)S(1)}, bf16[8,3328]{1,0:T(8,128)(2,1)S(1)}, u32[]{:S(2)}, u32[]{:S(2)}) collective-permute-start(bf16[8,3328]{1,0:T(8,128)(2,1)S(1)} %shard_map.85.a), channel_id=1, source_target_pairs={{0,192},{8,200},{16,208},{24,216},{32,224},{40,232},{48,240},{56,2... | collective-permute-start | bytes 159752 | tf_op jit(solution)/shard_map/ppermute | solution.py:26
  58.7 2.1 %collective-permute-done.15.c = bf16[8,3328]{1,0:T(8,128)(2,1)S(1)} collective-permute-done((bf16[8,3328]{1,0:T(8,128)(2,1)S(1)}, bf16[8,3328]{1,0:T(8,128)(2,1)S(1)}, u32[]{:S(2)}, u32[]{:S(2)}) %collective-permute-start.15) | collective-permute-done | bytes 53280 | tf_op jit(solution)/shard_map/ppermute | solution.py:26
  60.8 2.0 %collective-permute-done.14.b = bf16[8,3328]{1,0:T(8,128)(2,1)S(1)} collective-permute-done((bf16[8,3328]{1,0:T(8,128)(2,1)S(1)}, bf16[8,3328]{1,0:T(8,128)(2,1)S(1)}, u32[]{:S(2)}, u32[]{:S(2)}) %collective-permute-start.14) | collective-permute-done | bytes 53280 | tf_op jit(solution)/shard_map/ppermute | solution.py:26
  62.9 3.3 %collective-permute-start.18 = (bf16[32,3328]{1,0:T(8,128)(2,1)S(1)}, bf16[32,3328]{1,0:T(8,128)(2,1)S(1)}, u32[]{:S(2)}, u32[]{:S(2)}) collective-permute-start(bf16[32,3328]{1,0:T(8,128)(2,1)S(1)} %shard_map.86.refs_0_), channel_id=1, source_target_pairs={{0,32},{8,40},{16,48},{24,56},{32,0},{40,8},{48,16},{56,24},{64,96... | collective-permute-start | bytes 638984 | tf_op jit(solution)/shard_map/ppermute | solution.py:26
  66.2 2.0 %collective-permute-start.17 = (bf16[32,3328]{1,0:T(8,128)(2,1)S(1)}, bf16[32,3328]{1,0:T(8,128)(2,1)S(1)}, u32[]{:S(2)}, u32[]{:S(2)}) collective-permute-start(bf16[32,3328]{1,0:T(8,128)(2,1)S(1)} %shard_map.86.refs_0_), channel_id=1, source_target_pairs={{0,48},{8,56},{16,0},{24,8},{32,16},{40,24},{48,32},{56,40},{64,11... | collective-permute-start | bytes 638984 | tf_op jit(solution)/shard_map/ppermute | solution.py:26
  68.2 2.7 %collective-permute-done.18.refs_2_ = bf16[32,3328]{1,0:T(8,128)(2,1)S(1)} collective-permute-done((bf16[32,3328]{1,0:T(8,128)(2,1)S(1)}, bf16[32,3328]{1,0:T(8,128)(2,1)S(1)}, u32[]{:S(2)}, u32[]{:S(2)}) %collective-permute-start.18) | collective-permute-done | bytes 213024 | tf_op jit(solution)/shard_map/ppermute | solution.py:26
  70.9 2.7 %collective-permute-done.19.refs_3_ = bf16[32,3328]{1,0:T(8,128)(2,1)S(1)} collective-permute-done((bf16[32,3328]{1,0:T(8,128)(2,1)S(1)}, bf16[32,3328]{1,0:T(8,128)(2,1)S(1)}, u32[]{:S(2)}, u32[]{:S(2)}) %collective-permute-start.19) | collective-permute-done | bytes 213024 | tf_op jit(solution)/shard_map/ppermute | solution.py:26
  73.6 0.5 collective-permute-start.22
  74.1 0.6 shard_map.87.mine
  74.8 0.3 collective-permute-done.23.refs_3_
  75.1 0.3 collective-permute-done.22.refs_2_
  75.4 0.3 collective-permute-done.21.refs_1_
  75.7 0.6 shard_map.88
  76.3 0.6 collective-permute-start.24
  77.0 0.9 collective-permute-start.25
  77.8 1.3 %collective-permute-start.26 = (bf16[64,512]{1,0:T(8,128)(2,1)S(1)}, bf16[64,512]{1,0:T(8,128)(2,1)S(1)}, u32[]{:S(2)}, u32[]{:S(2)}) collective-permute-start(bf16[64,512]{1,0:T(8,128)(2,1)S(1)} %get-tuple-element.50), channel_id=1, source_target_pairs={{0,1},{1,2},{2,3},{3,0},{4,5},{5,6},{6,7},{7,4},{8,9},{9,10},{10,1... | collective-permute-start | bytes 196616 | tf_op jit(solution)/shard_map/ppermute | solution.py:34
  79.2 2.2 %collective-permute-done.24.one = bf16[64,512]{1,0:T(8,128)(2,1)S(1)} collective-permute-done((bf16[64,512]{1,0:T(8,128)(2,1)S(1)}, bf16[64,512]{1,0:T(8,128)(2,1)S(1)}, u32[]{:S(2)}, u32[]{:S(2)}) %collective-permute-start.24) | collective-permute-done | bytes 65568 | tf_op jit(solution)/shard_map/ppermute | solution.py:34
  81.3 1.5 %collective-permute-done.25.two = bf16[64,512]{1,0:T(8,128)(2,1)S(1)} collective-permute-done((bf16[64,512]{1,0:T(8,128)(2,1)S(1)}, bf16[64,512]{1,0:T(8,128)(2,1)S(1)}, u32[]{:S(2)}, u32[]{:S(2)}) %collective-permute-start.25) | collective-permute-done | bytes 65568 | tf_op jit(solution)/shard_map/ppermute | solution.py:34
  82.8 1.0 %collective-permute-done.26.three = bf16[64,512]{1,0:T(8,128)(2,1)S(1)} collective-permute-done((bf16[64,512]{1,0:T(8,128)(2,1)S(1)}, bf16[64,512]{1,0:T(8,128)(2,1)S(1)}, u32[]{:S(2)}, u32[]{:S(2)}) %collective-permute-start.26) | collective-permute-done | bytes 65568 | tf_op jit(solution)/shard_map/ppermute | solution.py:34
  83.9 1.6 %collective-permute-start.27 = (bf16[32,512]{1,0:T(8,128)(2,1)S(1)}, bf16[32,512]{1,0:T(8,128)(2,1)S(1)}, u32[]{:S(2)}, u32[]{:S(2)}) collective-permute-start(bf16[32,512]{1,0:T(8,128)(2,1)S(1)} %get-tuple-element.52), channel_id=1, source_target_pairs={{0,4},{1,5},{2,6},{3,7},{4,0},{5,1},{6,2},{7,3},{8,12},{9,13},{10,... | collective-permute-start | bytes 98312 | tf_op jit(solution)/shard_map/ppermute | solution.py:34
  85.5 2.4 %collective-permute-done.27 = bf16[32,512]{1,0:T(8,128)(2,1)S(1)} collective-permute-done((bf16[32,512]{1,0:T(8,128)(2,1)S(1)}, bf16[32,512]{1,0:T(8,128)(2,1)S(1)}, u32[]{:S(2)}, u32[]{:S(2)}) %collective-permute-start.27) | collective-permute-done | bytes 32800 | tf_op jit(solution)/shard_map/ppermute | solution.py:34
  87.9 0.6 add_convert_fusion
  (28 shorter events, 0.9 us)
Async XLA Ops:
  0.0 4.1 %collective-permute-start = (bf16[32,512]{1,0:T(8,128)(2,1)}, bf16[32,512]{1,0:T(8,128)(2,1)S(1)}, u32[]{:S(2)}, u32[]{:S(2)}) collective-permute-start(bf16[32,512]{1,0:T(8,128)(2,1)} %refs_0_.2), channel_id=1, source_target_pairs={{0,4},{1,5},{2,6},{3,7},{4,0},{5,1},{6,2},{7,3},{8,12},{9,13},{10,... | collective-permute-start | bytes 98312 | tf_op jit(solution)/shard_map/ppermute | solution.py:34
  2.0 2.2 %copy-start = (bf16[32,512]{1,0:T(8,128)(2,1)S(1)}, bf16[32,512]{1,0:T(8,128)(2,1)}, u32[]{:S(2)}) copy-start(bf16[32,512]{1,0:T(8,128)(2,1)} %refs_0_.2) | copy-start | bytes 98308
  4.2 6.7 %collective-permute-start.3 = (bf16[64,512]{1,0:T(8,128)(2,1)S(1)}, bf16[64,512]{1,0:T(8,128)(2,1)S(1)}, u32[]{:S(2)}, u32[]{:S(2)}) collective-permute-start(bf16[64,512]{1,0:T(8,128)(2,1)S(1)} %shard_map.73.refs_0_), channel_id=1, source_target_pairs={{0,3},{1,0},{2,1},{3,2},{4,7},{5,4},{6,5},{7,6},{8,11},{9,8},{10,9... | collective-permute-start | bytes 196616 | tf_op jit(solution)/shard_map/ppermute | solution.py:34
  7.0 5.8 %collective-permute-start.2 = (bf16[64,512]{1,0:T(8,128)(2,1)S(1)}, bf16[64,512]{1,0:T(8,128)(2,1)S(1)}, u32[]{:S(2)}, u32[]{:S(2)}) collective-permute-start(bf16[64,512]{1,0:T(8,128)(2,1)S(1)} %shard_map.73.refs_0_), channel_id=1, source_target_pairs={{0,2},{1,3},{2,0},{3,1},{4,6},{5,7},{6,4},{7,5},{8,10},{9,11},{10,... | collective-permute-start | bytes 196616 | tf_op jit(solution)/shard_map/ppermute | solution.py:34
  7.8 5.7 %collective-permute-start.1 = (bf16[64,512]{1,0:T(8,128)(2,1)S(1)}, bf16[64,512]{1,0:T(8,128)(2,1)S(1)}, u32[]{:S(2)}, u32[]{:S(2)}) collective-permute-start(bf16[64,512]{1,0:T(8,128)(2,1)S(1)} %shard_map.73.refs_0_), channel_id=1, source_target_pairs={{0,1},{1,2},{2,3},{3,0},{4,5},{5,6},{6,7},{7,4},{8,9},{9,10},{10,1... | collective-permute-start | bytes 196616 | tf_op jit(solution)/shard_map/ppermute | solution.py:34
  14.7 3.7 %collective-permute-start.4 = (bf16[128,6656]{1,0:T(8,128)(2,1)S(1)}, bf16[128,6656]{1,0:T(8,128)(2,1)S(1)}, u32[]{:S(2)}, u32[]{:S(2)}) collective-permute-start(bf16[128,6656]{1,0:T(8,128)(2,1)S(1)} %get-tuple-element.33), channel_id=1, source_target_pairs={{0,8},{8,0},{16,24},{24,16},{32,40},{40,32},{48,56},{56,48},{64,72... | collective-permute-start | bytes 5111816 | tf_op jit(solution)/shard_map/ppermute | solution.py:26
  18.6 7.4 %collective-permute-start.6 = (bf16[16,6656]{1,0:T(8,128)(2,1)S(1)}, bf16[16,6656]{1,0:T(8,128)(2,1)S(1)}, u32[]{:S(2)}, u32[]{:S(2)}) collective-permute-start(bf16[16,6656]{1,0:T(8,128)(2,1)S(1)} %get-tuple-element.35), channel_id=1, source_target_pairs={{0,48},{8,56},{16,0},{24,8},{32,16},{40,24},{48,32},{56,40},{64,11... | collective-permute-start | bytes 638984 | tf_op jit(solution)/shard_map/ppermute | solution.py:26
  19.1 11.7 %collective-permute-start.5 = (bf16[16,6656]{1,0:T(8,128)(2,1)S(1)}, bf16[16,6656]{1,0:T(8,128)(2,1)S(1)}, u32[]{:S(2)}, u32[]{:S(2)}) collective-permute-start(bf16[16,6656]{1,0:T(8,128)(2,1)S(1)} %get-tuple-element.34), channel_id=1, source_target_pairs={{0,16},{8,24},{16,32},{24,40},{32,48},{40,56},{48,0},{56,8},{64,80... | collective-permute-start | bytes 638984 | tf_op jit(solution)/shard_map/ppermute | solution.py:26
  20.7 12.6 %collective-permute-start.10 = (bf16[16,6656]{1,0:T(8,128)(2,1)S(1)}, bf16[16,6656]{1,0:T(8,128)(2,1)S(1)}, u32[]{:S(2)}, u32[]{:S(2)}) collective-permute-start(bf16[16,6656]{1,0:T(8,128)(2,1)S(1)} %get-tuple-element.42), channel_id=1, source_target_pairs={{0,16},{8,24},{16,32},{24,40},{32,48},{40,56},{48,0},{56,8},{64,80... | collective-permute-start | bytes 638984 | tf_op jit(solution)/shard_map/ppermute | solution.py:26
  26.1 8.3 %collective-permute-start.11 = (bf16[16,6656]{1,0:T(8,128)(2,1)S(1)}, bf16[16,6656]{1,0:T(8,128)(2,1)S(1)}, u32[]{:S(2)}, u32[]{:S(2)}) collective-permute-start(bf16[16,6656]{1,0:T(8,128)(2,1)S(1)} %shard_map.80), channel_id=1, source_target_pairs={{0,48},{8,56},{16,0},{24,8},{32,16},{40,24},{48,32},{56,40},{64,11... | collective-permute-start | bytes 638984 | tf_op jit(solution)/shard_map/ppermute | solution.py:26
  27.1 14.6 %collective-permute-start.7 = (bf16[16,6656]{1,0:T(8,128)(2,1)S(1)}, bf16[16,6656]{1,0:T(8,128)(2,1)S(1)}, u32[]{:S(2)}, u32[]{:S(2)}) collective-permute-start(bf16[16,6656]{1,0:T(8,128)(2,1)S(1)} %get-tuple-element.39), channel_id=1, source_target_pairs={{0,48},{8,56},{16,0},{24,8},{32,16},{40,24},{48,32},{56,40},{64,11... | collective-permute-start | bytes 638984 | tf_op jit(solution)/shard_map/ppermute | solution.py:26
  30.9 10.8 %collective-permute-start.8 = (bf16[16,6656]{1,0:T(8,128)(2,1)S(1)}, bf16[16,6656]{1,0:T(8,128)(2,1)S(1)}, u32[]{:S(2)}, u32[]{:S(2)}) collective-permute-start(bf16[16,6656]{1,0:T(8,128)(2,1)S(1)} %shard_map.81), channel_id=1, source_target_pairs={{0,16},{8,24},{16,32},{24,40},{32,48},{40,56},{48,0},{56,8},{64,80... | collective-permute-start | bytes 638984 | tf_op jit(solution)/shard_map/ppermute | solution.py:26
  34.5 11.0 %collective-permute-start.12 = (bf16[16,3328]{1,0:T(8,128)(2,1)S(1)}, bf16[16,3328]{1,0:T(8,128)(2,1)S(1)}, u32[]{:S(2)}, u32[]{:S(2)}) collective-permute-start(bf16[16,3328]{1,0:T(8,128)(2,1)S(1)} %get-tuple-element.43), channel_id=1, source_target_pairs={{0,128},{8,136},{16,144},{24,152},{32,160},{40,168},{48,176},{56,1... | collective-permute-start | bytes 319496 | tf_op jit(solution)/shard_map/ppermute | solution.py:26
  41.7 8.3 %collective-permute-start.13 = (bf16[16,3328]{1,0:T(8,128)(2,1)S(1)}, bf16[16,3328]{1,0:T(8,128)(2,1)S(1)}, u32[]{:S(2)}, u32[]{:S(2)}) collective-permute-start(bf16[16,3328]{1,0:T(8,128)(2,1)S(1)} %get-tuple-element.44), channel_id=1, source_target_pairs={{0,192},{8,200},{16,208},{24,216},{32,224},{40,232},{48,240},{56,2... | collective-permute-start | bytes 319496 | tf_op jit(solution)/shard_map/ppermute | solution.py:26
  41.8 8.2 %collective-permute-start.9 = (bf16[16,3328]{1,0:T(8,128)(2,1)S(1)}, bf16[16,3328]{1,0:T(8,128)(2,1)S(1)}, u32[]{:S(2)}, u32[]{:S(2)}) collective-permute-start(bf16[16,3328]{1,0:T(8,128)(2,1)S(1)} %get-tuple-element.41), channel_id=1, source_target_pairs={{0,64},{8,72},{16,80},{24,88},{32,96},{40,104},{48,112},{56,120},{... | collective-permute-start | bytes 319496 | tf_op jit(solution)/shard_map/ppermute | solution.py:26
  50.1 8.6 %collective-permute-start.16 = (bf16[8,3328]{1,0:T(8,128)(2,1)S(1)}, bf16[8,3328]{1,0:T(8,128)(2,1)S(1)}, u32[]{:S(2)}, u32[]{:S(2)}) collective-permute-start(bf16[8,3328]{1,0:T(8,128)(2,1)S(1)} %shard_map.85.a), channel_id=1, source_target_pairs={{0,64},{8,72},{16,80},{24,88},{32,96},{40,104},{48,112},{56,120},{... | collective-permute-start | bytes 159752 | tf_op jit(solution)/shard_map/ppermute | solution.py:26
  51.6 9.2 %collective-permute-start.15 = (bf16[8,3328]{1,0:T(8,128)(2,1)S(1)}, bf16[8,3328]{1,0:T(8,128)(2,1)S(1)}, u32[]{:S(2)}, u32[]{:S(2)}) collective-permute-start(bf16[8,3328]{1,0:T(8,128)(2,1)S(1)} %shard_map.85.a), channel_id=1, source_target_pairs={{0,128},{8,136},{16,144},{24,152},{32,160},{40,168},{48,176},{56,1... | collective-permute-start | bytes 159752 | tf_op jit(solution)/shard_map/ppermute | solution.py:26
  55.6 7.3 %collective-permute-start.14 = (bf16[8,3328]{1,0:T(8,128)(2,1)S(1)}, bf16[8,3328]{1,0:T(8,128)(2,1)S(1)}, u32[]{:S(2)}, u32[]{:S(2)}) collective-permute-start(bf16[8,3328]{1,0:T(8,128)(2,1)S(1)} %shard_map.85.a), channel_id=1, source_target_pairs={{0,192},{8,200},{16,208},{24,216},{32,224},{40,232},{48,240},{56,2... | collective-permute-start | bytes 159752 | tf_op jit(solution)/shard_map/ppermute | solution.py:26
  62.9 8.1 %collective-permute-start.18 = (bf16[32,3328]{1,0:T(8,128)(2,1)S(1)}, bf16[32,3328]{1,0:T(8,128)(2,1)S(1)}, u32[]{:S(2)}, u32[]{:S(2)}) collective-permute-start(bf16[32,3328]{1,0:T(8,128)(2,1)S(1)} %shard_map.86.refs_0_), channel_id=1, source_target_pairs={{0,32},{8,40},{16,48},{24,56},{32,0},{40,8},{48,16},{56,24},{64,96... | collective-permute-start | bytes 638984 | tf_op jit(solution)/shard_map/ppermute | solution.py:26
  66.2 7.5 %collective-permute-start.19 = (bf16[32,3328]{1,0:T(8,128)(2,1)S(1)}, bf16[32,3328]{1,0:T(8,128)(2,1)S(1)}, u32[]{:S(2)}, u32[]{:S(2)}) collective-permute-start(bf16[32,3328]{1,0:T(8,128)(2,1)S(1)} %shard_map.86.refs_0_), channel_id=1, source_target_pairs={{0,16},{8,24},{16,32},{24,40},{32,48},{40,56},{48,0},{56,8},{64,80... | collective-permute-start | bytes 638984 | tf_op jit(solution)/shard_map/ppermute | solution.py:26
  66.2 7.5 %collective-permute-start.17 = (bf16[32,3328]{1,0:T(8,128)(2,1)S(1)}, bf16[32,3328]{1,0:T(8,128)(2,1)S(1)}, u32[]{:S(2)}, u32[]{:S(2)}) collective-permute-start(bf16[32,3328]{1,0:T(8,128)(2,1)S(1)} %shard_map.86.refs_0_), channel_id=1, source_target_pairs={{0,48},{8,56},{16,0},{24,8},{32,16},{40,24},{48,32},{56,40},{64,11... | collective-permute-start | bytes 638984 | tf_op jit(solution)/shard_map/ppermute | solution.py:26
  68.2 6.6 %collective-permute-start.20 = (bf16[32,3328]{1,0:T(8,128)(2,1)S(1)}, bf16[32,3328]{1,0:T(8,128)(2,1)S(1)}, u32[]{:S(2)}, u32[]{:S(2)}) collective-permute-start(bf16[32,3328]{1,0:T(8,128)(2,1)S(1)} %shard_map.86.refs_0_), channel_id=1, source_target_pairs={{0,8},{8,0},{16,24},{24,16},{32,40},{40,32},{48,56},{56,48},{64,72... | collective-permute-start | bytes 638984 | tf_op jit(solution)/shard_map/ppermute | solution.py:26
  73.6 1.5 %collective-permute-start.23 = (bf16[32,3328]{1,0:T(8,128)(2,1)S(1)}, bf16[32,3328]{1,0:T(8,128)(2,1)S(1)}, u32[]{:S(2)}, u32[]{:S(2)}) collective-permute-start(bf16[32,3328]{1,0:T(8,128)(2,1)S(1)} %collective-permute-done.19.refs_3_), channel_id=1, source_target_pairs={{0,8},{8,0},{16,24},{24,16},{32,40},{40,32},{48,56},{56,48},{64,72... | collective-permute-start | bytes 638984 | tf_op jit(solution)/shard_map/ppermute | solution.py:26
  73.6 1.8 %collective-permute-start.22 = (bf16[32,3328]{1,0:T(8,128)(2,1)S(1)}, bf16[32,3328]{1,0:T(8,128)(2,1)S(1)}, u32[]{:S(2)}, u32[]{:S(2)}) collective-permute-start(bf16[32,3328]{1,0:T(8,128)(2,1)S(1)} %collective-permute-done.18.refs_2_), channel_id=1, source_target_pairs={{0,8},{8,0},{16,24},{24,16},{32,40},{40,32},{48,56},{56,48},{64,72... | collective-permute-start | bytes 638984 | tf_op jit(solution)/shard_map/ppermute | solution.py:26
  74.1 1.6 %collective-permute-start.21 = (bf16[32,3328]{1,0:T(8,128)(2,1)S(1)}, bf16[32,3328]{1,0:T(8,128)(2,1)S(1)}, u32[]{:S(2)}, u32[]{:S(2)}) collective-permute-start(bf16[32,3328]{1,0:T(8,128)(2,1)S(1)} %collective-permute-done.17.refs_1_), channel_id=1, source_target_pairs={{0,8},{8,0},{16,24},{24,16},{32,40},{40,32},{48,56},{56,48},{64,72... | collective-permute-start | bytes 638984 | tf_op jit(solution)/shard_map/ppermute | solution.py:26
  76.3 5.0 %collective-permute-start.24 = (bf16[64,512]{1,0:T(8,128)(2,1)S(1)}, bf16[64,512]{1,0:T(8,128)(2,1)S(1)}, u32[]{:S(2)}, u32[]{:S(2)}) collective-permute-start(bf16[64,512]{1,0:T(8,128)(2,1)S(1)} %get-tuple-element.48), channel_id=1, source_target_pairs={{0,3},{1,0},{2,1},{3,2},{4,7},{5,4},{6,5},{7,6},{8,11},{9,8},{10,9... | collective-permute-start | bytes 196616 | tf_op jit(solution)/shard_map/ppermute | solution.py:34
  77.0 5.8 %collective-permute-start.25 = (bf16[64,512]{1,0:T(8,128)(2,1)S(1)}, bf16[64,512]{1,0:T(8,128)(2,1)S(1)}, u32[]{:S(2)}, u32[]{:S(2)}) collective-permute-start(bf16[64,512]{1,0:T(8,128)(2,1)S(1)} %get-tuple-element.49), channel_id=1, source_target_pairs={{0,2},{1,3},{2,0},{3,1},{4,6},{5,7},{6,4},{7,5},{8,10},{9,11},{10,... | collective-permute-start | bytes 196616 | tf_op jit(solution)/shard_map/ppermute | solution.py:34
  77.8 6.0 %collective-permute-start.26 = (bf16[64,512]{1,0:T(8,128)(2,1)S(1)}, bf16[64,512]{1,0:T(8,128)(2,1)S(1)}, u32[]{:S(2)}, u32[]{:S(2)}) collective-permute-start(bf16[64,512]{1,0:T(8,128)(2,1)S(1)} %get-tuple-element.50), channel_id=1, source_target_pairs={{0,1},{1,2},{2,3},{3,0},{4,5},{5,6},{6,7},{7,4},{8,9},{9,10},{10,1... | collective-permute-start | bytes 196616 | tf_op jit(solution)/shard_map/ppermute | solution.py:34
  83.9 4.0 %collective-permute-start.27 = (bf16[32,512]{1,0:T(8,128)(2,1)S(1)}, bf16[32,512]{1,0:T(8,128)(2,1)S(1)}, u32[]{:S(2)}, u32[]{:S(2)}) collective-permute-start(bf16[32,512]{1,0:T(8,128)(2,1)S(1)} %get-tuple-element.52), channel_id=1, source_target_pairs={{0,4},{1,5},{2,6},{3,7},{4,0},{5,1},{6,2},{7,3},{8,12},{9,13},{10,... | collective-permute-start | bytes 98312 | tf_op jit(solution)/shard_map/ppermute | solution.py:34
